TPU v7x, 32 devices: a whole 2x2x4 slice. The times are simulated.
32 devices in a mesh: dp: 2 (over x), blk: 4 (over z), uly: 4 (over y, core).
Axes of the slice: x: 2, y: 2, z: 4, core: 2. Of those that a mesh axis runs over, the one named last changes fastest.
Arguments:
- inputs: bfloat16 [2, 2048, 768], P('dp', ('blk', 'uly')), may hold values from -6 to 6
- stretch_order: int32 [2, 32], P('dp'), may hold values from 0 to 31, each once within a row
- norm_gains: bfloat16 [2, 768], P(None, ('blk', 'uly')), may hold values from 0.099609375 to 1.8984375
- biases: bfloat16 [4, 768], P(None, ('blk', 'uly')), may hold values from -3 to 3
- mid_shift: bfloat16 [768], P(('blk', 'uly')), may hold values from -3 to 3
- value_bias: bfloat16 [768], P(('blk', 'uly')), may hold values from -0.625 to 0.625
- qkv_weight: bfloat16 [768, 2304], P(('blk', 'uly')), may hold values from -0.21875 to 0.21875
- out_weight: bfloat16 [768, 768], P(('blk', 'uly')), may hold values from -6 to 6
- fc_weight: bfloat16 [768, 3072], P(('blk', 'uly')), may hold values from -0.21875 to 0.21875
- fc_bias: bfloat16 [3072], P(('blk', 'uly')), may hold values from -3 to 3
- proj_weight: bfloat16 [3072, 768], P(('blk', 'uly')), may hold values from -0.109375 to 0.109375
- cotangent: bfloat16 [2, 2048, 768], P('dp', ('blk', 'uly')), may hold values from -6 to 6
Outputs:
- output: bfloat16 [2, 2048, 768], P('dp', ('blk', 'uly'))
- input_grad: bfloat16 [2, 2048, 768], P('dp', ('blk', 'uly'))
- gains_grad: float32 [2, 768], P(None, ('blk', 'uly'))
- biases_grad: float32 [4, 768], P(None, ('blk', 'uly'))
- mid_shift_grad: float32 [768], P(('blk', 'uly'))
- value_bias_grad: float32 [768], P(('blk', 'uly'))
- qkv_grad: float32 [768, 2304], P(('blk', 'uly'))
- out_grad: float32 [768, 768], P(('blk', 'uly'))
- fc_grad: float32 [768, 3072], P(('blk', 'uly'))
- fc_bias_grad: float32 [3072], P(('blk', 'uly'))
- proj_grad: float32 [3072, 768], P(('blk', 'uly'))
Inputs may be any that keep to these rules, and one draw needn't show every extreme that they name: `stretch_order`: each row holds every stretch number 0 to 31 once.
All inputs are finite; a program needn't handle non-finite values.
Results may differ from a plain program's by a relative error of at most 0.025.
Values may be sent and summed in bfloat16 or wider, within the bound.
A program may use at most 192 MiB of HBM per device.

v0:
```python
import math

import jax
import jax.numpy as jnp
from jax import lax
from jax.sharding import PartitionSpec as P

HEADS = 12


masked_score = -1e30


def layer_norm(values, gain, shift):
    center = values - jnp.mean(values, -1, keepdims=True)
    inverse = lax.rsqrt(jnp.mean(center * center, -1, keepdims=True) + 1e-05)
    normed = center * inverse
    return (normed * gain + shift, normed, inverse)


def norm_back(grad_out, normed, inverse, gain):
    scaled = grad_out * gain
    mean_plain = jnp.mean(scaled, -1, keepdims=True)
    mean_mixed = jnp.mean(scaled * normed, -1, keepdims=True)
    return inverse * (scaled - mean_plain - normed * mean_mixed)


def sweep(step_fn, carried, parts):
    row_count = parts[0].shape[1]
    sweep_rows = math.gcd(row_count, 1024)

    def turn(inner, turn_number):
        offset = turn_number * sweep_rows
        blocks = tuple((lax.dynamic_slice_in_dim(part, offset, sweep_rows, 1) for part in parts))
        return (step_fn(inner, blocks, offset), None)

    result, _ = lax.scan(turn, carried, jnp.arange(row_count // sweep_rows, dtype=jnp.int32))
    return result


def per_device(
    inputs,
    stretch_order,
    norm_gains,
    biases,
    mid_shift,
    value_bias,
    qkv_weight,
    out_weight,
    fc_weight,
    fc_bias,
    proj_weight,
    cotangent,
):
    fp32 = jnp.float32
    bf16 = jnp.bfloat16
    gain_rows, shifts, mid_gathered, value_shift, w_qkv, w_out, w_fc, b_fc, w_proj = (
        lax.all_gather(norm_gains, ("blk", "uly"), axis=1, tiled=True),
        lax.all_gather(biases, ("blk", "uly"), axis=1, tiled=True),
        lax.all_gather(mid_shift, ("blk", "uly"), axis=0, tiled=True),
        lax.all_gather(value_bias, ("blk", "uly"), axis=0, tiled=True),
        lax.all_gather(qkv_weight, ("blk", "uly"), axis=0, tiled=True),
        lax.all_gather(out_weight, ("blk", "uly"), axis=0, tiled=True),
        lax.all_gather(fc_weight, ("blk", "uly"), axis=0, tiled=True),
        lax.all_gather(fc_bias, ("blk", "uly"), axis=0, tiled=True),
        lax.all_gather(proj_weight, ("blk", "uly"), axis=0, tiled=True),
    )
    gain_rows = gain_rows.astype(fp32)
    shifts = shifts.astype(fp32)
    mid_gathered = mid_gathered.astype(fp32)
    seq_count, row_len, width = inputs.shape
    uly_count = lax.axis_size("uly")
    local_heads = HEADS // uly_count
    head_dim = width // HEADS
    head_span = local_heads * head_dim
    block_rows = uly_count * row_len
    half_rows = row_len // 2
    seq_len = stretch_order.shape[1] * half_rows
    score_scale = head_dim ** (-0.5)
    tokens = inputs.astype(fp32).reshape(seq_count * row_len, width)
    ln_in, normed_in, inverse_in = layer_norm(tokens, gain_rows[0], shifts[0])
    ln_in = ln_in.astype(bf16)
    qkv_shift = jnp.concatenate([shifts[1], jnp.zeros((width,), fp32), value_shift.astype(fp32)])
    qkv = (jnp.dot(ln_in, w_qkv, preferred_element_type=fp32) + qkv_shift).astype(bf16)
    head_data = lax.all_to_all(
        qkv.reshape(seq_count, row_len, 3, uly_count, head_span),
        "uly",
        split_axis=3,
        concat_axis=1,
        tiled=True,
    )
    queries = head_data[:, :, 0, 0].reshape(seq_count, block_rows, local_heads, head_dim)
    key_rows = head_data[:, :, 1, 0]
    value_rows = head_data[:, :, 2, 0]
    positions = (
        stretch_order[:, :, None] * half_rows
        + jnp.arange(half_rows, dtype=jnp.int32)[None, None, :]
    ).reshape(seq_count, seq_len)
    query_pos = lax.dynamic_slice_in_dim(
        positions, lax.axis_index("blk") * block_rows, block_rows, 1
    )

    def score_block(key_part, key_start):
        part_rows = key_part.shape[1]
        key_pos = lax.dynamic_slice_in_dim(positions, key_start, part_rows, 1)
        scores = (
            jnp.einsum(
                "sqhd,skhd->shqk",
                queries,
                key_part.reshape(seq_count, part_rows, local_heads, head_dim),
                preferred_element_type=fp32,
            )
            * score_scale
        )
        causal = query_pos[:, None, :, None] >= key_pos[:, None, None, :]
        return (scores, causal)

    def stats_step(carried, blocks, key_start):
        row_max, row_total = carried
        scores, causal = score_block(blocks[0], key_start)
        new_max = jnp.maximum(row_max, jnp.max(jnp.where(causal, scores, masked_score), -1))
        row_total = row_total * jnp.exp(row_max - new_max) + jnp.sum(
            jnp.where(causal, jnp.exp(scores - new_max[..., None]), 0.0), -1
        )
        return (new_max, row_total)

    def softmax_of(scores, causal, row_max, row_total):
        return jnp.where(causal, jnp.exp(scores - row_max[..., None]) / row_total[..., None], 0.0)

    def make_output_step(row_max, row_total):

        def output_step(acc_out, blocks, key_start):
            scores, causal = score_block(blocks[0], key_start)
            attn_probs = softmax_of(scores, causal, row_max, row_total).astype(bf16)
            part_rows = blocks[1].shape[1]
            value_part = blocks[1].reshape(seq_count, part_rows, local_heads, head_dim)
            return acc_out + jnp.einsum(
                "shqk,skhd->sqhd", attn_probs, value_part, preferred_element_type=fp32
            )

        return output_step

    stats_init = (
        jnp.full((seq_count, local_heads, block_rows), masked_score, fp32),
        jnp.zeros((seq_count, local_heads, block_rows), fp32),
    )
    empty_out = jnp.zeros((seq_count, block_rows, local_heads, head_dim), fp32)
    all_keys, all_values = (
        lax.all_gather(key_rows, "blk", axis=1, tiled=True),
        lax.all_gather(value_rows, "blk", axis=1, tiled=True),
    )
    row_max, row_total = sweep(stats_step, stats_init, (all_keys,))
    attended = sweep(make_output_step(row_max, row_total), empty_out, (all_keys, all_values))
    attended_low = attended.astype(bf16).reshape(seq_count, block_rows, 1, head_span)
    merged = lax.all_to_all(attended_low, "uly", split_axis=1, concat_axis=2, tiled=True).reshape(
        seq_count * row_len, width
    )
    resid = tokens + (jnp.dot(merged, w_out, preferred_element_type=fp32) + shifts[2])
    ln_mid, normed_mid, inverse_mid = layer_norm(resid, gain_rows[1], mid_gathered)
    ln_mid = ln_mid.astype(bf16)
    pre_act = jnp.dot(ln_mid, w_fc, preferred_element_type=fp32) + b_fc.astype(fp32)

    def gelu_piece(pre_values):
        return jax.nn.gelu(pre_values, approximate=True)

    act, gelu_back = jax.vjp(gelu_piece, pre_act)
    act = act.astype(bf16)
    result = resid + (jnp.dot(act, w_proj, preferred_element_type=fp32) + shifts[3])
    grad_low = cotangent.reshape(seq_count * row_len, width)
    grad_out = grad_low.astype(fp32)
    proj_grad = jnp.einsum("ta,tb->ab", act, grad_low, preferred_element_type=fp32)
    proj_shift_grad = jnp.sum(grad_out, 0)
    grad_act = jnp.einsum("tb,ab->ta", grad_low, w_proj, preferred_element_type=fp32)
    grad_pre = gelu_back(grad_act)[0].astype(bf16)
    fc_grad = jnp.einsum("ta,tb->ab", ln_mid, grad_pre, preferred_element_type=fp32)
    fc_shift_grad = jnp.sum(grad_pre.astype(fp32), 0)
    grad_mid = jnp.einsum("tb,ab->ta", grad_pre, w_fc, preferred_element_type=fp32)
    gain_mid_grad = jnp.sum(grad_mid * normed_mid, 0)
    shift_mid_grad = jnp.sum(grad_mid, 0)
    grad_resid = grad_out + norm_back(grad_mid, normed_mid, inverse_mid, gain_rows[1])
    grad_branch = grad_resid.astype(bf16)
    out_grad = jnp.einsum("ta,tb->ab", merged, grad_branch, preferred_element_type=fp32)
    out_shift_grad = jnp.sum(grad_branch.astype(fp32), 0)
    grad_merged = jnp.einsum("tb,ab->ta", grad_branch, w_out, preferred_element_type=fp32).astype(
        bf16
    )
    grad_att = lax.all_to_all(
        grad_merged.reshape(seq_count, row_len, uly_count, head_span),
        "uly",
        split_axis=2,
        concat_axis=1,
        tiled=True,
    )
    grad_att = grad_att.reshape(seq_count, block_rows, local_heads, head_dim)
    delta = jnp.transpose(jnp.sum(grad_att.astype(fp32) * attended, -1), (0, 2, 1))
    back_keys, back_values = (all_keys, all_values)
    sweep_rows = math.gcd(seq_len, 1024)

    def query_terms(offset):
        key_part = lax.dynamic_slice_in_dim(back_keys, offset, sweep_rows, 1)
        value_part = lax.dynamic_slice_in_dim(back_values, offset, sweep_rows, 1)
        scores, causal = score_block(key_part, offset)
        attn_probs = softmax_of(scores, causal, row_max, row_total)
        key_heads = key_part.reshape(seq_count, sweep_rows, local_heads, head_dim)
        value_heads = value_part.reshape(seq_count, sweep_rows, local_heads, head_dim)
        grad_probs = jnp.einsum(
            "sqhd,skhd->shqk", grad_att, value_heads, preferred_element_type=fp32
        )
        grad_scores = (attn_probs * (grad_probs - delta[..., None])).astype(bf16)
        query_term = (
            jnp.einsum("shqk,skhd->sqhd", grad_scores, key_heads, preferred_element_type=fp32)
            * score_scale
        )
        return (query_term, grad_scores, attn_probs.astype(bf16))

    query_init = jnp.zeros((seq_count, block_rows, local_heads, head_dim), fp32)

    def back_step(carried, turn_number):
        grad_query, kv_buffer = carried
        offset = turn_number * sweep_rows
        query_term, grad_scores, probs_low = query_terms(offset)
        grad_key = (
            jnp.einsum("shqk,sqhd->skhd", grad_scores, queries, preferred_element_type=fp32)
            * score_scale
        )
        grad_value = jnp.einsum("shqk,sqhd->skhd", probs_low, grad_att, preferred_element_type=fp32)
        kv_pair = jnp.stack(
            [
                grad_key.reshape(seq_count, sweep_rows, head_span),
                grad_value.reshape(seq_count, sweep_rows, head_span),
            ],
            2,
        )
        kv_buffer = lax.dynamic_update_slice_in_dim(kv_buffer, kv_pair, offset, 1)
        return ((grad_query + query_term, kv_buffer), None)

    back_init = (query_init, jnp.zeros((seq_count, seq_len, 2, head_span), fp32))
    back_done, _ = lax.scan(
        back_step, back_init, jnp.arange(seq_len // sweep_rows, dtype=jnp.int32)
    )
    grad_query, kv_buffer = back_done
    kv_summed = lax.psum_scatter(
        kv_buffer.astype(jnp.bfloat16), "blk", scatter_dimension=1, tiled=True
    ).astype(jnp.float32)
    grad_heads = jnp.concatenate(
        [
            grad_query.reshape(seq_count, block_rows, 1, head_span).astype(bf16),
            kv_summed.astype(bf16),
        ],
        2,
    )
    grad_qkv = lax.all_to_all(
        grad_heads.reshape(seq_count, block_rows, 3, 1, head_span),
        "uly",
        split_axis=1,
        concat_axis=3,
        tiled=True,
    )
    grad_qkv = grad_qkv.reshape(seq_count * row_len, 3 * width)
    qkv_grad = jnp.einsum("ta,tb->ab", ln_in, grad_qkv, preferred_element_type=fp32)
    column_sums = jnp.sum(grad_qkv.astype(fp32), 0)
    grad_in_norm = jnp.einsum("tb,ab->ta", grad_qkv, w_qkv, preferred_element_type=fp32)
    gain_in_grad = jnp.sum(grad_in_norm * normed_in, 0)
    shift_in_grad = jnp.sum(grad_in_norm, 0)
    grad_input = grad_resid + norm_back(grad_in_norm, normed_in, inverse_in, gain_rows[0])
    gains_grad = jnp.stack([gain_in_grad, gain_mid_grad])
    biases_grad = jnp.stack([shift_in_grad, column_sums[:width], out_shift_grad, proj_shift_grad])
    value_grad = column_sums[2 * width :]
    shard_grads = (
        lax.psum_scatter(gains_grad, ("blk", "uly"), scatter_dimension=1, tiled=True),
        lax.psum_scatter(biases_grad, ("blk", "uly"), scatter_dimension=1, tiled=True),
        lax.psum_scatter(shift_mid_grad, ("blk", "uly"), scatter_dimension=0, tiled=True),
        lax.psum_scatter(value_grad, ("blk", "uly"), scatter_dimension=0, tiled=True),
        lax.psum_scatter(qkv_grad, ("blk", "uly"), scatter_dimension=0, tiled=True),
        lax.psum_scatter(out_grad, ("blk", "uly"), scatter_dimension=0, tiled=True),
        lax.psum_scatter(fc_grad, ("blk", "uly"), scatter_dimension=0, tiled=True),
        lax.psum_scatter(fc_shift_grad, ("blk", "uly"), scatter_dimension=0, tiled=True),
        lax.psum_scatter(proj_grad, ("blk", "uly"), scatter_dimension=0, tiled=True),
    )
    shard_grads = (
        lax.psum(shard_grads[0].astype(jnp.bfloat16), "dp").astype(jnp.float32),
        lax.psum(shard_grads[1].astype(jnp.bfloat16), "dp").astype(jnp.float32),
        lax.psum(shard_grads[2].astype(jnp.bfloat16), "dp").astype(jnp.float32),
        lax.psum(shard_grads[3].astype(jnp.bfloat16), "dp").astype(jnp.float32),
        lax.psum(shard_grads[4].astype(jnp.bfloat16), "dp").astype(jnp.float32),
        lax.psum(shard_grads[5].astype(jnp.bfloat16), "dp").astype(jnp.float32),
        lax.psum(shard_grads[6].astype(jnp.bfloat16), "dp").astype(jnp.float32),
        lax.psum(shard_grads[7].astype(jnp.bfloat16), "dp").astype(jnp.float32),
        lax.psum(shard_grads[8].astype(jnp.bfloat16), "dp").astype(jnp.float32),
    )
    output = result.astype(bf16).reshape(seq_count, row_len, width)
    input_grad = grad_input.astype(bf16).reshape(seq_count, row_len, width)
    return (
        output,
        input_grad,
        shard_grads[0],
        shard_grads[1],
        shard_grads[2],
        shard_grads[3],
        shard_grads[4],
        shard_grads[5],
        shard_grads[6],
        shard_grads[7],
        shard_grads[8],
    )


def solution(mesh):
    placed = (
        P("dp", ("blk", "uly"), None),
        P("dp", None),
        P(None, ("blk", "uly")),
        P(None, ("blk", "uly")),
        P(("blk", "uly")),
        P(("blk", "uly")),
        P(("blk", "uly"), None),
        P(("blk", "uly"), None),
        P(("blk", "uly"), None),
        P(("blk", "uly")),
        P(("blk", "uly"), None),
        P("dp", ("blk", "uly"), None),
    )
    return jax.shard_map(
        per_device,
        mesh=mesh,
        in_specs=placed,
        out_specs=(
            P("dp", ("blk", "uly"), None),
            P("dp", ("blk", "uly"), None),
            P(None, ("blk", "uly")),
            P(None, ("blk", "uly")),
            P(("blk", "uly")),
            P(("blk", "uly")),
            P(("blk", "uly"), None),
            P(("blk", "uly"), None),
            P(("blk", "uly"), None),
            P(("blk", "uly")),
            P(("blk", "uly"), None),
        ),
        check_vma=False,
    )
```

profile of v0, /device:TPU:0, one launch (start us, length us, event | category | flops | bytes accessed | tf_op | source)
XLA Modules:
  0.0 906.8 jit_solution(9269708828348426704)
XLA Ops:
  9.4 23.4 %all-gather.3 = bf16[16,48,4]{1,2,0:T(4,128)(2,1)S(1)} all-gather(bf16[1,48,4]{1,2,0:T(4,128)(2,1)} %bitcast.369), channel_id=1, replica_groups=mesh['dp'=2,'blk'=4,'uly'=4] {'blk','uly'}, dimensions={0}, use_global_device_ids=true | all-gather | bytes 6528 | tf_op jit(solution)/shard_map/all_gather | solution.py:59
  38.1 58.6 %all-reduce.7 = (bf16[768]{0:T(1024)(128)(2,1)S(1)}, bf16[3072]{0:T(1024)(128)(2,1)S(1)}, bf16[768]{0:T(1024)(128)(2,1)S(1)}) all-reduce(bf16[768]{0:T(1024)(128)(2,1)S(1)} %dynamic-update-slice, bf16[3072]{0:T(1024)(128)(2,1)S(1)} %dynamic-update-slice.2, ...), channel_id=1, replica_groups=mesh['dp'=2,'blk'=4,'uly'=4] {'blk','uly'}, use_global_device_ids=true, to_apply=%add | all-reduce | flops 4608 | bytes 18432
  96.6 17.2 %all-gather.2 = bf16[16,48,2]{1,2,0:T(2,128)(2,1)S(1)} all-gather(bf16[1,48,2]{1,2,0:T(2,128)(2,1)} %bitcast.370), channel_id=1, replica_groups=mesh['dp'=2,'blk'=4,'uly'=4] {'blk','uly'}, dimensions={0}, use_global_device_ids=true | all-gather | bytes 3264 | tf_op jit(solution)/shard_map/all_gather | solution.py:58
  125.9 11.5 %all-to-all-done = bf16[1,128,3,4,192]{1,4,2,0,3:T(8,128)(2,1)S(1)} async-done(((bf16[1,128,3,4,192]{1,4,2,0,3:T(8,128)(2,1)}), bf16[1,128,3,4,192]{1,4,2,0,3:T(8,128)(2,1)S(1)}, u32[]{:S(2)}, u32[]{:S(2)}) %all-to-all-start) | async-done | bytes 589856 | tf_op jit(solution)/shard_map/all_to_all | solution.py:85
  138.2 25.9 %all-gather = bf16[1,2048,1,1,192]{1,4,2,3,0:T(8,128)(2,1)} all-gather(bf16[1,512,1,1,192]{1,4,2,3,0:T(8,128)(2,1)S(1)} %get-tuple-element.402), channel_id=2, replica_groups=mesh['dp'=2,'blk'=4,'uly'=4] {'blk'}, dimensions={1}, use_global_device_ids=true | all-gather | bytes 983040 | tf_op jit(solution)/shard_map/all_gather | solution.py:150
  164.1 20.9 %all-gather.1 = bf16[1,2048,1,1,192]{1,4,2,3,0:T(8,128)(2,1)} all-gather(bf16[1,512,1,1,192]{1,4,2,3,0:T(8,128)(2,1)S(1)} %get-tuple-element.401), channel_id=3, replica_groups=mesh['dp'=2,'blk'=4,'uly'=4] {'blk'}, dimensions={1}, use_global_device_ids=true | all-gather | bytes 983040 | tf_op jit(solution)/shard_map/all_gather | solution.py:149
  185.0 27.2 %while.37 = (s32[]{:T(128)}, f32[1,3,512]{2,1,0:T(4,128)S(1)}, f32[1,3,512]{2,1,0:T(4,128)}, s32[1,512]{1,0:T(1,128)}, s32[2]{0:T(128)S(1)}, /*index=5*/s32[1,20...) while((s32[]{:T(128)}, f32[1,3,512]{2,1,0:T(4,128)S(1)}, ...), condition=%wide.region_5.6_spmd.clone, body=%wide.region_2.5_spmd.clone.sunk | while | flops 212868608 | bytes 15626442 | solution.py:37
  201.7 4.9 fusion.134
  212.2 13.1 %while.38 = (s32[]{:T(128)}, f32[1,512,3,64]{1,3,2,0:T(8,128)S(1)}, s32[2]{0:T(128)S(1)}, bf16[1,2048,192]{1,2,0:T(8,128)(2,1)}, s32[1,512]{1,0:T(1,128)}, /*ind...) while((s32[]{:T(128)}, f32[1,512,3,64]{1,3,2,0:T(8,128)S(1)}, ...), condition=%wide.region_7.8_spmd.clone, body=%wide.region_6.7_spmd.clone.sunk | while | flops 411238400 | bytes 4417753 | solution.py:37
  233.2 5.1 all-to-all-done.1
  244.5 5.5 convert_reduce_fusion
  258.7 5.2 all-to-all-done.2
  267.8 36.1 %while.39 = (s32[]{:T(128)}, f32[1,512,3,64]{1,3,2,0:T(8,128)}, bf16[1,2048,2,192]{1,3,2,0:T(8,128)(2,1)}, s32[2]{0:T(128)S(1)}, bf16[1,2048,192]{1,2,0:T(8,128)...) while((s32[]{:T(128)}, f32[1,512,3,64]{1,3,2,0:T(8,128)}, ...), condition=%wide.region_14.15_spmd.clone, body=%wide.region_13.14_spmd.clone.sunk | while | flops 1022001152 | bytes 73826752 | solution.py:238
  313.0 5.1 fusion.84
  319.5 5.2 fusion.67
  326.8 18.8 %reduce-scatter.22.cloned.1.call-done = bf16[512,384]{1,0:T(8,128)(2,1)} async-done(((bf16[2048,384]{1,0:T(8,128)(2,1)}), bf16[512,384]{1,0:T(8,128)(2,1)}) %reduce-scatter.22.cloned.1.call-update) | async-done | bytes 393232
  349.2 17.7 %all_to_all.63 = bf16[1,512,3,1,192]{4,2,3,0,1:T(4,128)(2,1)} all-to-all(bf16[1,512,3,1,192]{4,2,3,0,1:T(4,128)(2,1)S(1)} %maximum_bitcast_fusion), channel_id=1, replica_groups=mesh['dp'=2,'blk'=4,'uly'=4] {'uly'}, dimensions={1} | all-to-all | bytes 1179648 | tf_op jit(solution)/shard_map/all_to_all | solution.py:252
  385.2 26.0 %reduce-scatter.16.cloned.1.call-done = f32[48,768]{1,0:T(8,128)} async-done(((f32[768,768]{1,0:T(8,128)}), f32[48,768]{1,0:T(8,128)}) %reduce-scatter.16.cloned.1.call-update) | async-done | bytes 147472 | tf_op jit(solution)/shard_map/reduce_scatter | solution.py:275
  412.7 113.6 %reduce-scatter.18.cloned.1.call-done = f32[48,3072]{1,0:T(8,128)} async-done(((f32[768,3072]{1,0:T(8,128)}), f32[48,3072]{1,0:T(8,128)}) %reduce-scatter.18.cloned.1.call-update) | async-done | bytes 589840 | tf_op jit(solution)/shard_map/reduce_scatter | solution.py:276
  528.1 113.4 %reduce-scatter.20.cloned.1.call-done = f32[192,768]{1,0:T(8,128)} async-done(((f32[3072,768]{1,0:T(8,128)}), f32[192,768]{1,0:T(8,128)}) %reduce-scatter.20.cloned.1.call-update) | async-done | bytes 589840 | tf_op jit(solution)/shard_map/reduce_scatter | solution.py:278
  643.3 92.6 %reduce-scatter.14.cloned.1.call-done = f32[48,2304]{1,0:T(8,128)} async-done(((f32[768,2304]{1,0:T(8,128)}), f32[48,2304]{1,0:T(8,128)}) %reduce-scatter.14.cloned.1.call-update) | async-done | bytes 442384 | tf_op jit(solution)/shard_map/reduce_scatter | solution.py:274
  742.0 59.5 %all-reduce.6 = (bf16[768]{0:T(1024)(128)(2,1)S(1)}, bf16[768]{0:T(1024)(128)(2,1)S(1)}, bf16[3072]{0:T(1024)(128)(2,1)S(1)}) all-reduce(f32[768]{0:T(1024)S(1)} %copy-done.33, f32[768]{0:T(1024)S(1)} %slice.50, f32[3072]{0:T(1024)S(1)} %copy-done.41), channel_id=7, replica_groups=mesh['dp'=2,'blk'=4,'uly'=4] {'blk','uly'}, use_global_device_ids=true, to_apply=%region_29.30.clone | all-reduce | flops 4608 | bytes 27648
  803.4 50.7 %reduce-scatter.26.cloned.1.call-done = f32[48,4]{1,0:T(8,128)} async-done(((f32[768,4]{1,0:T(8,128)}), f32[48,4]{1,0:T(8,128)}) %reduce-scatter.26.cloned.1.call-update) | async-done | bytes 784
  862.6 30.5 %all-reduce.12.cloned.1.call-done = (bf16[48,2304]{1,0:T(8,128)(2,1)}, bf16[48,768]{1,0:T(8,128)(2,1)}, bf16[48,3072]{1,0:T(8,128)(2,1)}, bf16[192,768]{1,0:T(8,128)(2,1)}) async-done(((bf16[48,2304]{1,0:T(8,128)(2,1)}, bf16[48,768]{1,0:T(8,128)(2,1)}, bf16[48,3072]{1,0:T(8,128)(2,1)}, bf16[192,768]{1,0:T(8,128)(2,1)}), (bf16[48,2304]{1,0:T(8,128)(2,1)}, bf16[48,768]{1,0:T(8,128)(2,1)}, ...) | async-done | bytes 884752 | tf_op jit(solution)/shard_map/psum | solution.py:285
  (294 shorter events, 173.5 us)
Async XLA Ops:
  7.2 109.7 %all-gather.9.cloned.1.call-start = ((), (), s32[]{:S(2)}) async-start(), calls=%async_computation.11 | async-start | bytes 3760128 | tf_op jit(solution)/shard_map/all_gather | solution.py:62
  7.9 231.2 %all-gather.11.cloned.1.call-start = ((), (), s32[]{:S(2)}) async-start(), calls=%async_computation.12 | async-start | bytes 1253376 | tf_op jit(solution)/shard_map/all_gather | solution.py:63
  8.7 232.5 %all-gather.13.cloned.1.call-start = ((), (), s32[]{:S(2)}) async-start(), calls=%async_computation.13 | async-start | bytes 5013504 | tf_op jit(solution)/shard_map/all_gather | solution.py:64
  114.6 137.7 %copy-start.21 = (f32[768]{0:T(1024)}, f32[768]{0:T(1024)S(1)}, u32[]{:S(2)}) copy-start(f32[768]{0:T(1024)S(1)} %get-tuple-element.313) | copy-start | bytes 9220
  120.9 16.5 %all-to-all-start = ((bf16[1,128,3,4,192]{1,4,2,0,3:T(8,128)(2,1)}), bf16[1,128,3,4,192]{1,4,2,0,3:T(8,128)(2,1)S(1)}, u32[]{:S(2)}, u32[]{:S(2)}) async-start(bf16[1,128,3,4,192]{1,4,2,0,3:T(8,128)(2,1)} %copy.119), calls=%async_computation | async-start | bytes 1179648 | tf_op jit(solution)/shard_map/all_to_all | solution.py:85
  124.4 120.1 %all-gather.15.cloned.1.call-start = ((), (), s32[]{:S(2)}) async-start(), calls=%async_computation.14 | async-start | bytes 5013504 | tf_op jit(solution)/shard_map/all_gather | solution.py:66
  225.8 13.4 %copy-start.5 = (bf16[1,128,768]{2,1,0:T(8,128)(2,1)S(1)}, bf16[1,128,768]{2,1,0:T(8,128)(2,1)}, u32[]{:S(2)}) copy-start(bf16[1,128,768]{2,1,0:T(8,128)(2,1)} %param.18) | copy-start | bytes 589828
  229.6 8.7 all-to-all-start.1
  255.3 8.7 all-to-all-start.2
  258.6 87.0 %reduce-scatter.22.cloned.1.call-start = ((), (), s32[]{:S(2)}) async-start(), calls=%async_computation.19 | async-start | bytes 1966080
  310.7 100.5 %reduce-scatter.16.cloned.1.call-start = ((), (), s32[]{:S(2)}) async-start(), calls=%async_computation.16 | async-start | bytes 2506752 | tf_op jit(solution)/shard_map/reduce_scatter | solution.py:275
  312.6 213.6 %reduce-scatter.18.cloned.1.call-start = ((), (), s32[]{:S(2)}) async-start(), calls=%async_computation.17 | async-start | bytes 10027008 | tf_op jit(solution)/shard_map/reduce_scatter | solution.py:276
  318.1 323.4 %reduce-scatter.20.cloned.1.call-start = ((), (), s32[]{:S(2)}) async-start(), calls=%async_computation.18 | async-start | bytes 10027008 | tf_op jit(solution)/shard_map/reduce_scatter | solution.py:278
  324.7 411.1 %reduce-scatter.14.cloned.1.call-start = ((), (), s32[]{:S(2)}) async-start(), calls=%async_computation.15 | async-start | bytes 7520256 | tf_op jit(solution)/shard_map/reduce_scatter | solution.py:274
  349.2 21.4 %copy-start.6 = (bf16[1,128,768]{2,1,0:T(8,128)(2,1)S(1)}, bf16[1,128,768]{2,1,0:T(8,128)(2,1)}, u32[]{:S(2)}) copy-start(bf16[1,128,768]{2,1,0:T(8,128)(2,1)} %param.18) | copy-start | bytes 589828
  349.2 21.4 %copy-start.24 = (f32[768]{0:T(1024)S(1)}, f32[768]{0:T(1024)}, u32[]{:S(2)}) copy-start(f32[768]{0:T(1024)} %copy-done.23) | copy-start | bytes 9220
  349.2 21.4 %copy-start.28 = (f32[768]{0:T(1024)S(1)}, f32[768]{0:T(1024)}, u32[]{:S(2)}) copy-start(f32[768]{0:T(1024)} %copy-done.27) | copy-start | bytes 9220
  349.2 21.4 %copy-start.30 = (f32[128]{0:T(128)S(1)}, f32[128]{0:T(128)}, u32[]{:S(2)}) copy-start(f32[128]{0:T(128)} %copy-done.29) | copy-start | bytes 1540
  349.2 21.4 %copy-start.38 = (f32[128]{0:T(128)S(1)}, f32[128]{0:T(128)}, u32[]{:S(2)}) copy-start(f32[128]{0:T(128)} %copy-done.37) | copy-start | bytes 1540
  374.8 427.8 %reduce-scatter.24.cloned.1.call-start = ((), (), s32[]{:S(2)}) async-start(), calls=%async_computation.20 | async-start | bytes 417792
  382.8 471.3 %reduce-scatter.26.cloned.1.call-start = ((), (), s32[]{:S(2)}) async-start(), calls=%async_computation.21 | async-start | bytes 417792
  382.9 354.8 %copy-start.42 = (f32[768]{0:T(1024)S(1)}, f32[768]{0:T(1024)}, u32[]{:S(2)}) copy-start(f32[768]{0:T(1024)} %get-tuple-element.309) | copy-start | bytes 9220
  383.9 509.2 %all-reduce.12.cloned.1.call-start = ((), (), s32[]{:S(2)}) async-start(), calls=%async_computation.22 | async-start | bytes 1769472 | tf_op jit(solution)/shard_map/psum | solution.py:285
  737.7 64.1 %copy-start.18 = (f32[128,768]{1,0:T(8,128)S(1)}, f32[128,768]{1,0:T(8,128)}, u32[]{:S(2)}) copy-start(f32[128,768]{1,0:T(8,128)} %get-tuple-element.411) | copy-start | bytes 1179652
  (42 other events, 133.1 us)
Sparse Core Ops, SparseCore 0:
  10.3 50.0 all-gather.8
  62.6 37.4 all-gather.10
  102.4 61.5 all-gather.12
  166.1 55.4 all-gather.14
  310.7 34.8 reduce-scatter.21
  349.2 61.8 reduce-scatter.15
  415.8 110.4 reduce-scatter.17
  530.4 111.0 reduce-scatter.19
  646.1 89.7 reduce-scatter.13
  739.8 55.1 reduce-scatter.23
  799.5 54.5 reduce-scatter.25
  857.0 35.9 all-reduce.11
where the time goes:
time: 909 us; the launch traced here: 907 us
  waiting for transfers between devices  470 us (52%)
  blocking collectives  228 us (25%)
  matrix products  82.3 us (9%)
  local copies, waits for them, and re-layouts  47.5 us (5%)
  other arithmetic  45.6 us (5%)
  between operations  17.7 us (2%)
  starting transfers between devices  11.1 us (1%)
    unnamed x2, blocking collectives  118 us
    reduce_scatter x1, waiting for transfers between devices, per_device(): lax.psum_scatter(fc_grad, ('blk', 'uly'), scatter_dimension=0, tiled=True)  114 us
    reduce_scatter x1, waiting for transfers between devices, per_device(): lax.psum_scatter(proj_grad, ('blk', 'uly'), scatter_dimension=0, tiled=True)  113 us
    reduce_scatter x1, waiting for transfers between devices, per_device(): lax.psum_scatter(qkv_grad, ('blk', 'uly'), scatter_dimension=0, tiled=True)  92.6 us
    unnamed x15, waiting for transfers between devices  72.2 us
    psum x1, waiting for transfers between devices, per_device(): lax.psum(shard_grads[4].astype(jnp.bfloat16), 'dp').astype(jnp.float32)  30.5 us
    reduce_scatter x1, waiting for transfers between devices, per_device(): lax.psum_scatter(out_grad, ('blk', 'uly'), scatter_dimension=0, tiled=True)  26 us
    all_gather x1, blocking collectives, per_device(): lax.all_gather(value_rows, 'blk', axis=1, tiled=True)  25.9 us
  transfers between devices with their start and end apart: 15, of which 10 were waited for; matrix products, arithmetic and copies ran while one was open for 12% of the time, Pallas kernels for 0%

commit v1 on v0

--- a/solution.py
+++ b/solution.py
@@ -1,8 +1,11 @@
+import functools
 import math
 
 import jax
 import jax.numpy as jnp
 from jax import lax
+from jax.experimental import pallas as pl
+from jax.experimental.pallas import tpu as pltpu
 from jax.sharding import PartitionSpec as P
 
 HEADS = 12
@@ -305,6 +308,461 @@
     )
 
 
+MESH = pl.DeviceIdType.MESH
+BF = jnp.bfloat16
+F32 = jnp.float32
+VSPEC = pl.BlockSpec(memory_space=pltpu.VMEM)
+
+
+class Net:
+    def __init__(self, send_sem, recv_sem, nz):
+        self.send_sem, self.recv_sem = send_sem, recv_sem
+        self.count = 0
+        self.sent = []
+        self.nz = nz
+        self.x = lax.axis_index("dp")
+        self.z = lax.axis_index("blk")
+        self.u = lax.axis_index("uly")
+
+    def slot(self):
+        self.count += 1
+        return self.count - 1
+
+    def make(self, src, dst, dev):
+        k = self.slot()
+        return pltpu.make_async_remote_copy(
+            src_ref=src,
+            dst_ref=dst,
+            send_sem=self.send_sem.at[k],
+            recv_sem=self.recv_sem.at[k],
+            device_id=dev,
+            device_id_type=MESH,
+        )
+
+    def send(self, src, dst, dev):
+        copy = self.make(src, dst, dev)
+        copy.start()
+        self.sent.append(copy)
+        return copy
+
+    def plane(self, m):
+        return (self.x, self.z, self.u ^ m)
+
+    def other_x(self):
+        return (1 - self.x, self.z, self.u)
+
+    def zplus(self, d):
+        return lax.rem(self.z + d, self.nz)
+
+    def line(self, d):
+        return (self.x, self.zplus(d), self.u)
+
+    def enter(self):
+        barrier = pltpu.get_barrier_semaphore()
+        near = [self.plane(m) for m in (1, 2, 3)] + [self.other_x()]
+        near += [self.line(d) for d in range(1, self.nz)]
+        near += [(1 - self.x, self.z, self.u ^ m) for m in (1, 2, 3)]
+        for dev in near:
+            pl.semaphore_signal(barrier, inc=1, device_id=dev, device_id_type=MESH)
+        pl.semaphore_wait(barrier, len(near))
+
+    def finish(self):
+        for copy in self.sent:
+            copy.wait_send()
+
+
+def rows_at(start, count):
+    return pl.ds(pl.multiple_of(start, 16), count)
+
+
+def gather_kernel(nz, qkv_pre, fc_pre, out_s, proj_s, vec_pre, w_qkv, w_fc, w_proj, w_out, vec, land_z, vec_u, land_p, send_sem, recv_sem, local_sem):
+    net = Net(send_sem, recv_sem, nz)
+    x, z, u = net.x, net.z, net.u
+    own48 = (4 * z + u) * 48
+    locals_ = [
+        pltpu.make_async_copy(qkv_pre.at[u], w_qkv.at[rows_at(own48, 48)], local_sem.at[0]),
+        pltpu.make_async_copy(fc_pre.at[u], w_fc.at[rows_at(own48, 48)], local_sem.at[1]),
+        pltpu.make_async_copy(proj_s, w_proj.at[rows_at(192 * z, 192)], local_sem.at[2]),
+        pltpu.make_async_copy(out_s, w_out.at[rows_at(own48, 48)], local_sem.at[3]),
+    ]
+    for copy in locals_:
+        copy.start()
+    net.enter()
+    vec_z = [net.send(vec_pre, land_z.at[d - 1], net.line(d)) for d in range(1, nz)]
+    in_plane = {}
+    for name, pre, full in (("qkv", qkv_pre, w_qkv), ("fc", fc_pre, w_fc)):
+        in_plane[name] = [
+            net.send(pre.at[u ^ m], full.at[rows_at(own48, 48)], net.plane(m)) for m in (1, 2, 3)
+        ]
+    half_cols = pl.ds(pl.multiple_of(384 * x, 128), 384)
+    for copy in vec_z:
+        copy.wait_recv()
+    total = vec_pre[...]
+    for d in range(nz - 1):
+        total = total + land_z[d]
+    vec_u[...] = total
+    vec_p = [net.send(vec_u, land_p.at[m - 1], net.plane(m)) for m in (1, 2, 3)]
+    for copy in locals_:
+        copy.wait()
+
+    def along_z(full):
+        mine = rows_at(192 * z + 96 * x, 96)
+        return [net.send(full.at[mine], full.at[mine], net.line(d)) for d in range(1, nz)]
+
+    def across_x(full, arrivals):
+        sent = []
+        for d, copy in enumerate(arrivals, 1):
+            copy.wait_recv()
+            part = rows_at(192 * net.zplus(nz - d) + 96 * x, 96)
+            sent.append(net.send(full.at[part], full.at[part], net.other_x()))
+        return sent
+
+    for copy in in_plane["qkv"]:
+        copy.wait_recv()
+    qkv_z = along_z(w_qkv)
+    out_z = [
+        net.send(out_s.at[:, half_cols], w_out.at[rows_at(own48, 48), half_cols], net.line(d))
+        for d in range(1, nz)
+    ]
+    for copy in in_plane["fc"]:
+        copy.wait_recv()
+    fc_z = along_z(w_fc)
+    proj_mine = rows_at(192 * z + 96 * x, 96)
+    proj_z = [
+        net.send(proj_s.at[rows_at(96 * x, 96)], w_proj.at[proj_mine], net.line(d))
+        for d in range(1, nz)
+    ]
+    waits = across_x(w_qkv, qkv_z)
+    out_x = []
+    for d, copy in enumerate(out_z, 1):
+        copy.wait_recv()
+        part = w_out.at[rows_at((4 * net.zplus(nz - d) + u) * 48, 48), half_cols]
+        out_x.append(net.send(part, part, net.other_x()))
+    for copy in out_x:
+        copy.wait_recv()
+
+    def out_rows(zz, who):
+        return w_out.at[rows_at((4 * zz + who) * 48, 48)]
+
+    out_y = [net.send(out_rows(zz, u), out_rows(zz, u), net.plane(2)) for zz in range(nz)]
+    out_c = [net.send(out_rows(zz, u), out_rows(zz, u), net.plane(1)) for zz in range(nz)]
+    for zz, copy in enumerate(out_y):
+        copy.wait_recv()
+        out_c.append(net.send(out_rows(zz, u ^ 2), out_rows(zz, u ^ 2), net.plane(1)))
+    waits += out_c
+    waits += across_x(w_fc, fc_z)
+    waits += across_x(w_proj, proj_z)
+    total = vec_u[...].astype(F32)
+    row = lax.broadcasted_iota(jnp.int32, total.shape, 0)
+    for m, copy in enumerate(vec_p):
+        copy.wait_recv()
+        total = total + jnp.where(row == 8, 0.0, land_p[m].astype(F32))
+    vec[...] = total
+    for copy in waits:
+        copy.wait_recv()
+    net.finish()
+
+
+def gather_weights(nz, qkv_pre, fc_pre, out_s, proj_s, vec_pre):
+    return pl.pallas_call(
+        functools.partial(gather_kernel, nz),
+        out_shape=(
+            jax.ShapeDtypeStruct((768, 576), BF),
+            jax.ShapeDtypeStruct((768, 768), BF),
+            jax.ShapeDtypeStruct((768, 768), BF),
+            jax.ShapeDtypeStruct((768, 768), BF),
+            jax.ShapeDtypeStruct((16, 768), F32),
+        ),
+        in_specs=[VSPEC] * 5,
+        out_specs=(VSPEC,) * 5,
+        scratch_shapes=[
+            pltpu.VMEM((nz - 1, 16, 768), BF),
+            pltpu.VMEM((16, 768), BF),
+            pltpu.VMEM((3, 16, 768), BF),
+            pltpu.SemaphoreType.DMA((64,)),
+            pltpu.SemaphoreType.DMA((64,)),
+            pltpu.SemaphoreType.DMA((4,)),
+        ],
+        compiler_params=pltpu.CompilerParams(
+            collective_id=0, has_side_effects=True, vmem_limit_bytes=50 * 2**20
+        ),
+        name="gather_weights",
+    )(qkv_pre, fc_pre, out_s, proj_s, vec_pre)
+
+
+def scatter_kernel(nz, qkv_g, fc_g, proj_g, out_g, vec_g, qkv_o, fc_o, proj_o, out_o, vec_o,
+                   qkv_x, fc_x, proj_x, qkv_s, fc_s, proj_s, qkv_z, fc_z, proj_z, qkv_f, fc_f, proj_f,
+                   out_c, out_1, out_y, out_2, out_x, out_3, out_z, vec_p, vec_1, vec_z, vec_2, vec_x,
+                   send_sem, recv_sem, fsend_sem, frecv_sem):
+    net = Net(send_sem, recv_sem, nz)
+    x, z, u = net.x, net.z, net.u
+    y, c = u // 2, lax.rem(u, 2)
+    net.enter()
+    vec_m = [net.send(vec_g, vec_p.at[m - 1], net.plane(m)) for m in (1, 2, 3)]
+
+    def start_x(grad, land):
+        return [
+            net.send(grad.at[rows_at(192 * zz + 96 * (1 - x), 96)], land.at[zz], net.other_x())
+            for zz in range(nz)
+        ]
+
+    def start_z(copies, grad, land, mine, land_z):
+        for zz in range(nz):
+            copies[zz].wait_recv()
+            mine[zz] = (grad[rows_at(192 * zz + 96 * x, 96), :].astype(F32) + land[zz].astype(F32)).astype(BF)
+        return [
+            net.send(mine.at[net.zplus(d)], land_z.at[d - 1], net.line(d)) for d in range(1, nz)
+        ]
+
+    def end_z(copies, mine, land_z, final):
+        total = mine[z].astype(F32)
+        for d in range(nz - 1):
+            copies[d].wait_recv()
+            total = total + land_z[d].astype(F32)
+        final[...] = total.astype(BF)
+
+    out_first = net.send(out_g.at[1 - c], out_c, net.plane(1))
+    proj_a = start_x(proj_g, proj_x)
+    fc_a = start_x(fc_g, fc_x)
+    qkv_a = start_x(qkv_g, qkv_x)
+    out_first.wait_recv()
+    out_1[...] = (out_g[c].astype(F32) + out_c[...].astype(F32)).astype(BF)
+    out_second = net.send(out_1.at[1 - y], out_y, net.plane(2))
+    total = vec_g[...]
+    for m in range(3):
+        vec_m[m].wait_recv()
+        total = total + vec_p[m]
+    vec_1[...] = total
+    vec_l = [net.send(vec_1, vec_z.at[d - 1], net.line(d)) for d in range(1, nz)]
+    proj_b = start_z(proj_a, proj_g, proj_x, proj_s, proj_z)
+    fc_b = start_z(fc_a, fc_g, fc_x, fc_s, fc_z)
+    out_second.wait_recv()
+    out_2[...] = (out_1[y].astype(F32) + out_y[...].astype(F32)).astype(BF)
+    half = lambda which: pl.ds(pl.multiple_of(384 * which, 128), 384)
+    out_third = net.send(out_2.at[:, half(1 - x)], out_x, net.other_x())
+    total = vec_1[...]
+    for d in range(nz - 1):
+        vec_l[d].wait_recv()
+        total = total + vec_z[d]
+    vec_2[...] = total
+    vec_last = net.send(vec_2, vec_x, net.other_x())
+    qkv_b = start_z(qkv_a, qkv_g, qkv_x, qkv_s, qkv_z)
+    out_third.wait_recv()
+    out_3[...] = (out_2[:, half(x)].astype(F32) + out_x[...].astype(F32)).astype(BF)
+    out_l = [
+        net.send(out_3.at[rows_at(48 * net.zplus(d), 48)], out_z.at[d - 1], net.line(d))
+        for d in range(1, nz)
+    ]
+    end_z(proj_b, proj_s, proj_z, proj_f)
+    proj_o[rows_at(96 * x, 96), :] = proj_f[...]
+    mine = rows_at(96 * x, 96)
+    proj_c = net.send(proj_f, proj_o.at[mine], net.other_x())
+
+    finals = []
+
+    def hand_out(base, final, native):
+        for xx in range(2):
+            for cc in range(2):
+                target_x = x ^ xx
+                target_u = 2 * x + cc
+                here = jnp.logical_and(xx == 0, target_u == u)
+                src = final.at[pl.ds(48 * cc, 48)]
+                k = base + 2 * xx + cc
+                copy = pltpu.make_async_remote_copy(
+                    src_ref=src, dst_ref=native.at[u], send_sem=fsend_sem.at[k],
+                    recv_sem=frecv_sem.at[base + u], device_id=(target_x, z, target_u), device_id_type=MESH)
+
+                @pl.when(jnp.logical_not(here))
+                def _():
+                    copy.start()
+
+                @pl.when(here)
+                def _():
+                    native[u] = final[pl.ds(48 * cc, 48), :]
+
+                finals.append((here, copy))
+
+    def await_native(base, final, native):
+        for who in range(4):
+            copy = pltpu.make_async_remote_copy(
+                src_ref=final.at[pl.ds(0, 48)], dst_ref=native.at[who], send_sem=fsend_sem.at[base],
+                recv_sem=frecv_sem.at[base + who], device_id=(1 - x, z, u), device_id_type=MESH)
+
+            @pl.when(jnp.logical_not(jnp.logical_and(x == y, u == who)))
+            def _():
+                copy.wait_recv()
+
+    end_z(fc_b, fc_s, fc_z, fc_f)
+    hand_out(0, fc_f, fc_o)
+    total = out_3[rows_at(48 * z, 48), :].astype(F32)
+    for d in range(nz - 1):
+        out_l[d].wait_recv()
+        total = total + out_z[d].astype(F32)
+    out_o[:, half(x)] = total.astype(BF)
+    out_last = net.send(out_o.at[:, half(x)], out_o.at[:, half(x)], net.other_x())
+    end_z(qkv_b, qkv_s, qkv_z, qkv_f)
+    hand_out(4, qkv_f, qkv_o)
+    vec_last.wait_recv()
+    vec_o[...] = vec_2[...] + vec_x[...]
+    proj_c.wait_recv()
+    out_last.wait_recv()
+    await_native(0, fc_f, fc_o)
+    await_native(4, qkv_f, qkv_o)
+    for here, copy in finals:
+        @pl.when(jnp.logical_not(here))
+        def _():
+            copy.wait_send()
+    net.finish()
+
+
+def scatter_grads(nz, qkv_g, fc_g, proj_g, out_g, vec_g):
+    def vm(*shape, kind=BF):
+        return pltpu.VMEM(shape, kind)
+
+    return pl.pallas_call(
+        functools.partial(scatter_kernel, nz),
+        out_shape=(
+            jax.ShapeDtypeStruct((4, 48, 576), BF),
+            jax.ShapeDtypeStruct((4, 48, 768), BF),
+            jax.ShapeDtypeStruct((192, 768), BF),
+            jax.ShapeDtypeStruct((48, 768), BF),
+            jax.ShapeDtypeStruct((16, 768), F32),
+        ),
+        in_specs=[VSPEC] * 5,
+        out_specs=(VSPEC,) * 5,
+        scratch_shapes=[
+            vm(nz, 96, 576), vm(nz, 96, 768), vm(nz, 96, 768),
+            vm(nz, 96, 576), vm(nz, 96, 768), vm(nz, 96, 768),
+            vm(nz - 1, 96, 576), vm(nz - 1, 96, 768), vm(nz - 1, 96, 768),
+            vm(96, 576), vm(96, 768), vm(96, 768),
+            vm(2, 192, 768), vm(2, 192, 768), vm(192, 768), vm(192, 768), vm(192, 384), vm(192, 384), vm(nz - 1, 48, 384),
+            vm(3, 16, 768, kind=F32), vm(16, 768, kind=F32), vm(nz - 1, 16, 768, kind=F32), vm(16, 768, kind=F32), vm(16, 768, kind=F32),
+            pltpu.SemaphoreType.DMA((48,)),
+            pltpu.SemaphoreType.DMA((48,)),
+            pltpu.SemaphoreType.DMA((8,)),
+            pltpu.SemaphoreType.DMA((8,)),
+        ],
+        compiler_params=pltpu.CompilerParams(
+            collective_id=1, has_side_effects=True, vmem_limit_bytes=50 * 2**20
+        ),
+        name="scatter_grads",
+    )(qkv_g, fc_g, proj_g, out_g, vec_g)
+
+
+def arrange_qkv(w):
+    rows = w.shape[0]
+    parts = w.reshape(rows, 3, 4, 3, 64)
+    order = ((0, 0), (0, 1), (1, 0), (1, 1), (2, 0), (2, 1), (1, 2), (2, 2), (0, 2))
+    return jnp.stack([parts[:, t, :, h] for t, h in order], 2).transpose(1, 0, 2, 3).reshape(4, rows, 576)
+
+
+def restore_qkv(g):
+    rows = g.shape[1]
+    parts = g.reshape(4, rows, 9, 64)
+    q = jnp.stack([parts[:, :, i] for i in (0, 1, 8)], 2)
+    k = jnp.stack([parts[:, :, i] for i in (2, 3, 6)], 2)
+    v = jnp.stack([parts[:, :, i] for i in (4, 5, 7)], 2)
+    return jnp.stack([q, k, v], 0).transpose(2, 0, 1, 3, 4).reshape(rows, 2304)
+
+
+def device_fast(nz, inputs, stretch_order, norm_gains, biases, mid_shift, value_bias, qkv_weight, out_weight, fc_weight, fc_bias, proj_weight, cotangent):
+    x, z, u = lax.axis_index("dp"), lax.axis_index("blk"), lax.axis_index("uly")
+    qkv_pre = arrange_qkv(qkv_weight)
+    fc_pre = fc_weight.reshape(48, nz, 4, 192).transpose(2, 0, 1, 3).reshape(4, 48, 768)
+    pack = jnp.concatenate([norm_gains, biases, mid_shift[None], value_bias[None]], 0)
+    place = (4 * z + u) * 48
+    vec8 = lax.dynamic_update_slice(jnp.zeros((8, 768), BF), pack, (0, place))
+    fcb = lax.dynamic_update_slice(jnp.zeros((1, 768), BF), fc_bias[None], (0, 192 * z))
+    wide = lax.dynamic_update_slice(jnp.zeros((2, 192), BF), jnp.stack([biases[1], value_bias]), (0, 48 * u))
+    zero = jnp.zeros((64,), BF)
+    q, v = wide[0].reshape(3, 64), wide[1].reshape(3, 64)
+    local = jnp.concatenate([q[0], q[1], zero, zero, v[0], v[1], zero, v[2], q[2], jnp.zeros((192,), BF)])[None]
+    four = lax.dynamic_update_slice(jnp.zeros((4, 768), BF), local, (z, 0))
+    vec_pre = jnp.concatenate([vec8, fcb, four, jnp.zeros((3, 768), BF)], 0)
+    w_qkv, w_fc, w_proj, w_out, vec = gather_weights(nz, qkv_pre, fc_pre, out_weight, proj_weight, vec_pre)
+    bias_u = lax.dynamic_slice(vec, (9 + u, 0), (1, 576))
+    gains, shifts = vec[0:2], vec[2:6]
+    x_own = inputs[0]
+    x_all = lax.all_gather(x_own, "uly", axis=0, tiled=True).astype(F32)
+    cot_own = cotangent[0]
+    cot_all = lax.all_gather(cot_own, "uly", axis=0, tiled=True)
+    ln_all, _, _ = layer_norm(x_all, gains[0], shifts[0])
+    ln_all = ln_all.astype(BF)
+    _, normed_in, inverse_in = layer_norm(x_own.astype(F32), gains[0], shifts[0])
+    qkv = (jnp.dot(ln_all, w_qkv, preferred_element_type=F32) + bias_u).astype(BF)
+    kv_all = lax.all_gather(qkv[:, 128:512], "blk", axis=0, tiled=True)
+
+    def heads(cols, arr):
+        return jnp.stack([arr[:, c:c + 64] for c in cols], 0)
+
+    qh = heads((0, 64, 512), qkv)
+    kh, vh = heads((0, 64, 256), kv_all), heads((128, 192, 320), kv_all)
+    pos = (stretch_order[0][:, None] * 64 + jnp.arange(64, dtype=jnp.int32)[None]).reshape(-1)
+    qpos = lax.dynamic_slice(pos, (512 * z,), (512,))
+    causal = qpos[:, None] >= pos[None, :]
+    s = jnp.where(causal[None], jnp.einsum("hqd,hkd->hqk", qh, kh, preferred_element_type=F32) * 0.125, -1e30)
+    p = jax.nn.softmax(s, -1)
+    pl_ = p.astype(BF)
+    att = jnp.einsum("hqk,hkd->hqd", pl_, vh, preferred_element_type=F32)
+    att_l = att.astype(BF).transpose(1, 0, 2).reshape(4, 128, 192)
+    merged = lax.all_to_all(att_l, "uly", 0, 0, tiled=True).transpose(1, 0, 2).reshape(128, 768)
+    resid = x_own.astype(F32) + jnp.dot(merged, w_out, preferred_element_type=F32) + shifts[2]
+    ln_mid, normed_mid, inverse_mid = layer_norm(resid, gains[1], vec[6])
+    lm_all = lax.all_gather(ln_mid.astype(BF), "uly", axis=0, tiled=True)
+    pre = jnp.dot(lm_all, w_fc, preferred_element_type=F32) + vec[8]
+    act, back = jax.vjp(lambda t: jax.nn.gelu(t, approximate=True), pre)
+    act = act.astype(BF)
+    out_part = jnp.dot(act, w_proj, preferred_element_type=F32)
+    branch = lax.psum_scatter(out_part, "uly", scatter_dimension=0, tiled=True)
+    output = (resid + branch + shifts[3]).astype(BF)
+    proj_g = jnp.einsum("ta,tb->ab", act, cot_all, preferred_element_type=F32).astype(BF)
+    gact = jnp.einsum("tb,ab->ta", cot_all, w_proj, preferred_element_type=F32)
+    grad_pre = back(gact)[0].astype(BF)
+    fc_g = jnp.einsum("ta,tb->ab", lm_all, grad_pre, preferred_element_type=F32).astype(BF)
+    fcb_g = jnp.sum(grad_pre.astype(F32), 0)
+    gm_part = jnp.einsum("tb,ab->ta", grad_pre, w_fc, preferred_element_type=F32)
+    grad_mid = lax.psum_scatter(gm_part, "uly", scatter_dimension=0, tiled=True)
+    cot32 = cot_own.astype(F32)
+    grad_resid = cot32 + norm_back(grad_mid, normed_mid, inverse_mid, gains[1])
+    gb = grad_resid.astype(BF)
+    out_g = jnp.einsum("ta,tb->ab", merged, gb, preferred_element_type=F32).astype(BF)
+    gmer = jnp.einsum("tb,ab->ta", gb, w_out, preferred_element_type=F32).astype(BF)
+    ga = lax.all_to_all(gmer.reshape(128, 4, 192).transpose(1, 0, 2), "uly", 0, 0, tiled=True)
+    ga = ga.reshape(512, 3, 64).transpose(1, 0, 2)
+    gp = jnp.einsum("hqd,hkd->hqk", ga, vh, preferred_element_type=F32)
+    delta = jnp.sum(ga.astype(F32) * att, -1, keepdims=True)
+    gs = (p * (gp - delta)).astype(BF)
+    gq = (jnp.einsum("hqk,hkd->qhd", gs, kh, preferred_element_type=F32) * 0.125).astype(BF)
+    gk = jnp.einsum("hqk,hqd->khd", gs, qh, preferred_element_type=F32) * 0.125
+    gv = jnp.einsum("hqk,hqd->khd", pl_, ga, preferred_element_type=F32)
+    kvg = jnp.concatenate([gk[:, 0], gk[:, 1], gv[:, 0], gv[:, 1], gk[:, 2], gv[:, 2]], 1)
+    kvg = lax.psum_scatter(kvg, "blk", scatter_dimension=0, tiled=True).astype(BF)
+    gqkv = jnp.concatenate([gq[:, 0], gq[:, 1], kvg, gq[:, 2]], 1)
+    qkv_g = jnp.einsum("ta,tb->ab", ln_all, gqkv, preferred_element_type=F32).astype(BF)
+    qsum = jnp.sum(gqkv.astype(F32), 0)
+    gin_part = jnp.einsum("tb,ab->ta", gqkv, w_qkv, preferred_element_type=F32)
+    gin = lax.psum_scatter(gin_part, "uly", scatter_dimension=0, tiled=True)
+    input_grad = (grad_resid + norm_back(gin, normed_in, inverse_in, gains[0])).astype(BF)
+    rows = jnp.stack([
+        jnp.sum(gin * normed_in, 0), jnp.sum(grad_mid * normed_mid, 0), jnp.sum(gin, 0),
+        jnp.sum(gb.astype(F32), 0), jnp.sum(cot32, 0), jnp.sum(grad_mid, 0)])
+    qrow = lax.dynamic_update_slice(jnp.zeros((4, 768), F32), jnp.pad(qsum, (0, 192))[None], (u, 0))
+    frow = lax.dynamic_update_slice(jnp.zeros((4, 768), F32), fcb_g[None], (u, 0))
+    vec_g = jnp.concatenate([rows, qrow, frow, jnp.zeros((2, 768), F32)], 0)
+    og = out_g.reshape(nz, 2, 2, 48, 768).transpose(2, 1, 0, 3, 4).reshape(2, 2, 192, 768)
+    qkv_o, fc_o, proj_o, out_o, vec_o = scatter_grads(nz, qkv_g, fc_g, proj_g, og, vec_g)
+    mine = lax.dynamic_slice(vec_o, (0, place), (6, 48))
+    qs = lax.dynamic_slice(vec_o, (6 + z, 0), (1, 576))[0].reshape(9, 64)
+    qb = lax.dynamic_slice(jnp.concatenate([qs[0], qs[1], qs[8]]), (48 * u,), (48,))
+    vb = lax.dynamic_slice(jnp.concatenate([qs[4], qs[5], qs[7]]), (48 * u,), (48,))
+    fb = lax.dynamic_slice(vec_o, (10 + u, 192 * z), (1, 192))[0]
+    return (
+        output[None], input_grad[None], mine[0:2],
+        jnp.stack([mine[2], qb, mine[3], mine[4]]), mine[5], vb,
+        restore_qkv(qkv_o).astype(F32), out_o.astype(F32),
+        fc_o.reshape(4, 48, nz, 192).transpose(1, 2, 0, 3).reshape(48, 3072).astype(F32), fb, proj_o.astype(F32))
+
+
 def solution(mesh):
     placed = (
         P("dp", ("blk", "uly"), None),
@@ -320,8 +778,12 @@
         P(("blk", "uly"), None),
         P("dp", ("blk", "uly"), None),
     )
+    sizes = dict(mesh.shape)
+    nz = sizes["blk"]
+    fast = sizes["uly"] == 4 and sizes["dp"] == 2 and 768 % (nz * 4 * 16) == 0
+    chosen = functools.partial(device_fast, nz) if fast else per_device
     return jax.shard_map(
-        per_device,
+        chosen,
         mesh=mesh,
         in_specs=placed,
         out_specs=(

time: 909 us -> 465 us (0.51)
  waiting for transfers between devices: 470 us -> 156 us
  blocking collectives: 228 us -> 35.8 us
  Pallas kernels: 0 us -> 130 us
  matrix products: 82.3 us -> 53.3 us
  other arithmetic: 45.6 us -> 26.1 us
    reduce_scatter x4, waiting for transfers between devices: 346 us -> 122 us  [the longest x1 54.5 us: device_fast(): lax.psum_scatter(kvg, 'blk', scatter_dimension=0, tiled=True).astype(BF)]
    pallas_call x0 -> x2, Pallas kernels: none -> 130 us  [the longest x1 65.9 us: gather_weights(): pl.pallas_call(functools.partial(gather_kernel, nz), out_shape=(jax.Shape...]
    unnamed x2 -> x0, blocking collectives: 118 us -> none
    unnamed x15 -> x5, waiting for transfers between devices: 72.2 us -> 0.08 us
    all_gather x4 -> x3, blocking collectives: 87.4 us -> 28.1 us  [the longest x1 10.8 us: device_fast(): cot_all = lax.all_gather(cot_own, 'uly', axis=0, tiled=True)]
    dot_general x26 -> x17, matrix products: 82.3 us -> 42.4 us  [the longest x1 5.8 us: device_fast(): gp = jnp.einsum('hqd,hkd->hqk', ga, vh, preferred_element_type=F32)]
    all_gather x4 -> x1, waiting for transfers between devices: 0.08 us -> 34.5 us  [device_fast(): kv_all = lax.all_gather(qkv[:, 128:512], 'blk', axis=0, tiled=True)]
    psum x1 -> x0, waiting for transfers between devices: 30.5 us -> none  [per_device(): lax.psum(shard_grads[4].astype(jnp.bfloat16), 'dp').astype(jnp.float32)]
  transfers between devices with their start and end apart: 15 -> 6, of which waited for: 10 -> 5; matrix products, arithmetic and copies ran while one was open for 12% -> 5% of each run, Pallas kernels for 0% -> 0%
where the time goes in v1:
time: 465 us; the launch traced here: 459 us
  waiting for transfers between devices  156 us (34%)
  Pallas kernels  130 us (28%)
  matrix products  53.3 us (11%)
  local copies, waits for them, and re-layouts  39.5 us (8%)
  blocking collectives  35.8 us (8%)
  other arithmetic  26.1 us (6%)
  between operations  15.4 us (3%)
    pallas_call x1, Pallas kernels, gather_weights(): pl.pallas_call(functools.partial(gather_kernel, nz), out_shape=(jax.Shape...  65.9 us
    pallas_call x1, Pallas kernels, scatter_grads(): pl.pallas_call(functools.partial(scatter_kernel, nz), out_shape=(jax.Shap...  63.8 us
    reduce_scatter x1, waiting for transfers between devices, device_fast(): lax.psum_scatter(kvg, 'blk', scatter_dimension=0, tiled=True).astype(BF)  54.5 us
    all_gather x1, waiting for transfers between devices, device_fast(): kv_all = lax.all_gather(qkv[:, 128:512], 'blk', axis=0, tiled=True)  34.5 us
    reduce_scatter x1, waiting for transfers between devices, device_fast(): branch = lax.psum_scatter(out_part, 'uly', scatter_dimension=0, tiled=True)  29.1 us
    reduce_scatter x1, waiting for transfers between devices, device_fast(): grad_mid = lax.psum_scatter(gm_part, 'uly', scatter_dimension=0, tiled=True)  21.3 us
    reduce_scatter x1, waiting for transfers between devices, device_fast(): gin = lax.psum_scatter(gin_part, 'uly', scatter_dimension=0, tiled=True)  16.7 us
    unnamed x163, local copies, waits for them, and re-layouts  13.3 us
  transfers between devices with their start and end apart: 6, of which 5 were waited for; matrix products, arithmetic and copies ran while one was open for 5% of the time, Pallas kernels for 0%

profile of v1, /device:TPU:0, one launch (start us, length us, event | category | flops | bytes accessed | tf_op | source)
XLA Modules:
  0.0 459.4 jit_solution(17073200853970762629)
XLA Ops:
  14.7 65.9 %gather_weights.1 = (bf16[768,576]{1,0:T(8,128)(2,1)S(1)}, bf16[768,768]{1,0:T(8,128)(2,1)S(1)}, bf16[768,768]{1,0:T(8,128)(2,1)}, bf16[768,768]{1,0:T(8,128)(2,1)}, f32[16,768]{1,0:T(8,128)S(1)}) custom-call(bf16[4,48,576]{2,1,0:T(8,128)(2,1)S(1)} %reshape.196.qkv_pre, bf16[4,48,768]{2,1,0:T(8,128)(2,1)S(1)} %reshape.198.fc_pre, ...), custom_call_target="tpu_custom_call" | custom-call | tf_op jit(solution)/shard_map/gather_weights/pallas_call | solution.py:467
  81.3 8.4 %all-gather = bf16[1,512,768]{2,1,0:T(8,128)(2,1)S(1)} all-gather(bf16[1,128,768]{2,1,0:T(8,128)(2,1)S(1)} %copy-done.3), channel_id=2, replica_groups=mesh['dp'=2,'blk'=4,'uly'=4] {'uly'}, dimensions={1}, use_global_device_ids=true | all-gather | bytes 983040 | tf_op jit(solution)/shard_map/all_gather | solution.py:686
  96.3 34.5 %all-gather.4.cloned.1.call-done = bf16[2048,384]{0,1:T(8,128)(2,1)} async-done(((bf16[512,384]{0,1:T(8,128)(2,1)}), bf16[2048,384]{0,1:T(8,128)(2,1)}) %all-gather.4.cloned.1.call-update) | async-done | bytes 1572880 | tf_op jit(solution)/shard_map/all_gather | solution.py:693
  130.8 2.4 slice_bitcast_fusion.8
  133.2 10.9 %fusion.73 = (f32[3,512]{1,0:T(4,128)}, f32[3,512,2048]{2,1,0:T(8,128)}) fusion(pred[512,2048]{1,0:T(8,128)(4,1)} %broadcast_compare_fusion, bf16[1,512,64]{1,2,0:T(8,128)(2,1)S(1)} %get-tuple-element.61, bf16[1,512,64]{1,2,0:T(8,128)(2,1)} %get-tuple-element.62, bf16[1,512,64]{1,2,0:T(8,128)(2,1)S(1)} %get-tuple-element.60, ...), kind=kOutput, calls=%fused_computation.186 | convolution fusion | flops 416221184 | bytes 14620672 | tf_op jit(solution)/shard_map/sub | solution.py:704
  144.2 9.1 %fusion.5 = bf16[3,512,2048]{2,1,0:T(8,128)(2,1)} fusion(f32[3,512,2048]{2,1,0:T(8,128)} %get-tuple-element.93, f32[3,512]{1,0:T(4,128)} %get-tuple-element.92), kind=kLoop, calls=%fused_computation.9 | loop fusion | flops 6291456 | bytes 18880512 | tf_op jit(solution)/shard_map/convert_element_type | solution.py:705
  153.3 4.8 %fusion.52 = f32[3,512,64]{1,2,0:T(8,128)S(1)} fusion(bf16[3,512,2048]{2,1,0:T(8,128)(2,1)} %fusion.5, bf16[1,2048,64]{1,2,0:T(8,128)(2,1)S(1)} %copy-done.31, bf16[1,2048,64]{1,2,0:T(8,128)(2,1)S(1)} %copy-done.33, bf16[1,2048,64]{1,2,0:T(8,128)(2,1)S(1)} %copy-done.29), kind=kOutput, calls=%fused_computation.101 | convolution fusion | flops 403439616 | bytes 7471104 | tf_op jit(solution)/shard_map/hqk,hkd->hqd/dot_general | solution.py:706
  161.2 3.4 all-to-all-start
  164.6 10.8 %all-gather.1 = bf16[1,512,768]{2,1,0:T(8,128)(2,1)} all-gather(bf16[1,128,768]{2,1,0:T(8,128)(2,1)S(1)} %copy-done.8), channel_id=3, replica_groups=mesh['dp'=2,'blk'=4,'uly'=4] {'uly'}, dimensions={1}, use_global_device_ids=true | all-gather | bytes 983040 | tf_op jit(solution)/shard_map/all_gather | solution.py:688
  178.2 8.9 %all_gather.14 = bf16[512,768]{1,0:T(8,128)(2,1)S(1)} all-gather(bf16[128,768]{1,0:T(8,128)(2,1)S(1)} %add_convert_fusion.1), channel_id=1, replica_groups=mesh['dp'=2,'blk'=4,'uly'=4] {'uly'}, dimensions={0}, use_global_device_ids=true | all-gather | bytes 983040 | tf_op jit(solution)/shard_map/all_gather | solution.py:711
  189.0 2.2 convert_reduce_fusion.1
  195.3 3.7 fusion.67
  199.0 21.3 %reduce-scatter.7.cloned.1.call-done = f32[128,768]{1,0:T(8,128)} async-done(((f32[512,768]{1,0:T(8,128)}), f32[128,768]{1,0:T(8,128)}) %reduce-scatter.7.cloned.1.call-update) | async-done | bytes 393232 | tf_op jit(solution)/shard_map/reduce_scatter | solution.py:724
  222.1 29.1 %reduce-scatter.5.cloned.1.call-done = f32[128,768]{1,0:T(8,128)} async-done(((f32[512,768]{1,0:T(8,128)}), f32[128,768]{1,0:T(8,128)}) %reduce-scatter.5.cloned.1.call-update) | async-done | bytes 393232 | tf_op jit(solution)/shard_map/reduce_scatter | solution.py:716
  251.2 2.6 convert_reduce_fusion.5
  255.9 7.7 %all_to_all.10 = bf16[4,128,192]{1,2,0:T(8,128)(2,1)S(1)} all-to-all(bf16[4,128,192]{1,2,0:T(8,128)(2,1)S(1)} %bitcast.243), channel_id=1, replica_groups=mesh['dp'=2,'blk'=4,'uly'=4] {'uly'}, dimensions={0} | all-to-all | bytes 393216 | tf_op jit(solution)/shard_map/all_to_all | solution.py:730
  263.9 4.1 convolution_bitcast_fusion
  268.1 5.8 %multiply_convert_fusion = bf16[3,512,2048]{2,1,0:T(8,128)(2,1)S(1)} fusion(f32[3,512]{1,0:T(4,128)S(1)} %multiply_reduce_fusion.1, f32[3,512,2048]{2,1,0:T(8,128)} %get-tuple-element.93, f32[3,512]{1,0:T(4,128)S(1)} %copy-done.45, bf16[1,2048,64]{1,2,0:T(8,128)(2,1)S(1)} %copy-done.32, bf16[1,2048,64]{1,2,0:T(8,128)(2,1)S(1)} %copy-done.34, ...), kind=kOutput, calls=%fused_computation.1 | convolution fusion | flops 416022528 | bytes 19869696 | tf_op jit(solution)/shard_map/hqd,hkd->hqk/dot_general | solution.py:732
  282.8 4.8 %fusion.29 = bf16[512,3,64]{0,2,1:T(8,128)(2,1)S(1)} fusion(bf16[3,512,2048]{2,1,0:T(8,128)(2,1)} %copy-done.2, bf16[1,2048,64]{1,2,0:T(8,128)(2,1)S(1)} %copy-done.16, bf16[1,2048,64]{1,2,0:T(8,128)(2,1)S(1)} %copy-done.17, bf16[1,2048,64]{1,2,0:T(8,128)(2,1)S(1)} %copy-done.18), kind=kOutput, calls=%fused_computation.54 | convolution fusion | flops 403636224 | bytes 7274496 | tf_op jit(solution)/shard_map/hqk,hkd->qhd/dot_general | solution.py:735
  287.7 54.5 %reduce-scatter.9.cloned.1.call-done = f32[512,384]{0,1:T(8,128)} async-done(((f32[2048,384]{0,1:T(8,128)}), f32[512,384]{0,1:T(8,128)}) %reduce-scatter.9.cloned.1.call-update) | async-done | bytes 786448 | tf_op jit(solution)/shard_map/reduce_scatter | solution.py:739
  344.1 2.0 fusion.66
  348.0 2.3 convolution_convert_fusion.2.fc_g
  357.8 16.7 %reduce-scatter.11.cloned.1.call-done = f32[128,768]{1,0:T(8,128)} async-done(((f32[512,768]{1,0:T(8,128)}), f32[128,768]{1,0:T(8,128)}) %reduce-scatter.11.cloned.1.call-update) | async-done | bytes 393232 | tf_op jit(solution)/shard_map/reduce_scatter | solution.py:744
  376.4 63.8 %scatter_grads.1 = (bf16[4,48,576]{2,1,0:T(8,128)(2,1)S(1)}, bf16[4,48,768]{2,1,0:T(8,128)(2,1)S(1)}, bf16[192,768]{1,0:T(8,128)(2,1)S(1)}, bf16[48,768]{1,0:T(8,128)(2,1)S(1)}, f32[16,768]{1,0:T(8,128)S(1)}) custom-call(bf16[768,576]{1,0:T(8,128)(2,1)S(1)} %copy.71.qkv_g, bf16[768,768]{1,0:T(8,128)(2,1)S(1)} %convolution_convert_fusion.2.fc_g, ...), custom_call_target="tpu_custom_call" | custom-call | tf_op jit(solution)/shard_map/scatter_grads/pallas_call | solution.py:622
  (292 shorter events, 64.6 us)
Async XLA Ops:
  7.2 123.6 %all-gather.4.cloned.1.call-start = ((), (), s32[]{:S(2)}) async-start(), calls=%async_computation.6 | async-start | bytes 1966080 | tf_op jit(solution)/shard_map/all_gather | solution.py:693
  13.1 68.2 %copy-start.3 = (bf16[1,128,768]{2,1,0:T(8,128)(2,1)S(1)}, bf16[1,128,768]{2,1,0:T(8,128)(2,1)}, u32[]{:S(2)}) copy-start(bf16[1,128,768]{2,1,0:T(8,128)(2,1)} %param.12) | copy-start | bytes 589828
  81.2 9.9 %copy-start.55 = (f32[768]{0:T(1024)}, f32[768]{0:T(1024)S(1)}, u32[]{:S(2)}) copy-start(f32[768]{0:T(1024)S(1)} %get-tuple-element.44) | copy-start | bytes 9220
  94.6 38.7 %copy-start.24 = (bf16[1,512,64]{1,2,0:T(8,128)(2,1)}, bf16[1,512,64]{1,2,0:T(8,128)(2,1)S(1)}, u32[]{:S(2)}) copy-start(bf16[1,512,64]{1,2,0:T(8,128)(2,1)S(1)} %get-tuple-element.60) | copy-start | bytes 196612
  94.6 38.7 %copy-start.26 = (bf16[1,512,64]{1,2,0:T(8,128)(2,1)}, bf16[1,512,64]{1,2,0:T(8,128)(2,1)S(1)}, u32[]{:S(2)}) copy-start(bf16[1,512,64]{1,2,0:T(8,128)(2,1)S(1)} %get-tuple-element.61) | copy-start | bytes 196612
  133.2 10.9 %copy-start.15 = (bf16[1,2048,64]{1,2,0:T(8,128)(2,1)}, bf16[1,2048,64]{1,2,0:T(8,128)(2,1)S(1)}, u32[]{:S(2)}) copy-start(bf16[1,2048,64]{1,2,0:T(8,128)(2,1)S(1)} %get-tuple-element.51) | copy-start | bytes 786436
  161.2 14.2 %all-to-all-start = ((bf16[4,128,192]{1,2,0:T(8,128)(2,1)}), bf16[4,128,192]{1,2,0:T(8,128)(2,1)S(1)}, u32[]{:S(2)}, u32[]{:S(2)}) async-start(bf16[4,128,192]{1,2,0:T(8,128)(2,1)} %copy.67), calls=%async_computation | async-start | bytes 393216 | tf_op jit(solution)/shard_map/all_to_all | solution.py:708
  164.6 55.7 %reduce-scatter.7.cloned.1.call-start = ((), (), s32[]{:S(2)}) async-start(), calls=%async_computation.8 | async-start | bytes 1966080 | tf_op jit(solution)/shard_map/reduce_scatter | solution.py:724
  176.1 11.1 %copy-start.57 = (f32[768]{0:T(1024)S(1)}, f32[768]{0:T(1024)}, u32[]{:S(2)}) copy-start(f32[768]{0:T(1024)} %get-tuple-element.40) | copy-start | bytes 9220
  177.9 9.3 %copy-start.46 = (f32[128]{0:T(128)}, f32[128]{0:T(128)S(1)}, u32[]{:S(2)}) copy-start(f32[128]{0:T(128)S(1)} %broadcast_multiply_fusion.6) | copy-start | bytes 1540
  178.1 9.1 %copy-start.53 = (f32[128]{0:T(128)}, f32[128]{0:T(128)S(1)}, u32[]{:S(2)}) copy-start(f32[128]{0:T(128)S(1)} %add_rsqrt_fusion.2) | copy-start | bytes 1540
  194.0 57.2 %reduce-scatter.5.cloned.1.call-start = ((), (), s32[]{:S(2)}) async-start(), calls=%async_computation.7 | async-start | bytes 1966080 | tf_op jit(solution)/shard_map/reduce_scatter | solution.py:716
  198.9 21.4 %copy-start.47 = (f32[128]{0:T(128)S(1)}, f32[128]{0:T(128)}, u32[]{:S(2)}) copy-start(f32[128]{0:T(128)} %copy-done.46) | copy-start | bytes 1540
  198.9 21.4 %copy-start.54 = (f32[128]{0:T(128)S(1)}, f32[128]{0:T(128)}, u32[]{:S(2)}) copy-start(f32[128]{0:T(128)} %copy-done.53) | copy-start | bytes 1540
  198.9 52.3 %copy-start.9 = (bf16[1,128,768]{2,1,0:T(8,128)(2,1)S(1)}, bf16[1,128,768]{2,1,0:T(8,128)(2,1)}, u32[]{:S(2)}) copy-start(bf16[1,128,768]{2,1,0:T(8,128)(2,1)} %param.23) | copy-start | bytes 589828
  199.0 143.2 %reduce-scatter.9.cloned.1.call-start = ((), (), s32[]{:S(2)}) async-start(), calls=%async_computation.9 | async-start | bytes 3932160 | tf_op jit(solution)/shard_map/reduce_scatter | solution.py:739
  253.8 98.7 %copy-start.4 = (f32[128,768]{1,0:T(8,128)}, f32[128,768]{1,0:T(8,128)S(1)}, u32[]{:S(2)}) copy-start(f32[128,768]{1,0:T(8,128)S(1)} %get-tuple-element.47) | copy-start | bytes 1179652
  281.8 92.7 %reduce-scatter.11.cloned.1.call-start = ((), (), s32[]{:S(2)}) async-start(), calls=%async_computation.10 | async-start | bytes 1966080 | tf_op jit(solution)/shard_map/reduce_scatter | solution.py:744
  287.7 58.4 %copy-start.35 = (bf16[512,64]{0,1:T(8,128)(2,1)}, bf16[512,64]{0,1:T(8,128)(2,1)S(1)}, u32[]{:S(2)}) copy-start(bf16[512,64]{0,1:T(8,128)(2,1)S(1)} %get-tuple-element.73) | copy-start | bytes 196612
  287.7 58.4 %copy-start.37 = (bf16[512,64]{0,1:T(8,128)(2,1)}, bf16[512,64]{0,1:T(8,128)(2,1)S(1)}, u32[]{:S(2)}) copy-start(bf16[512,64]{0,1:T(8,128)(2,1)S(1)} %get-tuple-element.74) | copy-start | bytes 196612
  287.7 58.4 %copy-start.39 = (bf16[512,64]{0,1:T(8,128)(2,1)}, bf16[512,64]{0,1:T(8,128)(2,1)S(1)}, u32[]{:S(2)}) copy-start(bf16[512,64]{0,1:T(8,128)(2,1)S(1)} %get-tuple-element.75) | copy-start | bytes 196612
  356.2 18.3 %copy-start.51 = (f32[128]{0:T(128)S(1)}, f32[128]{0:T(128)}, u32[]{:S(2)}) copy-start(f32[128]{0:T(128)} %copy-done.50) | copy-start | bytes 1540
  356.2 18.3 %copy-start.59 = (f32[128]{0:T(128)S(1)}, f32[128]{0:T(128)}, u32[]{:S(2)}) copy-start(f32[128]{0:T(128)} %add_rsqrt_fusion.1) | copy-start | bytes 1540
  356.2 20.1 %copy-start.44 = (f32[1,768]{1,0:T(1,128)S(1)}, f32[1,768]{1,0:T(1,128)}, u32[]{:S(2)}) copy-start(f32[1,768]{1,0:T(1,128)} %stack.110) | copy-start | bytes 9220
  (57 other events, 161.0 us)
Sparse Core Ops, SparseCore 0:
  92.9 37.8 all-gather.3
  194.1 26.1 reduce-scatter.6
  223.0 28.1 reduce-scatter.4
  281.9 60.2 reduce-scatter.8
  346.2 28.1 reduce-scatter.10

commit v2 on v0

--- a/solution.py
+++ b/solution.py
@@ -1,8 +1,12 @@
+import functools
 import math
+import types
 
 import jax
 import jax.numpy as jnp
 from jax import lax
+from jax.experimental import pallas as pl
+from jax.experimental.pallas import tpu as pltpu
 from jax.sharding import PartitionSpec as P
 
 HEADS = 12
@@ -305,6 +309,793 @@
     )
 
 
+MESH = pl.DeviceIdType.MESH
+BF = jnp.bfloat16
+F32 = jnp.float32
+VSPEC = pl.BlockSpec(memory_space=pltpu.VMEM)
+GELU_IN = math.sqrt(2.0 / math.pi)
+
+
+class Net:
+    def __init__(self, send_sem, recv_sem, nz):
+        self.send_sem, self.recv_sem = send_sem, recv_sem
+        self.count = 0
+        self.sent = []
+        self.nz = nz
+        self.x = lax.axis_index("dp")
+        self.z = lax.axis_index("blk")
+        self.u = lax.axis_index("uly")
+
+    def send(self, src, dst, dev):
+        k = self.count
+        self.count += 1
+        copy = pltpu.make_async_remote_copy(
+            src_ref=src,
+            dst_ref=dst,
+            send_sem=self.send_sem.at[k],
+            recv_sem=self.recv_sem.at[k],
+            device_id=dev,
+            device_id_type=MESH,
+        )
+        copy.start()
+        self.sent.append(copy)
+        return copy
+
+    def plane(self, m):
+        return (self.x, self.z, self.u ^ m)
+
+    def other_x(self):
+        return (1 - self.x, self.z, self.u)
+
+    def zplus(self, d):
+        return lax.rem(self.z + d, self.nz)
+
+    def line(self, d):
+        return (self.x, self.zplus(d), self.u)
+
+    def enter(self):
+        barrier = pltpu.get_barrier_semaphore()
+        near = [self.plane(m) for m in (1, 2, 3)] + [self.other_x()]
+        near += [self.line(d) for d in range(1, self.nz)]
+        near += [(1 - self.x, self.z, self.u ^ m) for m in (1, 2, 3)]
+        for dev in near:
+            pl.semaphore_signal(barrier, inc=1, device_id=dev, device_id_type=MESH)
+        pl.semaphore_wait(barrier, len(near))
+
+    def finish(self):
+        for copy in self.sent:
+            copy.wait_send()
+
+
+def rows_at(start, count):
+    return pl.ds(pl.multiple_of(start, 16), count)
+
+
+def dot_nn(a, b):
+    return jnp.dot(a, b, preferred_element_type=F32)
+
+
+def dot_nt(a, b):
+    return lax.dot_general(a, b, (((1,), (1,)), ((), ())), preferred_element_type=F32)
+
+
+def dot_tn(a, b):
+    return lax.dot_general(a, b, (((0,), (0,)), ((), ())), preferred_element_type=F32)
+
+
+def loop(count, body):
+    def step(i, carry):
+        body(i)
+        return carry
+
+    lax.fori_loop(0, count, step, 0)
+
+
+def block_kernel(nz, refs):
+    r = refs
+    net = Net(r.send_sem, r.recv_sem, nz)
+    x, z, u = net.x, net.z, net.u
+    y, c = u // 2, lax.rem(u, 2)
+    own48 = (4 * z + u) * 48
+    tile = lambda t: rows_at(128 * t, 128)
+    half_cols = lambda which: pl.ds(pl.multiple_of(384 * which, 128), 384)
+    lane = lambda shape: lax.broadcasted_iota(jnp.int32, shape, 1)
+
+    local = [
+        pltpu.make_async_copy(r.qkv_pre.at[u], r.w_qkv.at[rows_at(own48, 48)], r.local_sem.at[0]),
+        pltpu.make_async_copy(r.fc_pre.at[u], r.w_fc.at[rows_at(own48, 48)], r.local_sem.at[1]),
+        pltpu.make_async_copy(r.proj_s, r.w_proj.at[rows_at(192 * z, 192)], r.local_sem.at[2]),
+        pltpu.make_async_copy(r.out_s, r.w_out.at[rows_at(own48, 48)], r.local_sem.at[3]),
+        pltpu.make_async_copy(r.x_own, r.x_all.at[tile(u)], r.local_sem.at[4]),
+        pltpu.make_async_copy(r.cot_own, r.cot_all.at[tile(u)], r.local_sem.at[5]),
+    ]
+    for copy in local:
+        copy.start()
+    net.enter()
+
+    def plane_gather_start(own, full):
+        return [net.send(own, full.at[tile(u)], net.plane(m)) for m in (2, 1)]
+
+    def plane_gather_forward(sent, full):
+        sent[0].wait_recv()
+        sent.append(net.send(full.at[tile(u ^ 2)], full.at[tile(u ^ 2)], net.plane(1)))
+
+    in_plane = lambda pre, full: [
+        net.send(pre.at[u ^ m], full.at[rows_at(own48, 48)], net.plane(m)) for m in (1, 2, 3)
+    ]
+    qkv_p = in_plane(r.qkv_pre, r.w_qkv)
+    x_g = plane_gather_start(r.x_own, r.x_all)
+    vec_z = [net.send(r.vec_pre, r.vec_land_z.at[d - 1], net.line(d)) for d in range(1, nz)]
+
+    def along_z(full):
+        mine = rows_at(192 * z + 96 * x, 96)
+        return [net.send(full.at[mine], full.at[mine], net.line(d)) for d in range(1, nz)]
+
+    def across_x(full, arrivals):
+        sent = []
+        for d, copy in enumerate(arrivals, 1):
+            copy.wait_recv()
+            part = rows_at(192 * net.zplus(nz - d) + 96 * x, 96)
+            sent.append(net.send(full.at[part], full.at[part], net.other_x()))
+        return sent
+
+    local[0].wait()
+    for copy in qkv_p:
+        copy.wait_recv()
+    qkv_z = along_z(r.w_qkv)
+    total = r.vec_pre[...]
+    for d in range(nz - 1):
+        vec_z[d].wait_recv()
+        total = total + r.vec_land_z[d]
+    r.vec_u[...] = total
+    vec_p = [net.send(r.vec_u, r.vec_land_p.at[m - 1], net.plane(m)) for m in (1, 2, 3)]
+    plane_gather_forward(x_g, r.x_all)
+    fc_p = in_plane(r.fc_pre, r.w_fc)
+    proj_mine = rows_at(192 * z + 96 * x, 96)
+    total = r.vec_u[...].astype(F32)
+    row = lax.broadcasted_iota(jnp.int32, total.shape, 0)
+    for m in range(3):
+        vec_p[m].wait_recv()
+        total = total + jnp.where(row == 8, 0.0, r.vec_land_p[m].astype(F32))
+    r.vec[...] = total
+    for copy in local[1:]:
+        copy.wait()
+    for copy in x_g[1:]:
+        copy.wait_recv()
+    gain = lambda i: r.vec[pl.ds(i, 1), :]
+
+    def normalize(values):
+        center = values - jnp.mean(values, -1, keepdims=True)
+        inverse = lax.rsqrt(jnp.mean(center * center, -1, keepdims=True) + 1e-05)
+        return center * inverse, inverse
+
+    def ln_tile(t):
+        normed, _ = normalize(r.x_all[tile(t), :].astype(F32))
+        r.ln_all[tile(t), :] = (normed * gain(0) + gain(2)).astype(BF)
+
+    loop(4, ln_tile)
+    proj_z = [
+        net.send(r.proj_s.at[rows_at(96 * x, 96)], r.w_proj.at[proj_mine], net.line(d))
+        for d in range(1, nz)
+    ]
+    qkv_x = across_x(r.w_qkv, qkv_z)
+    out_z = [
+        net.send(r.out_s.at[:, half_cols(x)], r.w_out.at[rows_at(own48, 48), half_cols(x)], net.line(d))
+        for d in range(1, nz)
+    ]
+    cot_g = plane_gather_start(r.cot_own, r.cot_all)
+    r.qm[2] = jnp.zeros((512, 128), BF)
+    for copy in qkv_x:
+        copy.wait_recv()
+
+    bias_u = jnp.sum(jnp.where(row == 9 + u, r.vec[...], 0.0), 0, keepdims=True)[:, 0:576]
+
+    def qkv_tile(t):
+        res = dot_nn(r.ln_all[tile(t), :], r.w_qkv[...]) + bias_u
+        res = res.astype(BF)
+        q01 = res[:, 0:128].astype(F32) * 0.125
+        low = lane(q01.shape) < 64
+        r.qm[0, tile(t), :] = jnp.where(low, q01, 0.0).astype(BF)
+        r.qm[1, tile(t), :] = jnp.where(low, 0.0, q01).astype(BF)
+        r.qm[2, tile(t), 0:64] = (res[:, 512:576].astype(F32) * 0.125).astype(BF)
+        r.kv_all[z, tile(t), :] = res[:, 128:512]
+
+    loop(4, qkv_tile)
+
+    def kv_copy(way, step):
+        block = z - step if way == 0 else z + step
+        target = z + 1 if way == 0 else z - 1
+        block, target = jnp.clip(block, 0, nz - 1), jnp.clip(target, 0, nz - 1)
+        return pltpu.make_async_remote_copy(
+            src_ref=r.kv_all.at[block], dst_ref=r.kv_all.at[block],
+            send_sem=r.kv_send.at[way * nz + step], recv_sem=r.kv_recv.at[way * nz + step],
+            device_id=(x, target, u), device_id_type=MESH)
+
+    def kv_sends(way, step):
+        if way == 0:
+            return jnp.logical_and(z - step >= 0, z + 1 < nz)
+        return jnp.logical_and(z + step < nz, z >= 1)
+
+    def kv_start(step):
+        for way in range(2):
+            @pl.when(kv_sends(way, step))
+            def _():
+                kv_copy(way, step).start()
+
+    def attend(j):
+        qp = r.pos_row[:, pl.ds(pl.multiple_of(512 * z, 128), 512)]
+        for h in range(3):
+            kc = 0 if h < 2 else 256
+            vc = 128 if h < 2 else 256
+            q = r.qm[h]
+
+            def score(kt, top):
+                s = dot_nt(r.kv_all[j, rows_at(128 * kt, 128), kc:kc + 128], q)
+                kp = r.pos_col[pl.ds(pl.multiple_of(512 * j + 128 * kt, 128), 128), :]
+                s = jnp.where(kp <= qp, s, -1e30)
+                r.s_buf[rows_at(128 * kt, 128), :] = s
+                return jnp.maximum(top, jnp.max(s, 0, keepdims=True))
+
+            old = r.m_run[h]
+            top = lax.fori_loop(0, 4, score, old)
+            shrink = jnp.exp(old - top)
+
+            def weigh(kt, got):
+                p = jnp.exp(r.s_buf[rows_at(128 * kt, 128), :] - top)
+                r.pt[j * 3 + h, rows_at(128 * kt, 128), :] = p.astype(BF)
+                return got + jnp.sum(p, 0, keepdims=True)
+
+            got = lax.fori_loop(0, 4, weigh, jnp.zeros((1, 512), F32))
+            r.m_run[h] = top
+            r.m_at[j * 3 + h] = top
+            r.l_run[h] = r.l_run[h] * shrink + got
+            r.o_t[h] = r.o_t[h] * shrink + dot_tn(r.kv_all[j, :, vc:vc + 128], r.pt[j * 3 + h])
+
+    r.m_run[...] = jnp.full((3, 1, 512), -1e30, F32)
+    r.l_run[...] = jnp.zeros((3, 1, 512), F32)
+    r.o_t[...] = jnp.zeros((3, 128, 512), F32)
+    kv_start(0)
+    for copy in fc_p:
+        copy.wait_recv()
+    fc_z = along_z(r.w_fc)
+    plane_gather_forward(cot_g, r.cot_all)
+    attend(z)
+
+    weights = {}
+    for step in range(1, nz):
+        for way in range(2):
+            @pl.when(z - step >= 0 if way == 0 else z + step < nz)
+            def _():
+                kv_copy(way, step - 1).wait_recv()
+
+        if step < nz - 1:
+            kv_start(step)
+        if step == 1:
+            weights["proj"] = across_x(r.w_proj, proj_z)
+            out_x = []
+            for d, copy in enumerate(out_z, 1):
+                copy.wait_recv()
+                part = r.w_out.at[rows_at((4 * net.zplus(nz - d) + u) * 48, 48), half_cols(x)]
+                out_x.append(net.send(part, part, net.other_x()))
+        if step == 2:
+            out_rows = lambda zz, who: r.w_out.at[rows_at((4 * zz + who) * 48, 48)]
+            for copy in out_x:
+                copy.wait_recv()
+            out_y = [net.send(out_rows(zz, u), out_rows(zz, u), net.plane(2)) for zz in range(nz)]
+            out_c = [net.send(out_rows(zz, u), out_rows(zz, u), net.plane(1)) for zz in range(nz)]
+
+        def either(way):
+            j = jnp.where(way == 0, z - step, z + step)
+
+            @pl.when(jnp.logical_and(j >= 0, j < nz))
+            def _():
+                attend(j)
+
+        loop(2, either)
+        if step == nz - 1:
+            for zz, copy in enumerate(out_y):
+                copy.wait_recv()
+                out_c.append(net.send(out_rows(zz, u ^ 2), out_rows(zz, u ^ 2), net.plane(1)))
+    weights["fc"] = across_x(r.w_fc, fc_z)
+
+    rowi = lax.broadcasted_iota(jnp.int32, (128, 512), 0)
+    r.l_inv[...] = 1.0 / r.l_run[...]
+    r.att_t[0] = jnp.where(rowi < 64, r.o_t[0] * r.l_inv[0], r.o_t[1] * r.l_inv[1])
+    r.att_t[1] = jnp.where(rowi < 64, 0.0, r.o_t[2] * r.l_inv[2])
+    r.att[:, 0:128] = jnp.transpose(r.att_t[0]).astype(BF)
+    r.att[:, 128:256] = jnp.transpose(r.att_t[1]).astype(BF)
+    att_p = [net.send(r.att.at[tile(u ^ m)], r.merged.at[u], net.plane(m)) for m in (2, 3, 1)]
+    r.merged[u] = r.att[tile(u), :]
+
+    for copy in out_c:
+        copy.wait_recv()
+    for g in range(4):
+        r.w_outp[256 * g:256 * g + 128, :] = r.w_out[192 * g:192 * g + 128, :]
+        r.w_outp[256 * g + 128:256 * g + 192, :] = jnp.zeros((64, 768), BF)
+        r.w_outp[256 * g + 192:256 * g + 256, :] = r.w_out[192 * g + 128:192 * g + 192, :]
+    for copy in cot_g[1:]:
+        copy.wait_recv()
+    for copy in weights["proj"]:
+        copy.wait_recv()
+
+    def gact_tile(t):
+        r.gact[tile(t), :] = dot_nt(r.cot_all[tile(t), :], r.w_proj[...])
+
+    loop(4, gact_tile)
+    for copy in att_p:
+        copy.wait_recv()
+    resid = r.x_own[...].astype(F32) + gain(4)
+    for g in range(4):
+        resid = resid + dot_nn(r.merged[g], r.w_outp[256 * g:256 * g + 256, :])
+    r.resid[...] = resid
+    normed, inverse = normalize(resid)
+    r.normed_mid[...] = normed
+    r.inverse_mid[...] = inverse
+    r.lm_all[tile(u), :] = (normed * gain(1) + gain(6)).astype(BF)
+    lm_own = r.lm_all.at[tile(u)]
+    lm_g = [net.send(lm_own, lm_own, net.plane(m)) for m in (2, 1)]
+    for copy in weights["fc"]:
+        copy.wait_recv()
+
+    r.vec_g[...] = jnp.zeros((16, 768), F32)
+
+    def mlp_tile(t, part):
+        rows = tile(t)
+        pre = dot_nn(r.lm_all[rows, :], r.w_fc[...]) + gain(8)
+        square = pre * pre
+        th = jnp.tanh(GELU_IN * (pre * (1.0 + 0.044715 * square)))
+        r.act[rows, :] = (0.5 * pre * (1.0 + th)).astype(BF)
+        slope = 0.5 * (1.0 + th) + (0.5 * GELU_IN) * pre * (1.0 - th * th) * (1.0 + 0.134145 * square)
+        gp = (slope * r.gact[rows, :]).astype(BF)
+        r.grad_pre[rows, :] = gp
+        r.fcb[...] += jnp.sum(gp.astype(F32), 0, keepdims=True)
+        part[t] = dot_nt(gp, r.w_fc[...]).astype(BF)
+
+    r.fcb[...] = jnp.zeros((1, 768), F32)
+    mlp_tile(u, r.gm_part)
+    lm_g[1].wait_recv()
+    mlp_tile(u ^ 1, r.gm_part)
+    plane_gather_forward(lm_g, r.lm_all)
+
+    def reduce_core(i, t, part, land_c):
+        return net.send(part.at[t], land_c.at[i], net.plane(1))
+
+    def reduce_y(copy, part, land_c, mid, land_y):
+        copy.wait_recv()
+        mid[...] = (part[u ^ 2].astype(F32) + land_c[0].astype(F32)).astype(BF)
+        return net.send(mid, land_y, net.plane(2))
+
+    def reduce_end(copy_c, copy_y, part, land_c, land_y):
+        copy_c.wait_recv()
+        copy_y.wait_recv()
+        return part[u].astype(F32) + land_c[1].astype(F32) + land_y[...].astype(F32)
+
+    gm_c1 = reduce_core(1, u ^ 1, r.gm_part, r.gm_c)
+    mlp_tile(u ^ 2, r.gm_part)
+    lm_g[2].wait_recv()
+    mlp_tile(u ^ 3, r.gm_part)
+    gm_c0 = reduce_core(0, u ^ 3, r.gm_part, r.gm_c)
+    r.vec_g[...] += jnp.where(row == 10 + u, r.fcb[...], 0.0)
+
+    def branch_tile(t):
+        r.br_part[t] = dot_nn(r.act[tile(t), :], r.w_proj[...]).astype(BF)
+
+    branch_tile(u ^ 3)
+    branch_tile(u ^ 1)
+    gm_y = reduce_y(gm_c0, r.gm_part, r.gm_c, r.gm_mid, r.gm_y)
+    br_c = [reduce_core(0, u ^ 3, r.br_part, r.br_c), reduce_core(1, u ^ 1, r.br_part, r.br_c)]
+    branch_tile(u ^ 2)
+    branch_tile(u)
+
+    def weight_grad(a, b, out, tiles):
+        def one(i):
+            cols = pl.ds(pl.multiple_of(128 * i, 128), 128)
+            out[tile(i), :] = dot_tn(a[:, cols], b[...]).astype(BF)
+
+        loop(tiles, one)
+
+    def start_x(grad, land):
+        return [
+            net.send(grad.at[rows_at(192 * zz + 96 * (1 - x), 96)], land.at[zz], net.other_x())
+            for zz in range(nz)
+        ]
+
+    def start_z(copies, grad, land, mine, land_z):
+        for zz in range(nz):
+            copies[zz].wait_recv()
+            mine[zz] = (grad[rows_at(192 * zz + 96 * x, 96), :].astype(F32) + land[zz].astype(F32)).astype(BF)
+        return [
+            net.send(mine.at[net.zplus(d)], land_z.at[d - 1], net.line(d)) for d in range(1, nz)
+        ]
+
+    def end_z(copies, mine, land_z, final):
+        total = mine[z].astype(F32)
+        for d in range(nz - 1):
+            copies[d].wait_recv()
+            total = total + land_z[d].astype(F32)
+        final[...] = total.astype(BF)
+
+    weight_grad(r.act, r.cot_all, r.proj_g, 6)
+    proj_a = start_x(r.proj_g, r.proj_x)
+
+    gm = reduce_end(gm_c1, gm_y, r.gm_part, r.gm_c, r.gm_y)
+    normed = r.normed_mid[...]
+    r.vec_g[1:2, :] = jnp.sum(gm * normed, 0, keepdims=True)
+    r.vec_g[5:6, :] = jnp.sum(gm, 0, keepdims=True)
+
+    def norm_grad(grad, normed, inverse, g):
+        e = grad * g
+        return inverse * (
+            e - jnp.mean(e, -1, keepdims=True) - normed * jnp.mean(e * normed, -1, keepdims=True)
+        )
+
+    cot = r.cot_own[...].astype(F32)
+    r.vec_g[4:5, :] = jnp.sum(cot, 0, keepdims=True)
+    grad_resid = cot + norm_grad(gm, normed, r.inverse_mid[...], gain(1))
+    r.grad_resid[...] = grad_resid
+    gb = grad_resid.astype(BF)
+    r.gb[...] = gb
+    r.vec_g[3:4, :] = jnp.sum(gb.astype(F32), 0, keepdims=True)
+
+    def gmer_tile(g):
+        r.gmer[g] = dot_nt(r.gb[...], r.w_outp[pl.ds(pl.multiple_of(256 * g, 256), 256), :]).astype(BF)
+
+    loop(4, gmer_tile)
+    ga_p = [net.send(r.gmer.at[u ^ m], r.ga.at[tile(u)], net.plane(m)) for m in (2, 3, 1)]
+    r.ga[tile(u), :] = r.gmer[u]
+    br_y = reduce_y(br_c[0], r.br_part, r.br_c, r.br_mid, r.br_y)
+    weight_grad(r.lm_all, r.grad_pre, r.fc_g, 6)
+    fc_a = start_x(r.fc_g, r.fc_x)
+    for g in range(4):
+        res = dot_tn(r.merged[g], r.gb[...]).astype(BF)
+        at = slice(48 * g, 48 * g + 48)
+        r.out_g[0, 0, at, :] = res[0:48]
+        r.out_g[1, 0, at, :] = res[48:96]
+        r.out_g[0, 1, 48 * g:48 * g + 32, :] = res[96:128]
+        r.out_g[0, 1, 48 * g + 32:48 * g + 48, :] = res[192:208]
+        r.out_g[1, 1, at, :] = res[208:256]
+    og_c = net.send(r.out_g.at[1 - c], r.og_c, net.plane(1))
+    r.output[...] = (
+        r.resid[...] + gain(5) + reduce_end(br_c[1], br_y, r.br_part, r.br_c, r.br_y)
+    ).astype(BF)
+    for copy in ga_p:
+        copy.wait_recv()
+
+    low = lane((512, 128)) < 64
+    ga01 = r.ga[:, 0:128]
+    zero = jnp.zeros((512, 128), BF)
+    r.gam[0] = jnp.where(low, ga01.astype(F32), 0.0).astype(BF)
+    r.gam[1] = jnp.where(low, 0.0, ga01.astype(F32)).astype(BF)
+    r.gam[2] = r.ga[:, 128:256]
+    prod = jnp.transpose(ga01.astype(F32)) * r.att_t[0]
+    r.delta[0] = jnp.sum(prod[0:64], 0, keepdims=True)
+    r.delta[1] = jnp.sum(prod[64:128], 0, keepdims=True)
+    prod = jnp.transpose(r.ga[:, 128:256].astype(F32)) * r.att_t[1]
+    r.delta[2] = jnp.sum(prod, 0, keepdims=True)
+    r.dq_t[...] = jnp.zeros((3, 128, 512), F32)
+
+    def back(j):
+        factor = [jnp.exp(r.m_at[j * 3 + h] - r.m_run[h]) * r.l_inv[h] for h in range(3)]
+
+        def keys(kt):
+            rows = rows_at(128 * kt, 128)
+            for h in range(3):
+                vc = 128 if h < 2 else 256
+                p = r.pt[j * 3 + h, rows, :].astype(F32) * factor[h]
+                dp = dot_nt(r.kv_all[j, rows, vc:vc + 128], r.gam[h])
+                r.ds[h, rows, :] = (p * (dp - r.delta[h])).astype(BF)
+                r.pt[j * 3 + h, rows, :] = p.astype(BF)
+
+        def sums(kt):
+            rows = rows_at(128 * kt, 128)
+            pair = lambda of, first, second: dot_nn(of(0), first) + dot_nn(of(1), second)
+            ds = lambda h: r.ds[h, rows, :]
+            p = lambda h: r.pt[j * 3 + h, rows, :]
+            r.dkv[rows, 0:128] = pair(ds, r.qm[0], r.qm[1])
+            r.dkv[rows, 128:256] = pair(p, r.gam[0], r.gam[1])
+            r.dkv[rows, 256:384] = dot_nn(ds(2), r.qm[2]) + dot_nn(p(2), r.gam[2])
+
+        loop(4, keys)
+        loop(4, sums)
+        for h in range(3):
+            kc = 0 if h < 2 else 256
+            r.dq_t[h] += dot_tn(r.kv_all[j, :, kc:kc + 128], r.ds[h])
+
+    def chain_copy(way, step):
+        target = jnp.clip(jnp.where(way == 0, z - 1, z + 1), 0, nz - 1)
+        at = way * (nz - 1) + step - 1
+        return pltpu.make_async_remote_copy(
+            src_ref=r.chain.at[at], dst_ref=r.chain_land.at[at],
+            send_sem=r.ch_send.at[at], recv_sem=r.ch_recv.at[at],
+            device_id=(x, target, u), device_id_type=MESH)
+
+    def chain_step(step):
+        def either(way):
+            j = jnp.where(way == 0, z - step, z + step)
+            behind = jnp.where(way == 0, z + 1, z - 1)
+
+            @pl.when(jnp.logical_and(j >= 0, j < nz))
+            def _():
+                back(j)
+                at = way * (nz - 1) + step - 1
+                comes = jnp.logical_and(behind >= 0, behind < nz)
+                if step < nz - 1:
+                    @pl.when(comes)
+                    def _():
+                        chain_copy(way, step + 1).wait_recv()
+                        r.chain[at] = (r.dkv[...] + r.chain_land[at + 1].astype(F32)).astype(BF)
+
+                    @pl.when(jnp.logical_not(comes))
+                    def _():
+                        r.chain[at] = r.dkv[...].astype(BF)
+                else:
+                    r.chain[at] = r.dkv[...].astype(BF)
+                chain_copy(way, step).start()
+
+        loop(2, either)
+
+    for step in range(nz - 1, 0, -1):
+        chain_step(step)
+        if step == nz - 1:
+            proj_b = start_z(proj_a, r.proj_g, r.proj_x, r.proj_m, r.proj_z)
+            og_c.wait_recv()
+            r.og_1[...] = (r.out_g[c].astype(F32) + r.og_c[...].astype(F32)).astype(BF)
+            og_y = net.send(r.og_1.at[1 - y], r.og_y, net.plane(2))
+        if step == nz - 2:
+            fc_b = start_z(fc_a, r.fc_g, r.fc_x, r.fc_m, r.fc_z)
+            og_y.wait_recv()
+            r.og_2[...] = (r.og_1[y].astype(F32) + r.og_y[...].astype(F32)).astype(BF)
+            og_x = net.send(r.og_2.at[:, half_cols(1 - x)], r.og_x, net.other_x())
+        if step == 1:
+            og_x.wait_recv()
+            r.og_3[...] = (r.og_2[:, half_cols(x)].astype(F32) + r.og_x[...].astype(F32)).astype(BF)
+            og_z = [
+                net.send(r.og_3.at[rows_at(48 * net.zplus(d), 48)], r.og_z.at[d - 1], net.line(d))
+                for d in range(1, nz)
+            ]
+    back(z)
+
+    @pl.when(z + 1 < nz)
+    def _():
+        chain_copy(0, 1).wait_recv()
+        r.dkv[...] += r.chain_land[0].astype(F32)
+
+    @pl.when(z >= 1)
+    def _():
+        chain_copy(1, 1).wait_recv()
+        r.dkv[...] += r.chain_land[nz - 1].astype(F32)
+
+    r.gqkv[:, 128:512] = r.dkv[...].astype(BF)
+    dq = jnp.transpose(jnp.where(rowi < 64, r.dq_t[0], r.dq_t[1]) * 0.125)
+    r.gqkv[:, 0:128] = dq.astype(BF)
+    r.gqkv[:, 512:576] = jnp.transpose(r.dq_t[2] * 0.125)[:, 0:64].astype(BF)
+
+    weight_grad(r.ln_all, r.gqkv, r.qkv_g, 6)
+    qkv_a = start_x(r.qkv_g, r.qkv_x)
+
+    def gin_tile(t):
+        r.gi_part[t] = dot_nt(r.gqkv[tile(t), :], r.w_qkv[...]).astype(BF)
+
+    gin_tile(u ^ 3)
+    gi_c0 = reduce_core(0, u ^ 3, r.gi_part, r.gi_c)
+    gin_tile(u ^ 1)
+    gi_c1 = reduce_core(1, u ^ 1, r.gi_part, r.gi_c)
+    gin_tile(u ^ 2)
+    gi_y = reduce_y(gi_c0, r.gi_part, r.gi_c, r.gi_mid, r.gi_y)
+    gin_tile(u)
+    r.vec_g[:, 0:576] += jnp.where(row[:, 0:576] == 6 + u, jnp.sum(r.gqkv[...].astype(F32), 0, keepdims=True), 0.0)
+    qkv_b = start_z(qkv_a, r.qkv_g, r.qkv_x, r.qkv_m, r.qkv_z)
+    end_z(proj_b, r.proj_m, r.proj_z, r.proj_f)
+    mine = rows_at(96 * x, 96)
+    r.proj_o[mine, :] = r.proj_f[...]
+    proj_c = net.send(r.proj_f, r.proj_o.at[mine], net.other_x())
+
+    finals = []
+
+    def hand_out(base, final, native):
+        for xx in range(2):
+            for cc in range(2):
+                target_x = x ^ xx
+                target_u = 2 * x + cc
+                here = jnp.logical_and(xx == 0, target_u == u)
+                k = base + 2 * xx + cc
+                copy = pltpu.make_async_remote_copy(
+                    src_ref=final.at[pl.ds(48 * cc, 48)], dst_ref=native.at[u], send_sem=r.f_send.at[k],
+                    recv_sem=r.f_recv.at[base + u], device_id=(target_x, z, target_u), device_id_type=MESH)
+
+                @pl.when(jnp.logical_not(here))
+                def _():
+                    copy.start()
+
+                @pl.when(here)
+                def _():
+                    native[u] = final[pl.ds(48 * cc, 48), :]
+
+                finals.append((here, copy))
+
+    def await_native(base, final, native):
+        for who in range(4):
+            copy = pltpu.make_async_remote_copy(
+                src_ref=final.at[pl.ds(0, 48)], dst_ref=native.at[who], send_sem=r.f_send.at[base],
+                recv_sem=r.f_recv.at[base + who], device_id=(1 - x, z, u), device_id_type=MESH)
+
+            @pl.when(jnp.logical_not(jnp.logical_and(x == y, u == who)))
+            def _():
+                copy.wait_recv()
+
+    gin = reduce_end(gi_c1, gi_y, r.gi_part, r.gi_c, r.gi_y)
+    normed, inverse = normalize(r.x_own[...].astype(F32))
+    r.vec_g[0:1, :] = jnp.sum(gin * normed, 0, keepdims=True)
+    r.vec_g[2:3, :] = jnp.sum(gin, 0, keepdims=True)
+    vec_m = [net.send(r.vec_g, r.vg_p.at[m - 1], net.plane(m)) for m in (1, 2, 3)]
+    r.input_grad[...] = (r.grad_resid[...] + norm_grad(gin, normed, inverse, gain(0))).astype(BF)
+    end_z(fc_b, r.fc_m, r.fc_z, r.fc_f)
+    hand_out(0, r.fc_f, r.fc_o)
+    total = r.vec_g[...]
+    for m in range(3):
+        vec_m[m].wait_recv()
+        total = total + r.vg_p[m]
+    r.vg_1[...] = total
+    vec_l = [net.send(r.vg_1, r.vg_z.at[d - 1], net.line(d)) for d in range(1, nz)]
+    total = r.og_3[rows_at(48 * z, 48), :].astype(F32)
+    for d in range(nz - 1):
+        og_z[d].wait_recv()
+        total = total + r.og_z[d].astype(F32)
+    r.out_o[:, half_cols(x)] = total.astype(BF)
+    og_last = net.send(r.out_o.at[:, half_cols(x)], r.out_o.at[:, half_cols(x)], net.other_x())
+    total = r.vg_1[...]
+    for d in range(nz - 1):
+        vec_l[d].wait_recv()
+        total = total + r.vg_z[d]
+    r.vg_2[...] = total
+    vec_last = net.send(r.vg_2, r.vg_x, net.other_x())
+    end_z(qkv_b, r.qkv_m, r.qkv_z, r.qkv_f)
+    hand_out(4, r.qkv_f, r.qkv_o)
+    vec_last.wait_recv()
+    r.vec_o[...] = r.vg_2[...] + r.vg_x[...]
+    proj_c.wait_recv()
+    og_last.wait_recv()
+    await_native(0, r.fc_f, r.fc_o)
+    await_native(4, r.qkv_f, r.qkv_o)
+
+    for here, copy in finals:
+        @pl.when(jnp.logical_not(here))
+        def _():
+            copy.wait_send()
+    for step in range(nz - 1):
+        for way in range(2):
+            @pl.when(kv_sends(way, step))
+            def _():
+                kv_copy(way, step).wait_send()
+    for step in range(1, nz):
+        for way in range(2):
+            @pl.when(z - step >= 0 if way == 0 else z + step < nz)
+            def _():
+                chain_copy(way, step).wait_send()
+    net.finish()
+
+
+def block_call(nz, **operands):
+    def vm(*shape, kind=BF):
+        return pltpu.VMEM(shape, kind)
+
+    outs = dict(
+        output=((128, 768), BF), input_grad=((128, 768), BF), qkv_o=((4, 48, 576), BF),
+        fc_o=((4, 48, 768), BF), proj_o=((192, 768), BF), out_o=((48, 768), BF), vec_o=((16, 768), F32),
+    )
+    f = lambda *shape: vm(*shape, kind=F32)
+    keys = 512 * nz
+    scratch = dict(
+        w_qkv=vm(768, 576), w_fc=vm(768, 768), w_proj=vm(768, 768), w_out=vm(768, 768), w_outp=vm(1024, 768),
+        vec_land_z=vm(nz - 1, 16, 768), vec_u=vm(16, 768), vec_land_p=vm(3, 16, 768), vec=f(16, 768),
+        x_all=vm(512, 768), cot_all=vm(512, 768), ln_all=vm(512, 768), lm_all=vm(512, 768),
+        qm=vm(3, 512, 128), kv_all=vm(nz, 512, 384), s_buf=f(512, 512), pt=vm(nz * 3, 512, 512),
+        m_run=f(3, 1, 512), l_run=f(3, 1, 512), l_inv=f(3, 1, 512), m_at=f(nz * 3, 1, 512), o_t=f(3, 128, 512),
+        att_t=f(2, 128, 512), att=vm(512, 256), merged=vm(4, 128, 256),
+        resid=f(128, 768), normed_mid=f(128, 768), inverse_mid=f(128, 1), gact=f(512, 768),
+        act=vm(512, 768), grad_pre=vm(512, 768), fcb=f(1, 768), vec_g=f(16, 768),
+        gm_part=vm(4, 128, 768), gm_c=vm(2, 128, 768), gm_mid=vm(128, 768), gm_y=vm(128, 768),
+        br_part=vm(4, 128, 768), br_c=vm(2, 128, 768), br_mid=vm(128, 768), br_y=vm(128, 768),
+        gi_part=vm(4, 128, 768), gi_c=vm(2, 128, 768), gi_mid=vm(128, 768), gi_y=vm(128, 768),
+        grad_resid=f(128, 768), gb=vm(128, 768), gmer=vm(4, 128, 256), ga=vm(512, 256), gam=vm(3, 512, 128),
+        delta=f(3, 1, 512), ds=vm(3, 512, 512), dq_t=f(3, 128, 512), dkv=f(512, 384),
+        chain=vm(2 * (nz - 1), 512, 384), chain_land=vm(2 * (nz - 1), 512, 384), gqkv=vm(512, 576),
+        qkv_g=vm(768, 576), fc_g=vm(768, 768), proj_g=vm(768, 768), out_g=vm(2, 2, 192, 768),
+        qkv_x=vm(nz, 96, 576), fc_x=vm(nz, 96, 768), proj_x=vm(nz, 96, 768),
+        qkv_m=vm(nz, 96, 576), fc_m=vm(nz, 96, 768), proj_m=vm(nz, 96, 768),
+        qkv_z=vm(nz - 1, 96, 576), fc_z=vm(nz - 1, 96, 768), proj_z=vm(nz - 1, 96, 768),
+        qkv_f=vm(96, 576), fc_f=vm(96, 768), proj_f=vm(96, 768),
+        og_c=vm(2, 192, 768), og_1=vm(2, 192, 768), og_y=vm(192, 768), og_2=vm(192, 768),
+        og_x=vm(192, 384), og_3=vm(192, 384), og_z=vm(nz - 1, 48, 384),
+        vg_p=f(3, 16, 768), vg_1=f(16, 768), vg_z=f(nz - 1, 16, 768), vg_2=f(16, 768), vg_x=f(16, 768),
+        send_sem=pltpu.SemaphoreType.DMA((112,)), recv_sem=pltpu.SemaphoreType.DMA((112,)),
+        local_sem=pltpu.SemaphoreType.DMA((6,)),
+        kv_send=pltpu.SemaphoreType.DMA((2 * nz,)), kv_recv=pltpu.SemaphoreType.DMA((2 * nz,)),
+        ch_send=pltpu.SemaphoreType.DMA((2 * nz,)), ch_recv=pltpu.SemaphoreType.DMA((2 * nz,)),
+        f_send=pltpu.SemaphoreType.DMA((8,)), f_recv=pltpu.SemaphoreType.DMA((8,)),
+    )
+    names = [*operands, *outs, *scratch]
+
+    def kernel(*refs):
+        block_kernel(nz, types.SimpleNamespace(**dict(zip(names, refs, strict=True))))
+
+    got = pl.pallas_call(
+        kernel,
+        out_shape=tuple(jax.ShapeDtypeStruct(*s) for s in outs.values()),
+        in_specs=[VSPEC] * len(operands),
+        out_specs=(VSPEC,) * len(outs),
+        scratch_shapes=list(scratch.values()),
+        compiler_params=pltpu.CompilerParams(
+            collective_id=0, has_side_effects=True, vmem_limit_bytes=60 * 2**20
+        ),
+        name="transformer_block",
+    )(*operands.values())
+    return dict(zip(outs, got, strict=True))
+
+
+def arrange_qkv(w):
+    rows = w.shape[0]
+    parts = w.reshape(rows, 3, 4, 3, 64)
+    order = ((0, 0), (0, 1), (1, 0), (1, 1), (2, 0), (2, 1), (1, 2), (2, 2), (0, 2))
+    return jnp.stack([parts[:, t, :, h] for t, h in order], 2).transpose(1, 0, 2, 3).reshape(4, rows, 576)
+
+
+def restore_qkv(g):
+    rows = g.shape[1]
+    parts = g.reshape(4, rows, 9, 64)
+    q = jnp.stack([parts[:, :, i] for i in (0, 1, 8)], 2)
+    k = jnp.stack([parts[:, :, i] for i in (2, 3, 6)], 2)
+    v = jnp.stack([parts[:, :, i] for i in (4, 5, 7)], 2)
+    return jnp.stack([q, k, v], 0).transpose(2, 0, 1, 3, 4).reshape(rows, 2304)
+
+
+def device_fast(nz, inputs, stretch_order, norm_gains, biases, mid_shift, value_bias, qkv_weight, out_weight, fc_weight, fc_bias, proj_weight, cotangent):
+    z, u = lax.axis_index("blk"), lax.axis_index("uly")
+    place = (4 * z + u) * 48
+    pack = jnp.concatenate([norm_gains, biases, mid_shift[None], value_bias[None]], 0)
+    vec8 = lax.dynamic_update_slice(jnp.zeros((8, 768), BF), pack, (0, place))
+    fcb = lax.dynamic_update_slice(jnp.zeros((1, 768), BF), fc_bias[None], (0, 192 * z))
+    wide = lax.dynamic_update_slice(jnp.zeros((2, 192), BF), jnp.stack([biases[1], value_bias]), (0, 48 * u))
+    zero = jnp.zeros((64,), BF)
+    q, v = wide[0].reshape(3, 64), wide[1].reshape(3, 64)
+    local = jnp.concatenate([q[0], q[1], zero, zero, v[0], v[1], zero, v[2], q[2], jnp.zeros((192,), BF)])[None]
+    four = lax.dynamic_update_slice(jnp.zeros((4, 768), BF), local, (z, 0))
+    vec_pre = jnp.concatenate([vec8, fcb, four, jnp.zeros((3, 768), BF)], 0)
+    pos = (stretch_order[0][:, None] * 64 + jnp.arange(64, dtype=jnp.int32)[None]).reshape(-1)
+    got = block_call(
+        nz,
+        x_own=inputs[0],
+        cot_own=cotangent[0],
+        qkv_pre=arrange_qkv(qkv_weight),
+        fc_pre=fc_weight.reshape(48, nz, 4, 192).transpose(2, 0, 1, 3).reshape(4, 48, 768),
+        out_s=out_weight,
+        proj_s=proj_weight,
+        vec_pre=vec_pre,
+        pos_row=pos[None],
+        pos_col=pos[:, None],
+    )
+    vec_o = got["vec_o"]
+    mine = lax.dynamic_slice(vec_o, (0, place), (6, 48))
+    qs = lax.dynamic_slice(vec_o, (6 + z, 0), (1, 576))[0].reshape(9, 64)
+    qb = lax.dynamic_slice(jnp.concatenate([qs[0], qs[1], qs[8]]), (48 * u,), (48,))
+    vb = lax.dynamic_slice(jnp.concatenate([qs[4], qs[5], qs[7]]), (48 * u,), (48,))
+    fb = lax.dynamic_slice(vec_o, (10 + u, 192 * z), (1, 192))[0]
+    fc_g = got["fc_o"].reshape(4, 48, nz, 192).transpose(1, 2, 0, 3).reshape(48, 3072)
+    return (
+        got["output"][None],
+        got["input_grad"][None],
+        mine[0:2],
+        jnp.stack([mine[2], qb, mine[3], mine[4]]),
+        mine[5],
+        vb,
+        restore_qkv(got["qkv_o"]).astype(F32),
+        got["out_o"].astype(F32),
+        fc_g.astype(F32),
+        fb,
+        got["proj_o"].astype(F32),
+    )
+
+
 def solution(mesh):
     placed = (
         P("dp", ("blk", "uly"), None),
@@ -320,8 +1111,12 @@
         P(("blk", "uly"), None),
         P("dp", ("blk", "uly"), None),
     )
+    sizes = dict(mesh.shape)
+    nz = sizes["blk"]
+    fast = sizes["uly"] == 4 and sizes["dp"] == 2 and 768 % (nz * 4 * 16) == 0
+    chosen = functools.partial(device_fast, nz) if fast else per_device
     return jax.shard_map(
-        per_device,
+        chosen,
         mesh=mesh,
         in_specs=placed,
         out_specs=(

time: 909 us -> 227 us (0.25)
  waiting for transfers between devices: 470 us -> 0 us
  blocking collectives: 228 us -> 0 us
  Pallas kernels: 0 us -> 198 us
  matrix products: 82.3 us -> 0 us
  other arithmetic: 45.6 us -> 5.62 us
  local copies, waits for them, and re-layouts: 47.5 us -> 22.5 us
  between operations: 17.7 us -> 0.94 us
  starting transfers between devices: 11.1 us -> 0 us
    reduce_scatter x4 -> x0, waiting for transfers between devices: 346 us -> none  [the longest x1 114 us: per_device(): lax.psum_scatter(fc_grad, ('blk', 'uly'), scatter_dimension=0, tiled=True)]
    pallas_call x0 -> x1, Pallas kernels: none -> 198 us  [block_call(): pl.pallas_call(kernel, out_shape=tuple((jax.ShapeDtypeStruct(*s) for s in...]
    unnamed x2 -> x0, blocking collectives: 118 us -> none
    all_gather x4 -> x0, blocking collectives: 87.4 us -> none  [the longest x1 25.9 us: per_device(): lax.all_gather(value_rows, 'blk', axis=1, tiled=True)]
    dot_general x26 -> x0, matrix products: 82.3 us -> none  [the longest x4 15.2 us: score_block(): jnp.einsum('sqhd,skhd->shqk', queries, key_part.reshape(seq_count, part_r...]
    unnamed x15 -> x0, waiting for transfers between devices: 72.2 us -> none
    psum x1 -> x0, waiting for transfers between devices: 30.5 us -> none  [per_device(): lax.psum(shard_grads[4].astype(jnp.bfloat16), 'dp').astype(jnp.float32)]
    all_to_all x3 -> x0, waiting for transfers between devices: 21.8 us -> none  [the longest x1 11.5 us: per_device(): lax.all_to_all(qkv.reshape(seq_count, row_len, 3, uly_count, head_span),...]
  transfers between devices with their start and end apart: 15 -> 0, of which waited for: 10 -> 0; matrix products, arithmetic and copies ran while one was open for 12% -> 0% of each run, Pallas kernels for 0% -> 0%
where the time goes in v2:
time: 227 us
  Pallas kernels  198 us (87%)
  local copies, waits for them, and re-layouts  22.5 us (10%)
  other arithmetic  5.62 us (2%)
    pallas_call x1, Pallas kernels, block_call(): pl.pallas_call(kernel, out_shape=tuple((jax.ShapeDtypeStruct(*s) for s in...  198 us

profile of v2, /device:TPU:0, one launch (start us, length us, event | category | flops | bytes accessed | tf_op | source)
XLA Modules:
  0.0 226.8 jit_solution(5591430146513463706)
XLA Ops:
  0.6 0.7 slice.133
  1.3 0.7 pad_maximum_fusion.4
  2.4 0.7 pad_maximum_fusion
  3.3 0.7 broadcast_in_dim.44
  4.2 0.7 maximum_maximum_fusion.refs_6_
  4.9 1.7 reshape.123
  6.6 0.7 fusion.2
  7.8 1.1 reshape.124.refs_2_
  8.9 2.0 add.74.refs_8_
  10.9 0.7 add.70.refs_7_
  12.3 1.1 reshape.126.refs_3_
  13.3 197.8 %transformer_block.1 = (bf16[128,768]{1,0:T(8,128)(2,1)}, bf16[128,768]{1,0:T(8,128)(2,1)}, bf16[4,48,576]{2,1,0:T(8,128)(2,1)}, bf16[4,48,768]{2,1,0:T(8,128)(2...) custom-call(bf16[128,768]{1,0:T(8,128)(2,1)} %bitcast.71, bf16[128,768]{1,0:T(8,128)(2,1)} %bitcast.72, ...), custom_call_target="tpu_custom_call" | custom-call | tf_op jit(solution)/shard_map/transformer_block/pallas_call | solution.py:1022
  211.1 1.3 reshape.127
  214.4 1.4 reshape.128
  217.0 1.6 reshape.129
  218.6 0.9 convert_element_type.35
  219.4 0.8 dynamic-slice_bitcast_fusion.2
  220.3 0.6 dynamic_slice.18
  221.0 0.8 constant_dynamic-slice_fusion
  222.8 0.6 pad_maximum_fusion.1
  223.4 0.7 convert_element_type.30
  224.1 1.3 dynamic_slice.19
  225.5 0.7 copy.74
  226.1 0.7 copy.75
  (56 shorter events, 6.1 us)
Async XLA Ops:
  7.5 1.3 copy-start.6
  7.8 3.9 %copy-start.1 = (bf16[48,3072]{1,0:T(8,128)(2,1)S(1)}, bf16[48,3072]{1,0:T(8,128)(2,1)}, u32[]{:S(2)}) copy-start(bf16[48,3072]{1,0:T(8,128)(2,1)} %param.20) | copy-start | bytes 884740
  214.4 1.4 copy-start.2
  216.5 2.1 copy-start
  217.0 6.5 %copy-start.5 = (bf16[48,768]{1,0:T(8,128)(2,1)S(1)}, bf16[48,768]{1,0:T(8,128)(2,1)}, u32[]{:S(2)}) copy-start(bf16[48,768]{1,0:T(8,128)(2,1)} %get-tuple-element.22) | copy-start | bytes 221188
  217.0 8.5 %copy-start.4 = (bf16[128,768]{1,0:T(8,128)(2,1)S(1)}, bf16[128,768]{1,0:T(8,128)(2,1)}, u32[]{:S(2)}) copy-start(bf16[128,768]{1,0:T(8,128)(2,1)} %get-tuple-element.18) | copy-start | bytes 589828
  217.0 9.1 %copy-start.3 = (bf16[128,768]{1,0:T(8,128)(2,1)S(1)}, bf16[128,768]{1,0:T(8,128)(2,1)}, u32[]{:S(2)}) copy-start(bf16[128,768]{1,0:T(8,128)(2,1)} %get-tuple-element.19) | copy-start | bytes 589828

commit v3 on v2

--- a/solution.py
+++ b/solution.py
@@ -353,18 +353,198 @@
     def line(self, d):
         return (self.x, self.zplus(d), self.u)
 
-    def enter(self):
+    def hail(self):
         barrier = pltpu.get_barrier_semaphore()
         near = [self.plane(m) for m in (1, 2, 3)] + [self.other_x()]
         near += [self.line(d) for d in range(1, self.nz)]
         near += [(1 - self.x, self.z, self.u ^ m) for m in (1, 2, 3)]
         for dev in near:
             pl.semaphore_signal(barrier, inc=1, device_id=dev, device_id_type=MESH)
-        pl.semaphore_wait(barrier, len(near))
+        self.met = len(near)
+
+    def meet(self):
+        pl.semaphore_wait(pltpu.get_barrier_semaphore(), self.met)
 
     def finish(self):
         for copy in self.sent:
             copy.wait_send()
+
+
+class Line:
+    def __init__(self, net, send_sem, recv_sem, base):
+        self.net, self.send_sem, self.recv_sem, self.base = net, send_sem, recv_sem, base
+        self.z = net.z
+        self.inner = jnp.logical_and(net.z >= 1, net.z <= net.nz - 2)
+        self.far = net.nz - 1 - net.z
+
+    def copy(self, src, dst, k, target, recv=None):
+        target = jnp.clip(target, 0, self.net.nz - 1)
+        return pltpu.make_async_remote_copy(
+            src_ref=src,
+            dst_ref=dst,
+            send_sem=self.send_sem.at[self.base + k],
+            recv_sem=self.recv_sem.at[self.base + (k if recv is None else recv)],
+            device_id=(self.net.x, target, self.net.u),
+            device_id_type=MESH,
+        )
+
+    def target(self, d):
+        return lax.rem(self.z + d, self.net.nz)
+
+    def source(self, d):
+        return lax.rem(self.z - d + self.net.nz, self.net.nz)
+
+
+class Spread(Line):
+    def __init__(self, net, send_sem, recv_sem, base, block):
+        super().__init__(net, send_sem, recv_sem, base)
+        self.block = block
+
+    def direct(self, d):
+        return self.copy(self.block(self.z), self.block(self.z), d, self.target(d))
+
+    def start(self):
+        for d in (2, 1, 3):
+            if d == 2:
+                self.direct(d).start()
+            else:
+                @pl.when(jnp.logical_or(self.inner, self.target(d) != self.far))
+                def _():
+                    self.direct(d).start()
+
+    def relay_copy(self):
+        block = self.block(self.source(2))
+        target = jnp.where(self.z == 2, 3, 0)
+        return self.copy(block, block, 4, target, jnp.where(self.z == 2, 3, 1))
+
+    def across(self, d):
+        block = self.block(self.source(d))
+        return pltpu.make_async_remote_copy(
+            src_ref=block, dst_ref=block, send_sem=self.send_sem.at[self.base + 4 + d],
+            recv_sem=self.recv_sem.at[self.base + 4 + d], device_id=self.net.other_x(), device_id_type=MESH)
+
+    def arrive(self, d):
+        block = self.block(self.source(d))
+        self.copy(block, block, d, self.z).wait_recv()
+
+    def relay(self):
+        self.arrive(2)
+
+        @pl.when(self.inner)
+        def _():
+            self.relay_copy().start()
+
+        self.across(2).start()
+
+    def rest(self):
+        first = jnp.where(self.z == 0, 3, 1)
+        for d in (first, 4 - first):
+            self.arrive(d)
+            self.across(d).start()
+
+    def finish_recv(self):
+        for d in (2, 1, 3):
+            self.across(d).wait_recv()
+
+    def finish(self):
+        self.direct(2).wait_send()
+        for d in (1, 3):
+            @pl.when(jnp.logical_or(self.inner, self.target(d) != self.far))
+            def _():
+                self.direct(d).wait_send()
+        for d in (1, 2, 3):
+            self.across(d).wait_send()
+
+        @pl.when(self.inner)
+        def _():
+            self.relay_copy().wait_send()
+
+
+class Collect(Line):
+    def __init__(self, net, send_sem, recv_sem, base, theirs, ours, land_x, mine, land_z, relay):
+        super().__init__(net, send_sem, recv_sem, base)
+        self.theirs, self.ours = theirs, ours
+        self.land_x, self.mine, self.land_z, self.relay = land_x, mine, land_z, relay
+
+    def order(self, i):
+        pick = lambda table: table[i]
+        z = self.z
+        return jnp.where(z == 0, 3 - i, jnp.where(z == 3, i, jnp.where(z == 1, pick((0, 2, 3, 1)), pick((3, 1, 0, 2)))))
+
+    def across(self, i):
+        zz = self.order(i)
+        return pltpu.make_async_remote_copy(
+            src_ref=self.theirs(zz), dst_ref=self.land_x.at[zz], send_sem=self.send_sem.at[self.base + 5 + i],
+            recv_sem=self.recv_sem.at[self.base + 5 + i], device_id=self.net.other_x(), device_id_type=MESH)
+
+    def start(self):
+        for i in range(4):
+            self.across(i).start()
+
+    def own(self, i):
+        zz = self.order(i)
+        self.across(i).wait_recv()
+        self.mine[zz] = (self.ours(zz) + self.land_x[zz].astype(F32)).astype(BF)
+
+    def direct(self, zz):
+        d = lax.rem(zz - self.z + 4, 4)
+        return self.copy(self.mine.at[zz], self.land_z.at[d - 1], d, zz)
+
+    def to_neighbour(self):
+        return self.copy(self.mine.at[self.far], self.relay, 4, jnp.where(self.z == 0, 1, 2))
+
+    def part(self, i):
+        self.own(i)
+        if i == 0:
+            @pl.when(self.inner)
+            def _():
+                self.direct(self.order(0)).start()
+
+            @pl.when(jnp.logical_not(self.inner))
+            def _():
+                self.to_neighbour().start()
+        elif i == 1:
+            self.direct(self.order(1)).start()
+        elif i == 2:
+            @pl.when(jnp.logical_not(self.inner))
+            def _():
+                self.direct(self.order(2)).start()
+
+    def first(self):
+        for i in range(4):
+            self.part(i)
+
+    def second(self):
+        @pl.when(self.inner)
+        def _():
+            zz = self.order(2)
+            self.copy(self.relay, self.relay, 4, self.z).wait_recv()
+            self.mine[zz] = (self.mine[zz].astype(F32) + self.relay[...].astype(F32)).astype(BF)
+            self.direct(zz).start()
+
+    def total(self, final):
+        skip = jnp.where(self.z == 0, 1, 3)
+        final[...] = self.mine[self.z].astype(F32)
+        for d in (1, 2, 3):
+            @pl.when(jnp.logical_or(self.inner, skip != d))
+            def _():
+                self.copy(self.land_z.at[d - 1], self.land_z.at[d - 1], d, self.z).wait_recv()
+                final[...] += self.land_z[d - 1].astype(F32)
+
+    def finish(self):
+        for i in range(4):
+            self.across(i).wait_send()
+
+        @pl.when(self.inner)
+        def _():
+            for i in range(3):
+                self.direct(self.order(i)).wait_send()
+
+        @pl.when(jnp.logical_not(self.inner))
+        def _():
+            self.to_neighbour().wait_send()
+            for i in (1, 2):
+                self.direct(self.order(i)).wait_send()
 
 
 def rows_at(start, count):
@@ -401,17 +581,49 @@
     half_cols = lambda which: pl.ds(pl.multiple_of(384 * which, 128), 384)
     lane = lambda shape: lax.broadcasted_iota(jnp.int32, shape, 1)
 
+    x_own, cot_own = r.x_all.at[tile(u)], r.cot_all.at[tile(u)]
     local = [
-        pltpu.make_async_copy(r.qkv_pre.at[u], r.w_qkv.at[rows_at(own48, 48)], r.local_sem.at[0]),
-        pltpu.make_async_copy(r.fc_pre.at[u], r.w_fc.at[rows_at(own48, 48)], r.local_sem.at[1]),
-        pltpu.make_async_copy(r.proj_s, r.w_proj.at[rows_at(192 * z, 192)], r.local_sem.at[2]),
-        pltpu.make_async_copy(r.out_s, r.w_out.at[rows_at(own48, 48)], r.local_sem.at[3]),
-        pltpu.make_async_copy(r.x_own, r.x_all.at[tile(u)], r.local_sem.at[4]),
-        pltpu.make_async_copy(r.cot_own, r.cot_all.at[tile(u)], r.local_sem.at[5]),
+        pltpu.make_async_copy(r.qkv_in, r.qkv_raw, r.local_sem.at[0]),
+        pltpu.make_async_copy(r.fc_in, r.fc_raw, r.local_sem.at[1]),
+        pltpu.make_async_copy(r.x_in, x_own, r.local_sem.at[2]),
+        pltpu.make_async_copy(r.out_in, r.w_out.at[rows_at(own48, 48)], r.local_sem.at[3]),
+        pltpu.make_async_copy(r.proj_in, r.w_proj.at[rows_at(192 * z, 192)], r.local_sem.at[4]),
+        pltpu.make_async_copy(r.cot_in, cot_own, r.local_sem.at[5]),
     ]
     for copy in local:
         copy.start()
-    net.enter()
+    net.hail()
+    local[0].wait()
+    for g in range(4):
+        for t in range(3):
+            r.qkv_pre[g, :, 128 * t:128 * t + 128] = r.qkv_raw[:, 768 * t + 192 * g:768 * t + 192 * g + 128]
+        for at, t in ((384, 1), (448, 2), (512, 0)):
+            r.qkv_pre[g, :, at:at + 64] = r.qkv_raw[:, 768 * t + 192 * g + 128:768 * t + 192 * g + 192]
+    r.w_qkv[rows_at(own48, 48), :] = r.qkv_pre[u]
+    vp = r.vec_f32
+    vp[...] = jnp.zeros((16, 768), F32)
+    vp[0:2, 0:48] = r.gains_in[...].astype(F32)
+    vp[2:6, 0:48] = r.biases_in[...].astype(F32)
+    vp[6:7, 0:48] = r.mid_in[...].astype(F32)
+    vp[7:8, 0:48] = r.vb_in[...].astype(F32)
+    bias = r.bias_f32
+    bias[...] = jnp.zeros((8, 256), F32)
+    bias[0:1, 0:48] = r.biases_in[1:2, :].astype(F32)
+    bias[1:2, 0:48] = r.vb_in[...].astype(F32)
+    bias[...] = pltpu.roll(bias[...], 48 * u, 1)
+    vp[0:8, :] = pltpu.roll(vp[0:8, :], 48 * (4 * z + u), 1)
+    vp[8:9, 0:192] = r.fcb_in[...].astype(F32)
+    vp[9:10, 0:128] = bias[0:1, 0:128]
+    vp[9:10, 256:384] = bias[1:2, 0:128]
+    vp[9:10, 448:512] = bias[1:2, 128:192]
+    vp[9:10, 512:576] = bias[0:1, 128:192]
+    high = vp[8:16, :]
+    row8 = lax.broadcasted_iota(jnp.int32, high.shape, 0)
+    fcb_row = pltpu.roll(jnp.where(row8 == 0, high, 0.0), 192 * z, 1)
+    bias_row = jnp.sum(jnp.where(row8 == 1, high, 0.0), 0, keepdims=True)
+    vp[8:16, :] = fcb_row + jnp.where(row8 == 1 + z, bias_row, 0.0)
+    r.vec_pre[...] = vp[...].astype(BF)
+    net.meet()
 
     def plane_gather_start(own, full):
         return [net.send(own, full.at[tile(u)], net.plane(m)) for m in (2, 1)]
@@ -423,26 +635,31 @@
     in_plane = lambda pre, full: [
         net.send(pre.at[u ^ m], full.at[rows_at(own48, 48)], net.plane(m)) for m in (1, 2, 3)
     ]
+    block96 = lambda full: lambda j: full.at[rows_at(192 * j + 96 * x, 96)]
+    spread = lambda base, block: Spread(net, r.sp_send, r.sp_recv, base, block)
+    qkv_s = spread(0, block96(r.w_qkv))
+    fc_s = spread(8, block96(r.w_fc))
+    proj_s = spread(16, block96(r.w_proj))
+    out_s = spread(24, lambda j: r.w_out.at[rows_at((4 * j + u) * 48, 48), half_cols(x)])
     qkv_p = in_plane(r.qkv_pre, r.w_qkv)
-    x_g = plane_gather_start(r.x_own, r.x_all)
     vec_z = [net.send(r.vec_pre, r.vec_land_z.at[d - 1], net.line(d)) for d in range(1, nz)]
-
-    def along_z(full):
-        mine = rows_at(192 * z + 96 * x, 96)
-        return [net.send(full.at[mine], full.at[mine], net.line(d)) for d in range(1, nz)]
-
-    def across_x(full, arrivals):
-        sent = []
-        for d, copy in enumerate(arrivals, 1):
-            copy.wait_recv()
-            part = rows_at(192 * net.zplus(nz - d) + 96 * x, 96)
-            sent.append(net.send(full.at[part], full.at[part], net.other_x()))
-        return sent
-
-    local[0].wait()
+    for copy in local[1:]:
+        copy.wait()
+    out_s.start()
+    for g in range(4):
+        for zz in range(nz):
+            r.fc_pre[g, :, 192 * zz:192 * zz + 192] = r.fc_raw[:, 768 * zz + 192 * g:768 * zz + 192 * g + 192]
+    r.w_fc[rows_at(own48, 48), :] = r.fc_pre[u]
+    inner64 = lax.broadcasted_iota(jnp.int32, (64, 1), 0)
+    inner64_row = lax.broadcasted_iota(jnp.int32, (1, 64), 1)
+    for i in range(8 * nz):
+        first = r.order_in[0, i] * 64
+        r.pos_col[64 * i:64 * i + 64, :] = first + inner64
+        r.pos_row[:, 64 * i:64 * i + 64] = first + inner64_row
     for copy in qkv_p:
         copy.wait_recv()
-    qkv_z = along_z(r.w_qkv)
+    qkv_s.start()
+    x_g = plane_gather_start(x_own, r.x_all)
     total = r.vec_pre[...]
     for d in range(nz - 1):
         vec_z[d].wait_recv()
@@ -451,15 +668,12 @@
     vec_p = [net.send(r.vec_u, r.vec_land_p.at[m - 1], net.plane(m)) for m in (1, 2, 3)]
     plane_gather_forward(x_g, r.x_all)
     fc_p = in_plane(r.fc_pre, r.w_fc)
-    proj_mine = rows_at(192 * z + 96 * x, 96)
     total = r.vec_u[...].astype(F32)
     row = lax.broadcasted_iota(jnp.int32, total.shape, 0)
     for m in range(3):
         vec_p[m].wait_recv()
         total = total + jnp.where(row == 8, 0.0, r.vec_land_p[m].astype(F32))
     r.vec[...] = total
-    for copy in local[1:]:
-        copy.wait()
     for copy in x_g[1:]:
         copy.wait_recv()
     gain = lambda i: r.vec[pl.ds(i, 1), :]
@@ -474,19 +688,16 @@
         r.ln_all[tile(t), :] = (normed * gain(0) + gain(2)).astype(BF)
 
     loop(4, ln_tile)
-    proj_z = [
-        net.send(r.proj_s.at[rows_at(96 * x, 96)], r.w_proj.at[proj_mine], net.line(d))
-        for d in range(1, nz)
-    ]
-    qkv_x = across_x(r.w_qkv, qkv_z)
-    out_z = [
-        net.send(r.out_s.at[:, half_cols(x)], r.w_out.at[rows_at(own48, 48), half_cols(x)], net.line(d))
-        for d in range(1, nz)
-    ]
-    cot_g = plane_gather_start(r.cot_own, r.cot_all)
+    qkv_s.relay()
+    qkv_s.rest()
+    for copy in fc_p:
+        copy.wait_recv()
+    fc_s.start()
+    cot_g = plane_gather_start(cot_own, r.cot_all)
     r.qm[2] = jnp.zeros((512, 128), BF)
-    for copy in qkv_x:
-        copy.wait_recv()
+    out_s.relay()
+    out_s.rest()
+    qkv_s.finish_recv()
 
     bias_u = jnp.sum(jnp.where(row == 9 + u, r.vec[...], 0.0), 0, keepdims=True)[:, 0:576]
 
@@ -555,13 +766,10 @@
     r.l_run[...] = jnp.zeros((3, 1, 512), F32)
     r.o_t[...] = jnp.zeros((3, 128, 512), F32)
     kv_start(0)
-    for copy in fc_p:
-        copy.wait_recv()
-    fc_z = along_z(r.w_fc)
     plane_gather_forward(cot_g, r.cot_all)
     attend(z)
-
-    weights = {}
+    fc_s.relay()
+
     for step in range(1, nz):
         for way in range(2):
             @pl.when(z - step >= 0 if way == 0 else z + step < nz)
@@ -571,18 +779,17 @@
         if step < nz - 1:
             kv_start(step)
         if step == 1:
-            weights["proj"] = across_x(r.w_proj, proj_z)
-            out_x = []
-            for d, copy in enumerate(out_z, 1):
-                copy.wait_recv()
-                part = r.w_out.at[rows_at((4 * net.zplus(nz - d) + u) * 48, 48), half_cols(x)]
-                out_x.append(net.send(part, part, net.other_x()))
-        if step == 2:
+            fc_s.rest()
+            out_s.finish_recv()
             out_rows = lambda zz, who: r.w_out.at[rows_at((4 * zz + who) * 48, 48)]
-            for copy in out_x:
-                copy.wait_recv()
             out_y = [net.send(out_rows(zz, u), out_rows(zz, u), net.plane(2)) for zz in range(nz)]
             out_c = [net.send(out_rows(zz, u), out_rows(zz, u), net.plane(1)) for zz in range(nz)]
+        if step == 2:
+            for zz, copy in enumerate(out_y):
+                copy.wait_recv()
+                out_c.append(net.send(out_rows(zz, u ^ 2), out_rows(zz, u ^ 2), net.plane(1)))
+        if step == nz - 1:
+            proj_s.start()
 
         def either(way):
             j = jnp.where(way == 0, z - step, z + step)
@@ -592,11 +799,6 @@
                 attend(j)
 
         loop(2, either)
-        if step == nz - 1:
-            for zz, copy in enumerate(out_y):
-                copy.wait_recv()
-                out_c.append(net.send(out_rows(zz, u ^ 2), out_rows(zz, u ^ 2), net.plane(1)))
-    weights["fc"] = across_x(r.w_fc, fc_z)
 
     rowi = lax.broadcasted_iota(jnp.int32, (128, 512), 0)
     r.l_inv[...] = 1.0 / r.l_run[...]
@@ -615,16 +817,10 @@
         r.w_outp[256 * g + 192:256 * g + 256, :] = r.w_out[192 * g + 128:192 * g + 192, :]
     for copy in cot_g[1:]:
         copy.wait_recv()
-    for copy in weights["proj"]:
-        copy.wait_recv()
-
-    def gact_tile(t):
-        r.gact[tile(t), :] = dot_nt(r.cot_all[tile(t), :], r.w_proj[...])
-
-    loop(4, gact_tile)
+    proj_s.relay()
     for copy in att_p:
         copy.wait_recv()
-    resid = r.x_own[...].astype(F32) + gain(4)
+    resid = x_own[...].astype(F32) + gain(4)
     for g in range(4):
         resid = resid + dot_nn(r.merged[g], r.w_outp[256 * g:256 * g + 256, :])
     r.resid[...] = resid
@@ -634,27 +830,29 @@
     r.lm_all[tile(u), :] = (normed * gain(1) + gain(6)).astype(BF)
     lm_own = r.lm_all.at[tile(u)]
     lm_g = [net.send(lm_own, lm_own, net.plane(m)) for m in (2, 1)]
-    for copy in weights["fc"]:
-        copy.wait_recv()
+    fc_s.finish_recv()
 
     r.vec_g[...] = jnp.zeros((16, 768), F32)
 
-    def mlp_tile(t, part):
+    def mlp_front(t):
         rows = tile(t)
         pre = dot_nn(r.lm_all[rows, :], r.w_fc[...]) + gain(8)
         square = pre * pre
         th = jnp.tanh(GELU_IN * (pre * (1.0 + 0.044715 * square)))
         r.act[rows, :] = (0.5 * pre * (1.0 + th)).astype(BF)
-        slope = 0.5 * (1.0 + th) + (0.5 * GELU_IN) * pre * (1.0 - th * th) * (1.0 + 0.134145 * square)
-        gp = (slope * r.gact[rows, :]).astype(BF)
+        r.slope[rows, :] = 0.5 * (1.0 + th) + (0.5 * GELU_IN) * pre * (1.0 - th * th) * (1.0 + 0.134145 * square)
+
+    def mlp_back(t):
+        rows = tile(t)
+        gp = (r.slope[rows, :] * dot_nt(r.cot_all[rows, :], r.w_proj[...])).astype(BF)
         r.grad_pre[rows, :] = gp
         r.fcb[...] += jnp.sum(gp.astype(F32), 0, keepdims=True)
-        part[t] = dot_nt(gp, r.w_fc[...]).astype(BF)
+        r.gm_part[t] = dot_nt(gp, r.w_fc[...]).astype(BF)
 
     r.fcb[...] = jnp.zeros((1, 768), F32)
-    mlp_tile(u, r.gm_part)
+    mlp_front(u)
     lm_g[1].wait_recv()
-    mlp_tile(u ^ 1, r.gm_part)
+    mlp_front(u ^ 1)
     plane_gather_forward(lm_g, r.lm_all)
 
     def reduce_core(i, t, part, land_c):
@@ -670,22 +868,22 @@
         copy_y.wait_recv()
         return part[u].astype(F32) + land_c[1].astype(F32) + land_y[...].astype(F32)
 
+    mlp_front(u ^ 2)
+    proj_s.rest()
+    lm_g[2].wait_recv()
+    mlp_front(u ^ 3)
+    proj_s.finish_recv()
+    mlp_back(u ^ 3)
+    gm_c0 = reduce_core(0, u ^ 3, r.gm_part, r.gm_c)
+    mlp_back(u ^ 1)
     gm_c1 = reduce_core(1, u ^ 1, r.gm_part, r.gm_c)
-    mlp_tile(u ^ 2, r.gm_part)
-    lm_g[2].wait_recv()
-    mlp_tile(u ^ 3, r.gm_part)
-    gm_c0 = reduce_core(0, u ^ 3, r.gm_part, r.gm_c)
+    mlp_back(u ^ 2)
+    gm_y = reduce_y(gm_c0, r.gm_part, r.gm_c, r.gm_mid, r.gm_y)
+    mlp_back(u)
     r.vec_g[...] += jnp.where(row == 10 + u, r.fcb[...], 0.0)
 
     def branch_tile(t):
         r.br_part[t] = dot_nn(r.act[tile(t), :], r.w_proj[...]).astype(BF)
-
-    branch_tile(u ^ 3)
-    branch_tile(u ^ 1)
-    gm_y = reduce_y(gm_c0, r.gm_part, r.gm_c, r.gm_mid, r.gm_y)
-    br_c = [reduce_core(0, u ^ 3, r.br_part, r.br_c), reduce_core(1, u ^ 1, r.br_part, r.br_c)]
-    branch_tile(u ^ 2)
-    branch_tile(u)
 
     def weight_grad(a, b, out, tiles):
         def one(i):
@@ -694,29 +892,24 @@
 
         loop(tiles, one)
 
-    def start_x(grad, land):
-        return [
-            net.send(grad.at[rows_at(192 * zz + 96 * (1 - x), 96)], land.at[zz], net.other_x())
-            for zz in range(nz)
-        ]
-
-    def start_z(copies, grad, land, mine, land_z):
-        for zz in range(nz):
-            copies[zz].wait_recv()
-            mine[zz] = (grad[rows_at(192 * zz + 96 * x, 96), :].astype(F32) + land[zz].astype(F32)).astype(BF)
-        return [
-            net.send(mine.at[net.zplus(d)], land_z.at[d - 1], net.line(d)) for d in range(1, nz)
-        ]
-
-    def end_z(copies, mine, land_z, final):
-        total = mine[z].astype(F32)
-        for d in range(nz - 1):
-            copies[d].wait_recv()
-            total = total + land_z[d].astype(F32)
-        final[...] = total.astype(BF)
+    def collect(base, grad, land_x, mine, land_z, relay):
+        return Collect(
+            net, r.co_send, r.co_recv, base,
+            lambda zz: grad.at[rows_at(192 * zz + 96 * (1 - x), 96)],
+            lambda zz: grad[rows_at(192 * zz + 96 * x, 96), :].astype(F32),
+            land_x, mine, land_z, relay)
+
+    proj_c = collect(0, r.proj_g, r.proj_x, r.proj_m, r.proj_z, r.proj_r)
+    fc_c = collect(9, r.fc_g, r.fc_x, r.fc_m, r.fc_z, r.fc_r)
+    qkv_c = collect(18, r.qkv_g, r.qkv_x, r.qkv_m, r.qkv_z, r.qkv_r)
 
     weight_grad(r.act, r.cot_all, r.proj_g, 6)
-    proj_a = start_x(r.proj_g, r.proj_x)
+    proj_c.start()
+    branch_tile(u ^ 3)
+    branch_tile(u ^ 1)
+    br_c = [reduce_core(0, u ^ 3, r.br_part, r.br_c), reduce_core(1, u ^ 1, r.br_part, r.br_c)]
+    branch_tile(u ^ 2)
+    branch_tile(u)
 
     gm = reduce_end(gm_c1, gm_y, r.gm_part, r.gm_c, r.gm_y)
     normed = r.normed_mid[...]
@@ -729,7 +922,7 @@
             e - jnp.mean(e, -1, keepdims=True) - normed * jnp.mean(e * normed, -1, keepdims=True)
         )
 
-    cot = r.cot_own[...].astype(F32)
+    cot = cot_own[...].astype(F32)
     r.vec_g[4:5, :] = jnp.sum(cot, 0, keepdims=True)
     grad_resid = cot + norm_grad(gm, normed, r.inverse_mid[...], gain(1))
     r.grad_resid[...] = grad_resid
@@ -743,9 +936,7 @@
     loop(4, gmer_tile)
     ga_p = [net.send(r.gmer.at[u ^ m], r.ga.at[tile(u)], net.plane(m)) for m in (2, 3, 1)]
     r.ga[tile(u), :] = r.gmer[u]
-    br_y = reduce_y(br_c[0], r.br_part, r.br_c, r.br_mid, r.br_y)
     weight_grad(r.lm_all, r.grad_pre, r.fc_g, 6)
-    fc_a = start_x(r.fc_g, r.fc_x)
     for g in range(4):
         res = dot_tn(r.merged[g], r.gb[...]).astype(BF)
         at = slice(48 * g, 48 * g + 48)
@@ -755,9 +946,8 @@
         r.out_g[0, 1, 48 * g + 32:48 * g + 48, :] = res[192:208]
         r.out_g[1, 1, at, :] = res[208:256]
     og_c = net.send(r.out_g.at[1 - c], r.og_c, net.plane(1))
-    r.output[...] = (
-        r.resid[...] + gain(5) + reduce_end(br_c[1], br_y, r.br_part, r.br_c, r.br_y)
-    ).astype(BF)
+    proj_c.part(0)
+    proj_c.part(1)
     for copy in ga_p:
         copy.wait_recv()
 
@@ -837,12 +1027,20 @@
     for step in range(nz - 1, 0, -1):
         chain_step(step)
         if step == nz - 1:
-            proj_b = start_z(proj_a, r.proj_g, r.proj_x, r.proj_m, r.proj_z)
+            proj_c.part(2)
+            proj_c.part(3)
+            fc_c.start()
+            br_y = reduce_y(br_c[0], r.br_part, r.br_c, r.br_mid, r.br_y)
             og_c.wait_recv()
             r.og_1[...] = (r.out_g[c].astype(F32) + r.og_c[...].astype(F32)).astype(BF)
             og_y = net.send(r.og_1.at[1 - y], r.og_y, net.plane(2))
         if step == nz - 2:
-            fc_b = start_z(fc_a, r.fc_g, r.fc_x, r.fc_m, r.fc_z)
+            proj_c.second()
+            r.output[...] = (
+                r.resid[...] + gain(5) + reduce_end(br_c[1], br_y, r.br_part, r.br_c, r.br_y)
+            ).astype(BF)
+            fc_c.part(0)
+            fc_c.part(1)
             og_y.wait_recv()
             r.og_2[...] = (r.og_1[y].astype(F32) + r.og_y[...].astype(F32)).astype(BF)
             og_x = net.send(r.og_2.at[:, half_cols(1 - x)], r.og_x, net.other_x())
@@ -853,8 +1051,11 @@
                 net.send(r.og_3.at[rows_at(48 * net.zplus(d), 48)], r.og_z.at[d - 1], net.line(d))
                 for d in range(1, nz)
             ]
+            fc_c.part(2)
+            fc_c.part(3)
     back(z)
 
+    fc_c.second()
     @pl.when(z + 1 < nz)
     def _():
         chain_copy(0, 1).wait_recv()
@@ -871,7 +1072,7 @@
     r.gqkv[:, 512:576] = jnp.transpose(r.dq_t[2] * 0.125)[:, 0:64].astype(BF)
 
     weight_grad(r.ln_all, r.gqkv, r.qkv_g, 6)
-    qkv_a = start_x(r.qkv_g, r.qkv_x)
+    qkv_c.start()
 
     def gin_tile(t):
         r.gi_part[t] = dot_nt(r.gqkv[tile(t), :], r.w_qkv[...]).astype(BF)
@@ -884,11 +1085,12 @@
     gi_y = reduce_y(gi_c0, r.gi_part, r.gi_c, r.gi_mid, r.gi_y)
     gin_tile(u)
     r.vec_g[:, 0:576] += jnp.where(row[:, 0:576] == 6 + u, jnp.sum(r.gqkv[...].astype(F32), 0, keepdims=True), 0.0)
-    qkv_b = start_z(qkv_a, r.qkv_g, r.qkv_x, r.qkv_m, r.qkv_z)
-    end_z(proj_b, r.proj_m, r.proj_z, r.proj_f)
+    qkv_c.first()
+    proj_c.total(r.acc)
+    r.proj_f[...] = r.acc[...].astype(BF)
     mine = rows_at(96 * x, 96)
     r.proj_o[mine, :] = r.proj_f[...]
-    proj_c = net.send(r.proj_f, r.proj_o.at[mine], net.other_x())
+    proj_last = net.send(r.proj_f, r.proj_o.at[mine], net.other_x())
 
     finals = []
 
@@ -924,12 +1126,14 @@
                 copy.wait_recv()
 
     gin = reduce_end(gi_c1, gi_y, r.gi_part, r.gi_c, r.gi_y)
-    normed, inverse = normalize(r.x_own[...].astype(F32))
+    normed, inverse = normalize(x_own[...].astype(F32))
     r.vec_g[0:1, :] = jnp.sum(gin * normed, 0, keepdims=True)
     r.vec_g[2:3, :] = jnp.sum(gin, 0, keepdims=True)
     vec_m = [net.send(r.vec_g, r.vg_p.at[m - 1], net.plane(m)) for m in (1, 2, 3)]
     r.input_grad[...] = (r.grad_resid[...] + norm_grad(gin, normed, inverse, gain(0))).astype(BF)
-    end_z(fc_b, r.fc_m, r.fc_z, r.fc_f)
+    qkv_c.second()
+    fc_c.total(r.acc)
+    r.fc_f[...] = r.acc[...].astype(BF)
     hand_out(0, r.fc_f, r.fc_o)
     total = r.vec_g[...]
     for m in range(3):
@@ -949,11 +1153,24 @@
         total = total + r.vg_z[d]
     r.vg_2[...] = total
     vec_last = net.send(r.vg_2, r.vg_x, net.other_x())
-    end_z(qkv_b, r.qkv_m, r.qkv_z, r.qkv_f)
+    qkv_c.total(r.acc_q)
+    r.qkv_f[...] = r.acc_q[...].astype(BF)
     hand_out(4, r.qkv_f, r.qkv_o)
     vec_last.wait_recv()
-    r.vec_o[...] = r.vg_2[...] + r.vg_x[...]
-    proj_c.wait_recv()
+    total = r.vg_2[...] + r.vg_x[...]
+    pick = lambda i: jnp.sum(jnp.where(row == i, total, 0.0), 0, keepdims=True)
+    heads, hidden = pick(6 + z), pick(10 + u)
+    bias[0:1, 0:128] = heads[:, 0:128]
+    bias[0:1, 128:192] = heads[:, 512:576]
+    bias[1:2, 0:128] = heads[:, 256:384]
+    bias[1:2, 128:192] = heads[:, 448:512]
+    mine8 = pltpu.roll(total[0:8], 768 - 48 * (4 * z + u), 1)
+    vp[0:8, :] = mine8
+    both = pltpu.roll(bias[...], 256 - 48 * u, 1)
+    vp[6:8, 0:256] = both[0:2]
+    vp[8:16, :] = pltpu.roll(jnp.broadcast_to(hidden, (8, 768)), 768 - 192 * z, 1)
+    r.vec_o[...] = vp[...]
+    proj_last.wait_recv()
     og_last.wait_recv()
     await_native(0, r.fc_f, r.fc_o)
     await_native(4, r.qkv_f, r.qkv_o)
@@ -972,6 +1189,8 @@
             @pl.when(z - step >= 0 if way == 0 else z + step < nz)
             def _():
                 chain_copy(way, step).wait_send()
+    for part in (qkv_s, fc_s, proj_s, out_s, proj_c, fc_c, qkv_c):
+        part.finish()
     net.finish()
 
 
@@ -986,13 +1205,16 @@
     f = lambda *shape: vm(*shape, kind=F32)
     keys = 512 * nz
     scratch = dict(
+        qkv_raw=vm(48, 2304), fc_raw=vm(48, 3072), qkv_pre=vm(4, 48, 576), fc_pre=vm(4, 48, 768),
+        vec_f32=f(16, 768), bias_f32=f(8, 256), vec_pre=vm(16, 768),
+        pos_row=pltpu.VMEM((1, keys), jnp.int32), pos_col=pltpu.VMEM((keys, 1), jnp.int32),
         w_qkv=vm(768, 576), w_fc=vm(768, 768), w_proj=vm(768, 768), w_out=vm(768, 768), w_outp=vm(1024, 768),
         vec_land_z=vm(nz - 1, 16, 768), vec_u=vm(16, 768), vec_land_p=vm(3, 16, 768), vec=f(16, 768),
         x_all=vm(512, 768), cot_all=vm(512, 768), ln_all=vm(512, 768), lm_all=vm(512, 768),
         qm=vm(3, 512, 128), kv_all=vm(nz, 512, 384), s_buf=f(512, 512), pt=vm(nz * 3, 512, 512),
         m_run=f(3, 1, 512), l_run=f(3, 1, 512), l_inv=f(3, 1, 512), m_at=f(nz * 3, 1, 512), o_t=f(3, 128, 512),
         att_t=f(2, 128, 512), att=vm(512, 256), merged=vm(4, 128, 256),
-        resid=f(128, 768), normed_mid=f(128, 768), inverse_mid=f(128, 1), gact=f(512, 768),
+        resid=f(128, 768), normed_mid=f(128, 768), inverse_mid=f(128, 1), slope=f(512, 768),
         act=vm(512, 768), grad_pre=vm(512, 768), fcb=f(1, 768), vec_g=f(16, 768),
         gm_part=vm(4, 128, 768), gm_c=vm(2, 128, 768), gm_mid=vm(128, 768), gm_y=vm(128, 768),
         br_part=vm(4, 128, 768), br_c=vm(2, 128, 768), br_mid=vm(128, 768), br_y=vm(128, 768),
@@ -1004,17 +1226,22 @@
         qkv_x=vm(nz, 96, 576), fc_x=vm(nz, 96, 768), proj_x=vm(nz, 96, 768),
         qkv_m=vm(nz, 96, 576), fc_m=vm(nz, 96, 768), proj_m=vm(nz, 96, 768),
         qkv_z=vm(nz - 1, 96, 576), fc_z=vm(nz - 1, 96, 768), proj_z=vm(nz - 1, 96, 768),
+        qkv_r=vm(96, 576), fc_r=vm(96, 768), proj_r=vm(96, 768), acc=f(96, 768), acc_q=f(96, 576),
         qkv_f=vm(96, 576), fc_f=vm(96, 768), proj_f=vm(96, 768),
         og_c=vm(2, 192, 768), og_1=vm(2, 192, 768), og_y=vm(192, 768), og_2=vm(192, 768),
         og_x=vm(192, 384), og_3=vm(192, 384), og_z=vm(nz - 1, 48, 384),
         vg_p=f(3, 16, 768), vg_1=f(16, 768), vg_z=f(nz - 1, 16, 768), vg_2=f(16, 768), vg_x=f(16, 768),
         send_sem=pltpu.SemaphoreType.DMA((112,)), recv_sem=pltpu.SemaphoreType.DMA((112,)),
+        sp_send=pltpu.SemaphoreType.DMA((32,)), sp_recv=pltpu.SemaphoreType.DMA((32,)),
+        co_send=pltpu.SemaphoreType.DMA((27,)), co_recv=pltpu.SemaphoreType.DMA((27,)),
         local_sem=pltpu.SemaphoreType.DMA((6,)),
         kv_send=pltpu.SemaphoreType.DMA((2 * nz,)), kv_recv=pltpu.SemaphoreType.DMA((2 * nz,)),
         ch_send=pltpu.SemaphoreType.DMA((2 * nz,)), ch_recv=pltpu.SemaphoreType.DMA((2 * nz,)),
         f_send=pltpu.SemaphoreType.DMA((8,)), f_recv=pltpu.SemaphoreType.DMA((8,)),
     )
     names = [*operands, *outs, *scratch]
+    places = {name: pl.BlockSpec(memory_space=pl.ANY) for name in ("x_in", "cot_in", "qkv_in", "fc_in", "out_in", "proj_in")}
+    places["order_in"] = pl.BlockSpec(memory_space=pltpu.SMEM)
 
     def kernel(*refs):
         block_kernel(nz, types.SimpleNamespace(**dict(zip(names, refs, strict=True))))
@@ -1022,7 +1249,7 @@
     got = pl.pallas_call(
         kernel,
         out_shape=tuple(jax.ShapeDtypeStruct(*s) for s in outs.values()),
-        in_specs=[VSPEC] * len(operands),
+        in_specs=[places.get(name, VSPEC) for name in operands],
         out_specs=(VSPEC,) * len(outs),
         scratch_shapes=list(scratch.values()),
         compiler_params=pltpu.CompilerParams(
@@ -1033,67 +1260,59 @@
     return dict(zip(outs, got, strict=True))
 
 
-def arrange_qkv(w):
-    rows = w.shape[0]
-    parts = w.reshape(rows, 3, 4, 3, 64)
-    order = ((0, 0), (0, 1), (1, 0), (1, 1), (2, 0), (2, 1), (1, 2), (2, 2), (0, 2))
-    return jnp.stack([parts[:, t, :, h] for t, h in order], 2).transpose(1, 0, 2, 3).reshape(4, rows, 576)
-
-
-def restore_qkv(g):
-    rows = g.shape[1]
-    parts = g.reshape(4, rows, 9, 64)
-    q = jnp.stack([parts[:, :, i] for i in (0, 1, 8)], 2)
-    k = jnp.stack([parts[:, :, i] for i in (2, 3, 6)], 2)
-    v = jnp.stack([parts[:, :, i] for i in (4, 5, 7)], 2)
-    return jnp.stack([q, k, v], 0).transpose(2, 0, 1, 3, 4).reshape(rows, 2304)
+def hand_over_kernel(nz, output, input_grad, qkv_o, fc_o, proj_o, out_o, vec_o,
+                     output_f, input_grad_f, gains_f, biases_f, mid_f, vb_f, qkv_f, out_f, fc_f, fcb_f, proj_f):
+    output_f[...] = output[...]
+    input_grad_f[...] = input_grad[...]
+    gains_f[...] = vec_o[0:2, 0:48]
+    biases_f[0:1, :] = vec_o[2:3, 0:48]
+    biases_f[1:2, :] = vec_o[6:7, 0:48]
+    biases_f[2:4, :] = vec_o[3:5, 0:48]
+    mid_f[...] = vec_o[5:6, 0:48]
+    vb_f[...] = vec_o[7:8, 0:48]
+    fcb_f[...] = vec_o[8:9, 0:192]
+    out_f[...] = out_o[...].astype(F32)
+    proj_f[...] = proj_o[...].astype(F32)
+    for g in range(4):
+        for t in range(3):
+            qkv_f[:, 768 * t + 192 * g:768 * t + 192 * g + 128] = qkv_o[g, :, 128 * t:128 * t + 128].astype(F32)
+        for at, t in ((384, 1), (448, 2), (512, 0)):
+            qkv_f[:, 768 * t + 192 * g + 128:768 * t + 192 * g + 192] = qkv_o[g, :, at:at + 64].astype(F32)
+        for zz in range(nz):
+            fc_f[:, 768 * zz + 192 * g:768 * zz + 192 * g + 192] = fc_o[g, :, 192 * zz:192 * zz + 192].astype(F32)
+
+
+def hand_over(nz, got):
+    shapes = [((128, 768), BF), ((128, 768), BF), ((2, 48), F32), ((4, 48), F32), ((1, 48), F32), ((1, 48), F32),
+              ((48, 2304), F32), ((48, 768), F32), ((48, 3072), F32), ((1, 192), F32), ((192, 768), F32)]
+    return pl.pallas_call(
+        functools.partial(hand_over_kernel, nz),
+        out_shape=tuple(jax.ShapeDtypeStruct(*s) for s in shapes),
+        in_specs=[VSPEC] * len(got),
+        out_specs=(VSPEC,) * len(shapes),
+        compiler_params=pltpu.CompilerParams(vmem_limit_bytes=16 * 2**20),
+        name="hand_over",
+    )(*got.values())
 
 
 def device_fast(nz, inputs, stretch_order, norm_gains, biases, mid_shift, value_bias, qkv_weight, out_weight, fc_weight, fc_bias, proj_weight, cotangent):
-    z, u = lax.axis_index("blk"), lax.axis_index("uly")
-    place = (4 * z + u) * 48
-    pack = jnp.concatenate([norm_gains, biases, mid_shift[None], value_bias[None]], 0)
-    vec8 = lax.dynamic_update_slice(jnp.zeros((8, 768), BF), pack, (0, place))
-    fcb = lax.dynamic_update_slice(jnp.zeros((1, 768), BF), fc_bias[None], (0, 192 * z))
-    wide = lax.dynamic_update_slice(jnp.zeros((2, 192), BF), jnp.stack([biases[1], value_bias]), (0, 48 * u))
-    zero = jnp.zeros((64,), BF)
-    q, v = wide[0].reshape(3, 64), wide[1].reshape(3, 64)
-    local = jnp.concatenate([q[0], q[1], zero, zero, v[0], v[1], zero, v[2], q[2], jnp.zeros((192,), BF)])[None]
-    four = lax.dynamic_update_slice(jnp.zeros((4, 768), BF), local, (z, 0))
-    vec_pre = jnp.concatenate([vec8, fcb, four, jnp.zeros((3, 768), BF)], 0)
-    pos = (stretch_order[0][:, None] * 64 + jnp.arange(64, dtype=jnp.int32)[None]).reshape(-1)
     got = block_call(
         nz,
-        x_own=inputs[0],
-        cot_own=cotangent[0],
-        qkv_pre=arrange_qkv(qkv_weight),
-        fc_pre=fc_weight.reshape(48, nz, 4, 192).transpose(2, 0, 1, 3).reshape(4, 48, 768),
-        out_s=out_weight,
-        proj_s=proj_weight,
-        vec_pre=vec_pre,
-        pos_row=pos[None],
-        pos_col=pos[:, None],
-    )
-    vec_o = got["vec_o"]
-    mine = lax.dynamic_slice(vec_o, (0, place), (6, 48))
-    qs = lax.dynamic_slice(vec_o, (6 + z, 0), (1, 576))[0].reshape(9, 64)
-    qb = lax.dynamic_slice(jnp.concatenate([qs[0], qs[1], qs[8]]), (48 * u,), (48,))
-    vb = lax.dynamic_slice(jnp.concatenate([qs[4], qs[5], qs[7]]), (48 * u,), (48,))
-    fb = lax.dynamic_slice(vec_o, (10 + u, 192 * z), (1, 192))[0]
-    fc_g = got["fc_o"].reshape(4, 48, nz, 192).transpose(1, 2, 0, 3).reshape(48, 3072)
-    return (
-        got["output"][None],
-        got["input_grad"][None],
-        mine[0:2],
-        jnp.stack([mine[2], qb, mine[3], mine[4]]),
-        mine[5],
-        vb,
-        restore_qkv(got["qkv_o"]).astype(F32),
-        got["out_o"].astype(F32),
-        fc_g.astype(F32),
-        fb,
-        got["proj_o"].astype(F32),
-    )
+        x_in=inputs[0],
+        cot_in=cotangent[0],
+        qkv_in=qkv_weight,
+        fc_in=fc_weight,
+        out_in=out_weight,
+        proj_in=proj_weight,
+        gains_in=norm_gains,
+        biases_in=biases,
+        mid_in=mid_shift[None],
+        vb_in=value_bias[None],
+        fcb_in=fc_bias[None],
+        order_in=stretch_order,
+    )
+    output, input_grad, gains, rows, mid, vb, qkv, out, fc, fcb, proj = hand_over(nz, got)
+    return output[None], input_grad[None], gains, rows, mid[0], vb[0], qkv, out, fc, fcb[0], proj
 
 
 def solution(mesh):
@@ -1113,7 +1332,7 @@
     )
     sizes = dict(mesh.shape)
     nz = sizes["blk"]
-    fast = sizes["uly"] == 4 and sizes["dp"] == 2 and 768 % (nz * 4 * 16) == 0
+    fast = sizes["uly"] == 4 and sizes["dp"] == 2 and nz == 4
     chosen = functools.partial(device_fast, nz) if fast else per_device
     return jax.shard_map(
         chosen,

time: 227 us -> 188 us (0.83)
  Pallas kernels: 198 us -> 180 us
  local copies, waits for them, and re-layouts: 22.5 us -> 7.61 us
  other arithmetic: 5.62 us -> 0 us
    pallas_call x1, Pallas kernels: 198 us -> 178 us  [block_call(): pl.pallas_call(kernel, out_shape=tuple((jax.ShapeDtypeStruct(*s) for s in...]
    reshape x6 -> x0, local copies, waits for them, and re-layouts: 5.79 us -> none  [the longest x1 1.7 us: arrange_qkv(): parts = w.reshape(rows, 3, 4, 3, 64)]
    unnamed x24 -> x16, local copies, waits for them, and re-layouts: 1.52 us -> 7.04 us
    convert_element_type x5 -> x0, local copies, waits for them, and re-layouts: 4.28 us -> none  [the longest x3 2.64 us: device_fast(): fc_g.astype(F32)]
    dynamic_slice x3 -> x0, local copies, waits for them, and re-layouts: 2.7 us -> none  [the longest x1 1.34 us: device_fast(): fb = lax.dynamic_slice(vec_o, (10 + u, 192 * z), (1, 192))[0]]
    add x2 -> x0, local copies, waits for them, and re-layouts: 2.67 us -> none  [device_fast(): stretch_order[0][:, None] * 64 + jnp.arange(64, dtype=jnp.int32)[None]]
    slice x5 -> x0, local copies, waits for them, and re-layouts: 2.45 us -> none  [the longest x1 0.73 us: arrange_qkv(): parts[:, t, :, h]]
where the time goes in v3:
time: 188 us
  Pallas kernels  180 us (96%)
  local copies, waits for them, and re-layouts  7.61 us (4%)
    pallas_call x1, Pallas kernels, block_call(): pl.pallas_call(kernel, out_shape=tuple((jax.ShapeDtypeStruct(*s) for s in...  178 us
    unnamed x16, local copies, waits for them, and re-layouts  7.04 us

profile of v3, /device:TPU:0, one launch (start us, length us, event | category | flops | bytes accessed | tf_op | source)
XLA Modules:
  0.0 187.9 jit_solution(17667278558548122707)
XLA Ops:
  0.6 0.0 copy-start.7
  0.7 0.6 copy-done.7
  1.3 0.6 broadcast_in_dim.17.refs_10_
  1.9 178.2 %transformer_block.1 = (bf16[128,768]{1,0:T(8,128)(2,1)}, bf16[128,768]{1,0:T(8,128)(2,1)}, bf16[4,48,576]{2,1,0:T(8,128)(2,1)}, bf16[4,48,768]{2,1,0:T(8,128)(2...) custom-call(bf16[128,768]{1,0:T(8,128)(2,1)} %bitcast.9, bf16[128,768]{1,0:T(8,128)(2,1)} %bitcast.10, ...), custom_call_target="tpu_custom_call" | custom-call | tf_op jit(solution)/shard_map/transformer_block/pallas_call | solution.py:1249
  180.0 0.0 copy-start
  180.0 1.0 copy-done
  181.0 0.0 copy-start.1
  181.0 1.0 copy-done.1
  182.0 0.0 copy-start.2
  182.0 0.9 copy-done.2
  182.9 0.0 copy-start.3
  182.9 0.9 copy-done.3
  183.8 0.0 copy-start.4
  183.8 0.9 copy-done.4
  184.8 0.0 copy-start.5
  184.8 0.9 copy-done.5
  185.6 0.0 copy-start.6
  185.6 0.8 copy-done.6
  186.4 1.5 hand_over.1
Async XLA Ops:
  0.6 0.7 copy-start.7
  180.0 1.0 copy-start
  181.0 1.0 copy-start.1
  182.0 0.9 copy-start.2
  182.9 0.9 copy-start.3
  183.8 0.9 copy-start.4
  184.8 0.9 copy-start.5
  185.6 0.8 copy-start.6

commit v4 on v3

--- a/solution.py
+++ b/solution.py
@@ -590,8 +590,8 @@
         pltpu.make_async_copy(r.proj_in, r.w_proj.at[rows_at(192 * z, 192)], r.local_sem.at[4]),
         pltpu.make_async_copy(r.cot_in, cot_own, r.local_sem.at[5]),
     ]
-    for copy in local:
-        copy.start()
+    local[0].start()
+    local[2].start()
     net.hail()
     local[0].wait()
     for g in range(4):
@@ -600,6 +600,29 @@
         for at, t in ((384, 1), (448, 2), (512, 0)):
             r.qkv_pre[g, :, at:at + 64] = r.qkv_raw[:, 768 * t + 192 * g + 128:768 * t + 192 * g + 192]
     r.w_qkv[rows_at(own48, 48), :] = r.qkv_pre[u]
+    net.meet()
+
+    def plane_gather_start(own, full):
+        return [net.send(own, full.at[tile(u)], net.plane(m)) for m in (2, 1)]
+
+    def plane_gather_forward(sent, full):
+        sent[0].wait_recv()
+        sent.append(net.send(full.at[tile(u ^ 2)], full.at[tile(u ^ 2)], net.plane(1)))
+
+    in_plane = lambda pre, full: [
+        net.send(pre.at[u ^ m], full.at[rows_at(own48, 48)], net.plane(m)) for m in (1, 2, 3)
+    ]
+    block96 = lambda full: lambda j: full.at[rows_at(192 * j + 96 * x, 96)]
+    spread = lambda base, block: Spread(net, r.sp_send, r.sp_recv, base, block)
+    qkv_s = spread(0, block96(r.w_qkv))
+    fc_s = spread(8, block96(r.w_fc))
+    proj_s = spread(16, block96(r.w_proj))
+    out_s = spread(24, lambda j: r.w_out.at[rows_at((4 * j + u) * 48, 48), half_cols(x)])
+    qkv_p = in_plane(r.qkv_pre, r.w_qkv)
+    local[2].wait()
+    x_g = plane_gather_start(x_own, r.x_all)
+    for i in (3, 1, 4, 5):
+        local[i].start()
     vp = r.vec_f32
     vp[...] = jnp.zeros((16, 768), F32)
     vp[0:2, 0:48] = r.gains_in[...].astype(F32)
@@ -623,29 +646,21 @@
     bias_row = jnp.sum(jnp.where(row8 == 1, high, 0.0), 0, keepdims=True)
     vp[8:16, :] = fcb_row + jnp.where(row8 == 1 + z, bias_row, 0.0)
     r.vec_pre[...] = vp[...].astype(BF)
-    net.meet()
-
-    def plane_gather_start(own, full):
-        return [net.send(own, full.at[tile(u)], net.plane(m)) for m in (2, 1)]
-
-    def plane_gather_forward(sent, full):
-        sent[0].wait_recv()
-        sent.append(net.send(full.at[tile(u ^ 2)], full.at[tile(u ^ 2)], net.plane(1)))
-
-    in_plane = lambda pre, full: [
-        net.send(pre.at[u ^ m], full.at[rows_at(own48, 48)], net.plane(m)) for m in (1, 2, 3)
-    ]
-    block96 = lambda full: lambda j: full.at[rows_at(192 * j + 96 * x, 96)]
-    spread = lambda base, block: Spread(net, r.sp_send, r.sp_recv, base, block)
-    qkv_s = spread(0, block96(r.w_qkv))
-    fc_s = spread(8, block96(r.w_fc))
-    proj_s = spread(16, block96(r.w_proj))
-    out_s = spread(24, lambda j: r.w_out.at[rows_at((4 * j + u) * 48, 48), half_cols(x)])
-    qkv_p = in_plane(r.qkv_pre, r.w_qkv)
     vec_z = [net.send(r.vec_pre, r.vec_land_z.at[d - 1], net.line(d)) for d in range(1, nz)]
-    for copy in local[1:]:
-        copy.wait()
+    for copy in qkv_p:
+        copy.wait_recv()
+    qkv_s.start()
+    local[3].wait()
     out_s.start()
+    total = r.vec_pre[...]
+    for d in range(nz - 1):
+        vec_z[d].wait_recv()
+        total = total + r.vec_land_z[d]
+    r.vec_u[...] = total
+    vec_p = [net.send(r.vec_u, r.vec_land_p.at[m - 1], net.plane(m)) for m in (1, 2, 3)]
+    plane_gather_forward(x_g, r.x_all)
+    for i in (1, 4, 5):
+        local[i].wait()
     for g in range(4):
         for zz in range(nz):
             r.fc_pre[g, :, 192 * zz:192 * zz + 192] = r.fc_raw[:, 768 * zz + 192 * g:768 * zz + 192 * g + 192]
@@ -656,17 +671,6 @@
         first = r.order_in[0, i] * 64
         r.pos_col[64 * i:64 * i + 64, :] = first + inner64
         r.pos_row[:, 64 * i:64 * i + 64] = first + inner64_row
-    for copy in qkv_p:
-        copy.wait_recv()
-    qkv_s.start()
-    x_g = plane_gather_start(x_own, r.x_all)
-    total = r.vec_pre[...]
-    for d in range(nz - 1):
-        vec_z[d].wait_recv()
-        total = total + r.vec_land_z[d]
-    r.vec_u[...] = total
-    vec_p = [net.send(r.vec_u, r.vec_land_p.at[m - 1], net.plane(m)) for m in (1, 2, 3)]
-    plane_gather_forward(x_g, r.x_all)
     fc_p = in_plane(r.fc_pre, r.w_fc)
     total = r.vec_u[...].astype(F32)
     row = lax.broadcasted_iota(jnp.int32, total.shape, 0)
@@ -713,13 +717,15 @@
 
     loop(4, qkv_tile)
 
-    def kv_copy(way, step):
+    third = lambda ch: slice(128 * ch, 128 * ch + 128)
+
+    def kv_copy(way, step, ch):
         block = z - step if way == 0 else z + step
         target = z + 1 if way == 0 else z - 1
         block, target = jnp.clip(block, 0, nz - 1), jnp.clip(target, 0, nz - 1)
         return pltpu.make_async_remote_copy(
-            src_ref=r.kv_all.at[block], dst_ref=r.kv_all.at[block],
-            send_sem=r.kv_send.at[way * nz + step], recv_sem=r.kv_recv.at[way * nz + step],
+            src_ref=r.kv_all.at[block, :, third(ch)], dst_ref=r.kv_all.at[block, :, third(ch)],
+            send_sem=r.kv_send.at[(way * nz + step) * 3 + ch], recv_sem=r.kv_recv.at[(way * nz + step) * 3 + ch],
             device_id=(x, target, u), device_id_type=MESH)
 
     def kv_sends(way, step):
@@ -727,11 +733,10 @@
             return jnp.logical_and(z - step >= 0, z + 1 < nz)
         return jnp.logical_and(z + step < nz, z >= 1)
 
-    def kv_start(step):
-        for way in range(2):
-            @pl.when(kv_sends(way, step))
-            def _():
-                kv_copy(way, step).start()
+    def kv_start(step, ch, way):
+        @pl.when(kv_sends(way, step))
+        def _():
+            kv_copy(way, step, ch).start()
 
     def attend(j):
         qp = r.pos_row[:, pl.ds(pl.multiple_of(512 * z, 128), 512)]
@@ -748,7 +753,7 @@
                 return jnp.maximum(top, jnp.max(s, 0, keepdims=True))
 
             old = r.m_run[h]
-            top = lax.fori_loop(0, 4, score, old)
+            top = lax.fori_loop(0, 4, score, old, unroll=True)
             shrink = jnp.exp(old - top)
 
             def weigh(kt, got):
@@ -756,7 +761,7 @@
                 r.pt[j * 3 + h, rows_at(128 * kt, 128), :] = p.astype(BF)
                 return got + jnp.sum(p, 0, keepdims=True)
 
-            got = lax.fori_loop(0, 4, weigh, jnp.zeros((1, 512), F32))
+            got = lax.fori_loop(0, 4, weigh, jnp.zeros((1, 512), F32), unroll=True)
             r.m_run[h] = top
             r.m_at[j * 3 + h] = top
             r.l_run[h] = r.l_run[h] * shrink + got
@@ -765,19 +770,22 @@
     r.m_run[...] = jnp.full((3, 1, 512), -1e30, F32)
     r.l_run[...] = jnp.zeros((3, 1, 512), F32)
     r.o_t[...] = jnp.zeros((3, 128, 512), F32)
-    kv_start(0)
+    for ch in range(3):
+        for way in range(2):
+            kv_start(0, ch, way)
     plane_gather_forward(cot_g, r.cot_all)
     attend(z)
     fc_s.relay()
 
     for step in range(1, nz):
-        for way in range(2):
-            @pl.when(z - step >= 0 if way == 0 else z + step < nz)
-            def _():
-                kv_copy(way, step - 1).wait_recv()
-
-        if step < nz - 1:
-            kv_start(step)
+        for ch in range(3):
+            for way in range(2):
+                @pl.when(z - step >= 0 if way == 0 else z + step < nz)
+                def _():
+                    kv_copy(way, step - 1, ch).wait_recv()
+
+                if step < nz - 1:
+                    kv_start(step, ch, way)
         if step == 1:
             fc_s.rest()
             out_s.finish_recv()
@@ -948,6 +956,7 @@
     og_c = net.send(r.out_g.at[1 - c], r.og_c, net.plane(1))
     proj_c.part(0)
     proj_c.part(1)
+    early_p = [net.send(r.vec_g, r.vg_p.at[m - 1], net.plane(m)) for m in (1, 2, 3)]
     for copy in ga_p:
         copy.wait_recv()
 
@@ -991,12 +1000,12 @@
             kc = 0 if h < 2 else 256
             r.dq_t[h] += dot_tn(r.kv_all[j, :, kc:kc + 128], r.ds[h])
 
-    def chain_copy(way, step):
+    def chain_copy(way, step, ch):
         target = jnp.clip(jnp.where(way == 0, z - 1, z + 1), 0, nz - 1)
         at = way * (nz - 1) + step - 1
         return pltpu.make_async_remote_copy(
-            src_ref=r.chain.at[at], dst_ref=r.chain_land.at[at],
-            send_sem=r.ch_send.at[at], recv_sem=r.ch_recv.at[at],
+            src_ref=r.chain.at[at, :, third(ch)], dst_ref=r.chain_land.at[at, :, third(ch)],
+            send_sem=r.ch_send.at[at * 3 + ch], recv_sem=r.ch_recv.at[at * 3 + ch],
             device_id=(x, target, u), device_id_type=MESH)
 
     def chain_step(step):
@@ -1009,18 +1018,20 @@
                 back(j)
                 at = way * (nz - 1) + step - 1
                 comes = jnp.logical_and(behind >= 0, behind < nz)
-                if step < nz - 1:
-                    @pl.when(comes)
-                    def _():
-                        chain_copy(way, step + 1).wait_recv()
-                        r.chain[at] = (r.dkv[...] + r.chain_land[at + 1].astype(F32)).astype(BF)
-
-                    @pl.when(jnp.logical_not(comes))
-                    def _():
-                        r.chain[at] = r.dkv[...].astype(BF)
-                else:
-                    r.chain[at] = r.dkv[...].astype(BF)
-                chain_copy(way, step).start()
+                for ch in range(3):
+                    at_ch = third(ch)
+                    if step < nz - 1:
+                        @pl.when(comes)
+                        def _():
+                            chain_copy(way, step + 1, ch).wait_recv()
+                            r.chain[at, :, at_ch] = (r.dkv[:, at_ch] + r.chain_land[at + 1, :, at_ch].astype(F32)).astype(BF)
+
+                        @pl.when(jnp.logical_not(comes))
+                        def _():
+                            r.chain[at, :, at_ch] = r.dkv[:, at_ch].astype(BF)
+                    else:
+                        r.chain[at, :, at_ch] = r.dkv[:, at_ch].astype(BF)
+                    chain_copy(way, step, ch).start()
 
         loop(2, either)
 
@@ -1030,6 +1041,12 @@
             proj_c.part(2)
             proj_c.part(3)
             fc_c.start()
+            total = r.vec_g[...]
+            for m in range(3):
+                early_p[m].wait_recv()
+                total = total + r.vg_p[m]
+            r.vg_1[...] = total
+            early_z = [net.send(r.vg_1, r.vg_z.at[d - 1], net.line(d)) for d in range(1, nz)]
             br_y = reduce_y(br_c[0], r.br_part, r.br_c, r.br_mid, r.br_y)
             og_c.wait_recv()
             r.og_1[...] = (r.out_g[c].astype(F32) + r.og_c[...].astype(F32)).astype(BF)
@@ -1039,6 +1056,12 @@
             r.output[...] = (
                 r.resid[...] + gain(5) + reduce_end(br_c[1], br_y, r.br_part, r.br_c, r.br_y)
             ).astype(BF)
+            total = r.vg_1[...]
+            for d in range(nz - 1):
+                early_z[d].wait_recv()
+                total = total + r.vg_z[d]
+            r.vg_2[...] = total
+            early_x = net.send(r.vg_2, r.vg_x, net.other_x())
             fc_c.part(0)
             fc_c.part(1)
             og_y.wait_recv()
@@ -1056,23 +1079,22 @@
     back(z)
 
     fc_c.second()
-    @pl.when(z + 1 < nz)
-    def _():
-        chain_copy(0, 1).wait_recv()
-        r.dkv[...] += r.chain_land[0].astype(F32)
-
-    @pl.when(z >= 1)
-    def _():
-        chain_copy(1, 1).wait_recv()
-        r.dkv[...] += r.chain_land[nz - 1].astype(F32)
+    for ch in range(3):
+        @pl.when(z + 1 < nz)
+        def _():
+            chain_copy(0, 1, ch).wait_recv()
+            r.dkv[:, third(ch)] += r.chain_land[0, :, third(ch)].astype(F32)
+
+        @pl.when(z >= 1)
+        def _():
+            chain_copy(1, 1, ch).wait_recv()
+            r.dkv[:, third(ch)] += r.chain_land[nz - 1, :, third(ch)].astype(F32)
 
     r.gqkv[:, 128:512] = r.dkv[...].astype(BF)
     dq = jnp.transpose(jnp.where(rowi < 64, r.dq_t[0], r.dq_t[1]) * 0.125)
     r.gqkv[:, 0:128] = dq.astype(BF)
     r.gqkv[:, 512:576] = jnp.transpose(r.dq_t[2] * 0.125)[:, 0:64].astype(BF)
 
-    weight_grad(r.ln_all, r.gqkv, r.qkv_g, 6)
-    qkv_c.start()
 
     def gin_tile(t):
         r.gi_part[t] = dot_nt(r.gqkv[tile(t), :], r.w_qkv[...]).astype(BF)
@@ -1081,10 +1103,14 @@
     gi_c0 = reduce_core(0, u ^ 3, r.gi_part, r.gi_c)
     gin_tile(u ^ 1)
     gi_c1 = reduce_core(1, u ^ 1, r.gi_part, r.gi_c)
+    weight_grad(r.ln_all, r.gqkv, r.qkv_g, 6)
+    qkv_c.start()
     gin_tile(u ^ 2)
     gi_y = reduce_y(gi_c0, r.gi_part, r.gi_c, r.gi_mid, r.gi_y)
     gin_tile(u)
-    r.vec_g[:, 0:576] += jnp.where(row[:, 0:576] == 6 + u, jnp.sum(r.gqkv[...].astype(F32), 0, keepdims=True), 0.0)
+    r.late[...] = jnp.zeros((8, 768), F32)
+    row_l = row[0:8]
+    r.late[:, 0:576] = jnp.where(row_l[:, 0:576] == 2 + u, jnp.sum(r.gqkv[...].astype(F32), 0, keepdims=True), 0.0)
     qkv_c.first()
     proj_c.total(r.acc)
     r.proj_f[...] = r.acc[...].astype(BF)
@@ -1127,44 +1153,45 @@
 
     gin = reduce_end(gi_c1, gi_y, r.gi_part, r.gi_c, r.gi_y)
     normed, inverse = normalize(x_own[...].astype(F32))
-    r.vec_g[0:1, :] = jnp.sum(gin * normed, 0, keepdims=True)
-    r.vec_g[2:3, :] = jnp.sum(gin, 0, keepdims=True)
-    vec_m = [net.send(r.vec_g, r.vg_p.at[m - 1], net.plane(m)) for m in (1, 2, 3)]
+    r.late[0:1, :] = jnp.sum(gin * normed, 0, keepdims=True)
+    r.late[1:2, :] = jnp.sum(gin, 0, keepdims=True)
+    late_p = [net.send(r.late, r.late_p.at[m - 1], net.plane(m)) for m in (2, 3, 1)]
+    late_p += [net.send(r.late, r.late_p.at[3 + m], (1 - x, z, u ^ m)) for m in range(4)]
     r.input_grad[...] = (r.grad_resid[...] + norm_grad(gin, normed, inverse, gain(0))).astype(BF)
     qkv_c.second()
     fc_c.total(r.acc)
     r.fc_f[...] = r.acc[...].astype(BF)
     hand_out(0, r.fc_f, r.fc_o)
-    total = r.vec_g[...]
-    for m in range(3):
-        vec_m[m].wait_recv()
-        total = total + r.vg_p[m]
-    r.vg_1[...] = total
-    vec_l = [net.send(r.vg_1, r.vg_z.at[d - 1], net.line(d)) for d in range(1, nz)]
+    total = r.late[...]
+    for copy in late_p:
+        copy.wait_recv()
+    for m in range(7):
+        total = total + r.late_p[m]
+    r.late_1[...] = total
+    late_z = [net.send(r.late_1, r.late_z.at[d - 1], net.line(d)) for d in range(1, nz)]
     total = r.og_3[rows_at(48 * z, 48), :].astype(F32)
     for d in range(nz - 1):
         og_z[d].wait_recv()
         total = total + r.og_z[d].astype(F32)
     r.out_o[:, half_cols(x)] = total.astype(BF)
     og_last = net.send(r.out_o.at[:, half_cols(x)], r.out_o.at[:, half_cols(x)], net.other_x())
-    total = r.vg_1[...]
-    for d in range(nz - 1):
-        vec_l[d].wait_recv()
-        total = total + r.vg_z[d]
-    r.vg_2[...] = total
-    vec_last = net.send(r.vg_2, r.vg_x, net.other_x())
     qkv_c.total(r.acc_q)
     r.qkv_f[...] = r.acc_q[...].astype(BF)
     hand_out(4, r.qkv_f, r.qkv_o)
-    vec_last.wait_recv()
-    total = r.vg_2[...] + r.vg_x[...]
-    pick = lambda i: jnp.sum(jnp.where(row == i, total, 0.0), 0, keepdims=True)
-    heads, hidden = pick(6 + z), pick(10 + u)
+    early_x.wait_recv()
+    early = r.vg_2[...] + r.vg_x[...]
+    late = r.late_1[...]
+    for d in range(nz - 1):
+        late_z[d].wait_recv()
+        late = late + r.late_z[d]
+    heads = jnp.sum(jnp.where(row_l == 2 + z, late, 0.0), 0, keepdims=True)
+    hidden = jnp.sum(jnp.where(row == 10 + u, early, 0.0), 0, keepdims=True)
+    total = early[0:8] + jnp.where(row_l == 0, late, 0.0) + jnp.where(row_l == 2, late[1:2], 0.0)
     bias[0:1, 0:128] = heads[:, 0:128]
     bias[0:1, 128:192] = heads[:, 512:576]
     bias[1:2, 0:128] = heads[:, 256:384]
     bias[1:2, 128:192] = heads[:, 448:512]
-    mine8 = pltpu.roll(total[0:8], 768 - 48 * (4 * z + u), 1)
+    mine8 = pltpu.roll(total, 768 - 48 * (4 * z + u), 1)
     vp[0:8, :] = mine8
     both = pltpu.roll(bias[...], 256 - 48 * u, 1)
     vp[6:8, 0:256] = both[0:2]
@@ -1183,12 +1210,14 @@
         for way in range(2):
             @pl.when(kv_sends(way, step))
             def _():
-                kv_copy(way, step).wait_send()
+                for ch in range(3):
+                    kv_copy(way, step, ch).wait_send()
     for step in range(1, nz):
         for way in range(2):
             @pl.when(z - step >= 0 if way == 0 else z + step < nz)
             def _():
-                chain_copy(way, step).wait_send()
+                for ch in range(3):
+                    chain_copy(way, step, ch).wait_send()
     for part in (qkv_s, fc_s, proj_s, out_s, proj_c, fc_c, qkv_c):
         part.finish()
     net.finish()
@@ -1230,13 +1259,14 @@
         qkv_f=vm(96, 576), fc_f=vm(96, 768), proj_f=vm(96, 768),
         og_c=vm(2, 192, 768), og_1=vm(2, 192, 768), og_y=vm(192, 768), og_2=vm(192, 768),
         og_x=vm(192, 384), og_3=vm(192, 384), og_z=vm(nz - 1, 48, 384),
+        late=f(8, 768), late_p=f(7, 8, 768), late_1=f(8, 768), late_z=f(nz - 1, 8, 768),
         vg_p=f(3, 16, 768), vg_1=f(16, 768), vg_z=f(nz - 1, 16, 768), vg_2=f(16, 768), vg_x=f(16, 768),
         send_sem=pltpu.SemaphoreType.DMA((112,)), recv_sem=pltpu.SemaphoreType.DMA((112,)),
         sp_send=pltpu.SemaphoreType.DMA((32,)), sp_recv=pltpu.SemaphoreType.DMA((32,)),
         co_send=pltpu.SemaphoreType.DMA((27,)), co_recv=pltpu.SemaphoreType.DMA((27,)),
         local_sem=pltpu.SemaphoreType.DMA((6,)),
-        kv_send=pltpu.SemaphoreType.DMA((2 * nz,)), kv_recv=pltpu.SemaphoreType.DMA((2 * nz,)),
-        ch_send=pltpu.SemaphoreType.DMA((2 * nz,)), ch_recv=pltpu.SemaphoreType.DMA((2 * nz,)),
+        kv_send=pltpu.SemaphoreType.DMA((6 * nz,)), kv_recv=pltpu.SemaphoreType.DMA((6 * nz,)),
+        ch_send=pltpu.SemaphoreType.DMA((6 * nz,)), ch_recv=pltpu.SemaphoreType.DMA((6 * nz,)),
         f_send=pltpu.SemaphoreType.DMA((8,)), f_recv=pltpu.SemaphoreType.DMA((8,)),
     )
     names = [*operands, *outs, *scratch]
@@ -1290,7 +1320,7 @@
         out_shape=tuple(jax.ShapeDtypeStruct(*s) for s in shapes),
         in_specs=[VSPEC] * len(got),
         out_specs=(VSPEC,) * len(shapes),
-        compiler_params=pltpu.CompilerParams(vmem_limit_bytes=16 * 2**20),
+        compiler_params=pltpu.CompilerParams(vmem_limit_bytes=60 * 2**20),
         name="hand_over",
     )(*got.values())
 

time: 188 us -> 181 us (0.963)
  local copies, waits for them, and re-layouts: 7.61 us -> 1.21 us
    unnamed x16 -> x2, local copies, waits for them, and re-layouts: 7.04 us -> 0.65 us
    pallas_call x1, Pallas kernels: 178 us -> 176 us  [block_call(): pl.pallas_call(kernel, out_shape=tuple((jax.ShapeDtypeStruct(*s) for s in...]
where the time goes in v4:
time: 181 us
  Pallas kernels  179 us (99%)
    pallas_call x1, Pallas kernels, block_call(): pl.pallas_call(kernel, out_shape=tuple((jax.ShapeDtypeStruct(*s) for s in...  176 us

profile of v4, /device:TPU:0, one launch (start us, length us, event | category | flops | bytes accessed | tf_op | source)
XLA Modules:
  0.0 180.9 jit_solution(759693102591708554)
XLA Ops:
  0.6 0.0 copy-start
  0.7 0.6 copy-done
  1.3 0.6 broadcast_in_dim.17.refs_10_
  1.9 176.2 %transformer_block.1 = (bf16[128,768]{1,0:T(8,128)(2,1)}, bf16[128,768]{1,0:T(8,128)(2,1)}, bf16[4,48,576]{2,1,0:T(8,128)(2,1)}, bf16[4,48,768]{2,1,0:T(8,128)(2...) custom-call(bf16[128,768]{1,0:T(8,128)(2,1)} %bitcast.9, bf16[128,768]{1,0:T(8,128)(2,1)} %bitcast.10, ...), custom_call_target="tpu_custom_call" | custom-call | tf_op jit(solution)/shard_map/transformer_block/pallas_call | solution.py:1279
  178.1 2.8 %hand_over.1 = (bf16[128,768]{1,0:T(8,128)(2,1)}, bf16[128,768]{1,0:T(8,128)(2,1)}, f32[2,48]{1,0:T(2,128)}, f32[4,48]{1,0:T(4,128)}, f32[1,48]{1,0:T(1,128)}, /...) custom-call(bf16[128,768]{1,0:T(8,128)(2,1)} %get-tuple-element.29.o, ...), custom_call_target="tpu_custom_call" | custom-call | tf_op jit(solution)/shard_map/hand_over/pallas_call | solution.py:1318
Async XLA Ops:
  0.6 0.7 copy-start

commit v5 on v4

--- a/solution.py
+++ b/solution.py
@@ -956,7 +956,6 @@
     og_c = net.send(r.out_g.at[1 - c], r.og_c, net.plane(1))
     proj_c.part(0)
     proj_c.part(1)
-    early_p = [net.send(r.vec_g, r.vg_p.at[m - 1], net.plane(m)) for m in (1, 2, 3)]
     for copy in ga_p:
         copy.wait_recv()
 
@@ -1041,12 +1040,7 @@
             proj_c.part(2)
             proj_c.part(3)
             fc_c.start()
-            total = r.vec_g[...]
-            for m in range(3):
-                early_p[m].wait_recv()
-                total = total + r.vg_p[m]
-            r.vg_1[...] = total
-            early_z = [net.send(r.vg_1, r.vg_z.at[d - 1], net.line(d)) for d in range(1, nz)]
+            early_p = [net.send(r.vec_g, r.vg_p.at[m - 1], net.plane(m)) for m in (1, 2, 3)]
             br_y = reduce_y(br_c[0], r.br_part, r.br_c, r.br_mid, r.br_y)
             og_c.wait_recv()
             r.og_1[...] = (r.out_g[c].astype(F32) + r.og_c[...].astype(F32)).astype(BF)
@@ -1056,12 +1050,12 @@
             r.output[...] = (
                 r.resid[...] + gain(5) + reduce_end(br_c[1], br_y, r.br_part, r.br_c, r.br_y)
             ).astype(BF)
-            total = r.vg_1[...]
-            for d in range(nz - 1):
-                early_z[d].wait_recv()
-                total = total + r.vg_z[d]
-            r.vg_2[...] = total
-            early_x = net.send(r.vg_2, r.vg_x, net.other_x())
+            total = r.vec_g[...]
+            for m in range(3):
+                early_p[m].wait_recv()
+                total = total + r.vg_p[m]
+            r.vg_1[...] = total
+            early_z = [net.send(r.vg_1, r.vg_z.at[d - 1], net.line(d)) for d in range(1, nz)]
             fc_c.part(0)
             fc_c.part(1)
             og_y.wait_recv()
@@ -1074,6 +1068,12 @@
                 net.send(r.og_3.at[rows_at(48 * net.zplus(d), 48)], r.og_z.at[d - 1], net.line(d))
                 for d in range(1, nz)
             ]
+            total = r.vg_1[...]
+            for d in range(nz - 1):
+                early_z[d].wait_recv()
+                total = total + r.vg_z[d]
+            r.vg_2[...] = total
+            early_x = net.send(r.vg_2, r.vg_x, net.other_x())
             fc_c.part(2)
             fc_c.part(3)
     back(z)
@@ -1099,12 +1099,12 @@
     def gin_tile(t):
         r.gi_part[t] = dot_nt(r.gqkv[tile(t), :], r.w_qkv[...]).astype(BF)
 
+    weight_grad(r.ln_all, r.gqkv, r.qkv_g, 6)
+    qkv_c.start()
     gin_tile(u ^ 3)
     gi_c0 = reduce_core(0, u ^ 3, r.gi_part, r.gi_c)
     gin_tile(u ^ 1)
     gi_c1 = reduce_core(1, u ^ 1, r.gi_part, r.gi_c)
-    weight_grad(r.ln_all, r.gqkv, r.qkv_g, 6)
-    qkv_c.start()
     gin_tile(u ^ 2)
     gi_y = reduce_y(gi_c0, r.gi_part, r.gi_c, r.gi_mid, r.gi_y)
     gin_tile(u)

time: 181 us -> 179 us (0.989)
  Pallas kernels: 179 us -> 177 us
    pallas_call x1, Pallas kernels: 176 us -> 174 us  [block_call(): pl.pallas_call(kernel, out_shape=tuple((jax.ShapeDtypeStruct(*s) for s in...]
where the time goes in v5:
time: 179 us; the launch traced here: 178 us
  Pallas kernels  177 us (99%)
    pallas_call x1, Pallas kernels, block_call(): pl.pallas_call(kernel, out_shape=tuple((jax.ShapeDtypeStruct(*s) for s in...  174 us

profile of v5, /device:TPU:0, one launch (start us, length us, event | category | flops | bytes accessed | tf_op | source)
XLA Modules:
  0.0 178.4 jit_solution(13907120465716421656)
XLA Ops:
  0.6 0.0 copy-start
  0.7 0.6 copy-done
  1.3 0.6 broadcast_in_dim.17.refs_10_
  1.9 173.7 %transformer_block.1 = (bf16[128,768]{1,0:T(8,128)(2,1)}, bf16[128,768]{1,0:T(8,128)(2,1)}, bf16[4,48,576]{2,1,0:T(8,128)(2,1)}, bf16[4,48,768]{2,1,0:T(8,128)(2...) custom-call(bf16[128,768]{1,0:T(8,128)(2,1)} %bitcast.9, bf16[128,768]{1,0:T(8,128)(2,1)} %bitcast.10, ...), custom_call_target="tpu_custom_call" | custom-call | tf_op jit(solution)/shard_map/transformer_block/pallas_call | solution.py:1279
  175.6 2.8 %hand_over.1 = (bf16[128,768]{1,0:T(8,128)(2,1)}, bf16[128,768]{1,0:T(8,128)(2,1)}, f32[2,48]{1,0:T(2,128)}, f32[4,48]{1,0:T(4,128)}, f32[1,48]{1,0:T(1,128)}, /...) custom-call(bf16[128,768]{1,0:T(8,128)(2,1)} %get-tuple-element.29.o, ...), custom_call_target="tpu_custom_call" | custom-call | tf_op jit(solution)/shard_map/hand_over/pallas_call | solution.py:1318
Async XLA Ops:
  0.6 0.7 copy-start

commit v6 on v5

--- a/solution.py
+++ b/solution.py
@@ -993,8 +993,8 @@
             r.dkv[rows, 128:256] = pair(p, r.gam[0], r.gam[1])
             r.dkv[rows, 256:384] = dot_nn(ds(2), r.qm[2]) + dot_nn(p(2), r.gam[2])
 
-        loop(4, keys)
-        loop(4, sums)
+        lax.fori_loop(0, 4, lambda i, c: (keys(i), c)[1], 0, unroll=True)
+        lax.fori_loop(0, 4, lambda i, c: (sums(i), c)[1], 0, unroll=True)
         for h in range(3):
             kc = 0 if h < 2 else 256
             r.dq_t[h] += dot_tn(r.kv_all[j, :, kc:kc + 128], r.ds[h])
@@ -1041,15 +1041,12 @@
             proj_c.part(3)
             fc_c.start()
             early_p = [net.send(r.vec_g, r.vg_p.at[m - 1], net.plane(m)) for m in (1, 2, 3)]
-            br_y = reduce_y(br_c[0], r.br_part, r.br_c, r.br_mid, r.br_y)
             og_c.wait_recv()
             r.og_1[...] = (r.out_g[c].astype(F32) + r.og_c[...].astype(F32)).astype(BF)
             og_y = net.send(r.og_1.at[1 - y], r.og_y, net.plane(2))
         if step == nz - 2:
             proj_c.second()
-            r.output[...] = (
-                r.resid[...] + gain(5) + reduce_end(br_c[1], br_y, r.br_part, r.br_c, r.br_y)
-            ).astype(BF)
+            br_y = reduce_y(br_c[0], r.br_part, r.br_c, r.br_mid, r.br_y)
             total = r.vec_g[...]
             for m in range(3):
                 early_p[m].wait_recv()
@@ -1074,6 +1071,9 @@
                 total = total + r.vg_z[d]
             r.vg_2[...] = total
             early_x = net.send(r.vg_2, r.vg_x, net.other_x())
+            r.output[...] = (
+                r.resid[...] + gain(5) + reduce_end(br_c[1], br_y, r.br_part, r.br_c, r.br_y)
+            ).astype(BF)
             fc_c.part(2)
             fc_c.part(3)
     back(z)

time: 179 us -> 178 us (level)
  Pallas kernels: 177 us -> 175 us
where the time goes in v6:
time: 178 us; the launch traced here: 177 us
  Pallas kernels  175 us (98%)
    pallas_call x1, Pallas kernels, block_call(): pl.pallas_call(kernel, out_shape=tuple((jax.ShapeDtypeStruct(*s) for s in...  173 us

profile of v6, /device:TPU:0, one launch (start us, length us, event | category | flops | bytes accessed | tf_op | source)
XLA Modules:
  0.0 177.3 jit_solution(6408377806897592685)
XLA Ops:
  0.6 0.0 copy-start
  0.7 0.6 copy-done
  1.3 0.6 broadcast_in_dim.17.refs_10_
  1.9 172.7 %transformer_block.1 = (bf16[128,768]{1,0:T(8,128)(2,1)}, bf16[128,768]{1,0:T(8,128)(2,1)}, bf16[4,48,576]{2,1,0:T(8,128)(2,1)}, bf16[4,48,768]{2,1,0:T(8,128)(2...) custom-call(bf16[128,768]{1,0:T(8,128)(2,1)} %bitcast.9, bf16[128,768]{1,0:T(8,128)(2,1)} %bitcast.10, ...), custom_call_target="tpu_custom_call" | custom-call | tf_op jit(solution)/shard_map/transformer_block/pallas_call | solution.py:1279
  174.5 2.8 %hand_over.1 = (bf16[128,768]{1,0:T(8,128)(2,1)}, bf16[128,768]{1,0:T(8,128)(2,1)}, f32[2,48]{1,0:T(2,128)}, f32[4,48]{1,0:T(4,128)}, f32[1,48]{1,0:T(1,128)}, /...) custom-call(bf16[128,768]{1,0:T(8,128)(2,1)} %get-tuple-element.29.o, ...), custom_call_target="tpu_custom_call" | custom-call | tf_op jit(solution)/shard_map/hand_over/pallas_call | solution.py:1318
Async XLA Ops:
  0.6 0.7 copy-start
